TPU v7x, 32 devices: a whole 2x2x4 slice. The times are simulated.
32 devices in a mesh: replica: 2 (over y), rows: 4 (over x, core), tensor: 4 (over z).
Axes of the slice: x: 2, y: 2, z: 4, core: 2. Of those that a mesh axis runs over, the one named last changes fastest.
Arguments:
- gate_in: bfloat16 [512, 16384], P(('replica', 'rows'), 'tensor'), parts along dimension 0, may hold values from -6 to 6
- up_in: bfloat16 [512, 16384], P(('replica', 'rows'), 'tensor'), parts along dimension 0, may hold values from -6 to 6
- down_weight: bfloat16 [16384, 8192], P('tensor', 'rows'), may hold values from -0.046875 to 0.046875
- delta_tiles: bfloat16 [4, 128, 6, 128, 128], P('rows', 'tensor'), may hold values from -0.15625 to 0.15625
- delta_cols: int32 [4, 128, 6], P('rows', 'tensor'), may hold values from 0 to 63, as said below
- tenant_of_row: int32 [512, 1], P(('replica', 'rows')), parts along dimension 0, may hold values from 0 to 3; in each aligned block of 64 rows (0 to 63, 64 to 127, ...) at most 24 rows name the same one
Outputs:
- mixed: bfloat16 [512, 8192], P(('replica', 'rows'), 'tensor'), parts along dimension 0
There are 2 independent parts, one for each index of `replica`. A program takes and returns all parts, laid end to end along the dimension named above; an argument that names none is the same for every part. Nothing has to cross between parts.
Inputs may be any that keep to these rules, and one draw needn't show every extreme that they name: `tenant_of_row`: tenant k's delta is held by row group k. Within the rows of one row group no tenant has more than 24 rows, and in every draw some tenant has exactly 24 in some group. `delta_cols`: the 6 tiles of one row of tiles of a tenant's delta have distinct column blocks.
All inputs are finite; a program needn't handle non-finite values.
Results may differ from a plain program's by a relative error of at most 0.009.
Values may be sent and summed in bfloat16 or wider, within the bound.
No kernel may reach another device: no remote copies, remote signals or barrier semaphores. Data moves between devices by JAX's collectives and lax.ppermute only.
A program may use at most 128 MiB of HBM per device.

v0:
```python
import jax
import jax.numpy as jnp
from jax import lax
from jax.sharding import PartitionSpec as P


def tile_products(rows_in, tiles, cols, ncol):
    count = rows_in.shape[0]
    nblk = tiles.shape[0]
    blocks = rows_in.reshape(count, nblk, 128)
    prods = jnp.einsum("srk,rjkc->srjc", blocks, tiles, preferred_element_type=jnp.float32)
    place = (cols[..., None] == jnp.arange(ncol, dtype=jnp.int32)).astype(jnp.float32)
    spread = jnp.einsum("srjc,rjn->snc", prods, place, precision=lax.Precision.HIGHEST)
    return spread.reshape(count, ncol * 128)


def shards(gate_in, up_in, down_weight, delta_tiles, delta_cols, tenant_of_row):
    count = gate_in.shape[0]
    groups = lax.axis_size("rows")
    width = down_weight.shape[1] * groups
    ncol = width // 128
    hidden = (jax.nn.silu(gate_in.astype(jnp.float32)) * up_in.astype(jnp.float32)).astype(
        jnp.bfloat16
    )
    tenant = tenant_of_row[:, 0]
    member = (tenant[:, None] == jnp.arange(groups, dtype=jnp.int32)[None, :]).astype(jnp.int32)
    capacity = count * 3 // (2 * groups)
    before = jnp.cumsum(member, axis=0) - member
    slot = jnp.sum(before * member, axis=1)
    in_tenant = tenant[None, None, :] == jnp.arange(groups, dtype=jnp.int32)[:, None, None]
    in_slot = slot[None, None, :] == jnp.arange(capacity, dtype=jnp.int32)[None, :, None]
    dispatch = (in_tenant & in_slot).astype(jnp.bfloat16)
    outgoing = jnp.einsum(
        "kcs,sf->kcf", dispatch, hidden, preferred_element_type=jnp.float32
    ).astype(jnp.bfloat16)
    own_tiles = delta_tiles[0]
    own_cols = delta_cols[0]
    arrived = lax.all_to_all(outgoing, "rows", split_axis=0, concat_axis=0, tiled=True)
    senders, items, feats = arrived.shape
    flat = arrived.reshape(senders * items, feats)
    answer = tile_products(flat, own_tiles, own_cols, ncol).astype(jnp.bfloat16)
    answer = answer.reshape(senders, items, ncol * 128)
    returned = lax.all_to_all(answer, "rows", split_axis=0, concat_axis=0, tiled=True)
    delta = jnp.einsum("kcs,kcd->sd", dispatch, returned, preferred_element_type=jnp.float32)
    base_all = jnp.dot(
        lax.all_gather(hidden, "rows", axis=0, tiled=True),
        down_weight,
        preferred_element_type=jnp.float32,
    )
    moved = lax.all_to_all(
        delta.astype(jnp.bfloat16), "rows", split_axis=1, concat_axis=0, tiled=True
    )
    local_term = lax.optimization_barrier(
        (base_all + moved.astype(jnp.float32)).astype(jnp.bfloat16)
    )
    term = lax.all_to_all(local_term, "rows", split_axis=0, concat_axis=1, tiled=True)
    mixed = lax.psum_scatter(
        term.astype(jnp.float32).astype(jnp.bfloat16), "tensor", scatter_dimension=1, tiled=True
    )
    return mixed


def solution(mesh):
    return jax.shard_map(
        shards,
        mesh=mesh,
        in_specs=(
            P(("replica", "rows"), "tensor"),
            P(("replica", "rows"), "tensor"),
            P("tensor", "rows"),
            P("rows", "tensor", None, None, None),
            P("rows", "tensor", None),
            P(("replica", "rows"), None),
        ),
        out_specs=P(("replica", "rows"), "tensor"),
        check_vma=False,
    )
```

profile of v0, /device:TPU:0, one launch (start us, length us, event | category | flops | bytes accessed | tf_op | source)
XLA Modules:
  0.0 146.5 jit_solution(10609262980717270874)
XLA Ops:
  6.5 0.7 fusion.24
  7.3 0.7 iota_compare_fusion.3
  7.9 0.1 reduce_window_sum.11
  8.0 0.8 select_reduce_fusion
  8.9 1.5 %fusion.16 = bf16[64,4096]{1,0:T(8,128)(2,1)S(1)} fusion(bf16[64,4096]{1,0:T(8,128)(2,1)} %param.7, bf16[64,4096]{1,0:T(8,128)(2,1)} %param.6), kind=kLoop, calls=%fused_computation.19 | loop fusion | flops 2097152 | bytes 1572864 | tf_op jit(solution)/shard_map/convert_element_type | solution.py:22
  10.4 0.0 copy-start
  10.4 0.0 copy-start.1
  10.4 1.3 convolution_convert_fusion
  11.7 4.2 %all-to-all-start = ((bf16[4,24,4096]{2,1,0:T(8,128)(2,1)}), bf16[4,24,4096]{2,1,0:T(8,128)(2,1)S(1)}, u32[]{:S(2)}, u32[]{:S(2)}) async-start(bf16[4,24,4096]{2,1,0:T(8,128)(2,1)} %convolution_convert_fusion), calls=%async_computation | async-start | bytes 1572864 | tf_op jit(solution)/shard_map/all_to_all | solution.py:38
  15.9 0.0 all-gather.2.cloned.1.call-start
  15.9 0.0 copy-done
  15.9 0.7 all-gather.2.cloned.1.call-update
  16.6 0.0 reduce-scatter.2.cloned.1.call-start
  16.6 0.0 copy-done.1
  16.7 10.9 %all-to-all-done = bf16[4,24,4096]{2,1,0:T(8,128)(2,1)S(1)} async-done(((bf16[4,24,4096]{2,1,0:T(8,128)(2,1)}), bf16[4,24,4096]{2,1,0:T(8,128)(2,1)S(1)}, u32[]{:S(2)}, u32[]{:S(2)}) %all-to-all-start) | async-done | bytes 786464 | tf_op jit(solution)/shard_map/all_to_all | solution.py:38
  27.5 0.2 copy.15
  27.7 4.6 %fusion.4 = f32[32,96,6,128]{3,1,2,0:T(8,128)S(1)} fusion(bf16[1,32,6,128,128]{4,3,2,1,0:T(8,128)(2,1)} %param.9, bf16[96,32,128,1]{2,1,0,3:T(8,128)(2,1)S(1)} %bitcast.50), kind=kOutput, calls=%fused_computation.5 | convolution fusion | flops 603979776 | bytes 16515072 | tf_op jit(solution)/shard_map/srk,rjkc->srjc/dot_general | solution.py:11
  32.3 9.4 %fusion.9 = bf16[96,64,128]{2,1,0:T(8,128)(2,1)S(1)} fusion(f32[32,96,6,128]{3,1,2,0:T(8,128)S(1)} %fusion.4, s32[32,6]{0,1:T(8,128)S(1)} %bitcast.58), kind=kOutput, calls=%fused_computation.11 | convolution fusion | flops 1812738048 | bytes 11010816 | tf_op jit(solution)/shard_map/srjc,rjn->snc/dot_general | solution.py:13
  41.7 0.7 convert_element_type.51
  42.5 22.5 %all_to_all.42 = bf16[4,24,8192]{2,1,0:T(8,128)(2,1)S(1)} all-to-all(bf16[4,24,8192]{2,1,0:T(8,128)(2,1)S(1)} %convert_element_type.51), channel_id=1, replica_groups=mesh['replica'=2,'rows'=4,'tensor'=4] {'rows'}, dimensions={0} | all-to-all | bytes 3145728 | tf_op jit(solution)/shard_map/all_to_all | solution.py:43
  65.0 0.5 fusion.3
  65.5 0.1 copy.28
  65.6 16.9 %all_to_all.43 = bf16[64,4,2048]{2,0,1:T(8,128)(2,1)S(1)} all-to-all(bf16[64,4,2048]{2,0,1:T(8,128)(2,1)S(1)} %bitcast.53), channel_id=1, replica_groups=mesh['replica'=2,'rows'=4,'tensor'=4] {'rows'}, dimensions={1} | all-to-all | bytes 2097152 | tf_op jit(solution)/shard_map/all_to_all | solution.py:50
  82.5 0.2 convert_element_type.58
  82.7 0.0 all-gather.2.cloned.1.call-done
  82.7 10.9 %fusion.6 = bf16[256,2048]{1,0:T(8,128)(2,1)S(1)} fusion(f32[256,2048]{1,0:T(8,128)S(1)} %bitcast.56, bf16[256,4096]{1,0:T(8,128)(2,1)} %all-gather.2.cloned.1.call-done, bf16[4096,2048]{1,0:T(8,128)(2,1)} %param.8), kind=kOutput, calls=%fused_computation.10 | convolution fusion | flops 4296015872 | bytes 22020096 | tf_op jit(solution)/shard_map/dot_general | solution.py:45
  93.7 16.9 %all_to_all.44 = bf16[4,64,2048]{2,1,0:T(8,128)(2,1)S(1)} all-to-all(bf16[4,64,2048]{2,1,0:T(8,128)(2,1)S(1)} %bitcast.57), channel_id=1, replica_groups=mesh['replica'=2,'rows'=4,'tensor'=4] {'rows'}, dimensions={0} | all-to-all | bytes 2097152 | tf_op jit(solution)/shard_map/all_to_all | solution.py:56
  110.5 1.0 copy.14
  111.6 0.0 reduce-scatter.2.cloned.1.call-update
  111.6 28.1 %reduce-scatter.2.cloned.1.call-done = bf16[64,2048]{1,0:T(8,128)(2,1)} async-done(((bf16[64,8192]{1,0:T(8,128)(2,1)}), bf16[64,2048]{1,0:T(8,128)(2,1)}) %reduce-scatter.2.cloned.1.call-update) | async-done | bytes 262160 | tf_op jit(solution)/shard_map/reduce_scatter | solution.py:57
  (2 shorter events, 0.0 us)
Async XLA Ops:
  10.4 5.5 %copy-start = (bf16[64,4096]{1,0:T(8,128)(2,1)}, bf16[64,4096]{1,0:T(8,128)(2,1)S(1)}, u32[]{:S(2)}) copy-start(bf16[64,4096]{1,0:T(8,128)(2,1)S(1)} %fusion.16) | copy-start | bytes 1572868
  10.4 6.2 %copy-start.1 = (s32[1,32,6]{1,0,2:T(1,128)S(1)}, s32[1,32,6]{1,0,2:T(1,128)}, u32[]{:S(2)}) copy-start(s32[1,32,6]{1,0,2:T(1,128)} %param.10) | copy-start | bytes 2308
  11.7 15.9 %all-to-all-start = ((bf16[4,24,4096]{2,1,0:T(8,128)(2,1)}), bf16[4,24,4096]{2,1,0:T(8,128)(2,1)S(1)}, u32[]{:S(2)}, u32[]{:S(2)}) async-start(bf16[4,24,4096]{2,1,0:T(8,128)(2,1)} %convolution_convert_fusion), calls=%async_computation | async-start | bytes 1572864 | tf_op jit(solution)/shard_map/all_to_all | solution.py:38
  15.9 66.9 %all-gather.2.cloned.1.call-start = ((), (), s32[]{:S(2)}) async-start(), calls=%async_computation.5 | async-start | bytes 2621440 | tf_op jit(solution)/shard_map/all_gather | solution.py:46
  16.6 123.1 %reduce-scatter.2.cloned.1.call-start = ((), (), s32[]{:S(2)}) async-start(), calls=%async_computation.6 | async-start | bytes 1310720 | tf_op jit(solution)/shard_map/reduce_scatter | solution.py:57
Sparse Core Ops, SparseCore 0:
  18.3 25.0 all-gather.1
  111.7 27.9 reduce-scatter.1
where the time goes:
time: 147 us
  blocking collectives  56.3 us (38%)
  waiting for transfers between devices  39.7 us (27%)
  matrix products  26.7 us (18%)
  between operations  13.5 us (9%)
  starting transfers between devices  4.25 us (3%)
  other arithmetic  4.07 us (3%)
  local copies, waits for them, and re-layouts  2.04 us (1%)
    reduce_scatter x1, waiting for transfers between devices, shards(): lax.psum_scatter(term.astype(jnp.float32).astype(jnp.bfloat16), 'tensor',...  28.1 us
    all_to_all x1, blocking collectives, shards(): lax.all_to_all(answer, 'rows', split_axis=0, concat_axis=0, tiled=True)  22.5 us
    all_to_all x1, blocking collectives, shards(): lax.all_to_all(delta.astype(jnp.bfloat16), 'rows', split_axis=1, concat_a...  16.9 us
    all_to_all x1, blocking collectives, shards(): lax.all_to_all(local_term, 'rows', split_axis=0, concat_axis=1, tiled=True)  16.9 us
    dot_general x1, matrix products, shards(): jnp.dot(lax.all_gather(hidden, 'rows', axis=0, tiled=True), down_weight,...  10.9 us
    all_to_all x1, waiting for transfers between devices, shards(): lax.all_to_all(outgoing, 'rows', split_axis=0, concat_axis=0, tiled=True)  10.9 us
    dot_general x1, matrix products, tile_products(): jnp.einsum('srjc,rjn->snc', prods, place, precision=lax.Precision.HIGHEST)  9.44 us
    dot_general x1, matrix products, tile_products(): jnp.einsum('srk,rjkc->srjc', blocks, tiles, preferred_element_type=jnp.fl...  4.59 us
  transfers between devices with their start and end apart: 3, of which 2 were waited for; matrix products, arithmetic and copies ran while one was open for 11% of the time, Pallas kernels for 0%

commit v1 on v0

v1 whole, which is shorter than its diff:
```python
import functools

import jax
import jax.numpy as jnp
from jax import lax
from jax.experimental import pallas as pl
from jax.experimental.pallas import tpu as pltpu
from jax.sharding import PartitionSpec as P

BF = jnp.bfloat16
F32 = jnp.float32
LANES = 128
VMEM_LIMIT = 48 * 1024 * 1024


def params():
    return pltpu.CompilerParams(vmem_limit_bytes=VMEM_LIMIT)


def whole():
    return pl.BlockSpec(memory_space=pltpu.VMEM)


def smem():
    return pl.BlockSpec(memory_space=pltpu.SMEM)


def hidden_kernel(gate_ref, up_ref, tenant_ref, out_ref):
    feats = gate_ref.shape[1]
    for start in range(0, feats, 512):
        at = pl.ds(start, min(512, feats - start))
        v = gate_ref[:, at].astype(F32)
        out_ref[:, at] = (v / (1.0 + jnp.exp(-v)) * up_ref[:, at].astype(F32)).astype(BF)
    count = out_ref.shape[0]
    out_ref[:, feats:] = jnp.broadcast_to(tenant_ref[...].astype(F32), (count, LANES)).astype(BF)


def hidden_of(gate, up, tenant):
    count, feats = gate.shape
    return pl.pallas_call(
        hidden_kernel,
        out_shape=jax.ShapeDtypeStruct((count, feats + LANES), BF),
        in_specs=[whole()] * 3,
        out_specs=whole(),
        compiler_params=params(),
        name="hidden",
        cost_estimate=pl.CostEstimate(
            flops=6 * count * feats, bytes_accessed=6 * count * feats, transcendentals=count * feats
        ),
    )(gate, up, tenant)


def slots_of(tenants, tenant):
    count = tenants.shape[0]
    mine = tenants == tenant.astype(F32)
    ones = jnp.where(mine, 1.0, 0.0).astype(BF)
    above = lax.broadcasted_iota(jnp.int32, (count, count), 0) > lax.broadcasted_iota(
        jnp.int32, (count, count), 1
    )
    earlier = jnp.dot(jnp.where(above, 1.0, 0.0).astype(BF), ones, preferred_element_type=F32)
    return jnp.where(mine, earlier, -1024.0)


def one_hot(slots, offset):
    lanes = lax.broadcasted_iota(jnp.int32, slots.shape, 1).astype(F32)
    return jnp.where(slots + offset == lanes, 1.0, 0.0).astype(BF)


def tenant_lanes(hidden_ref):
    return hidden_ref[:, hidden_ref.shape[1] - LANES :].astype(F32)


def delta_kernel(own, cap, bw, chunk, meta_ref, cols_ref, a_ref, b_ref, tiles_ref, *rest):
    outs, (packed, acc) = rest[:-2], rest[-2:]
    step = pl.program_id(0)
    feats = packed.shape[1]
    per_row = tiles_ref.shape[1]
    me = meta_ref[0]
    chip = me // 2

    @pl.when(step == 0)
    def _():
        hot = jnp.concatenate(
            [
                one_hot(slots_of(tenant_lanes(a_ref), me), 0),
                one_hot(slots_of(tenant_lanes(b_ref), me), cap),
            ],
            axis=0,
        )
        for start in range(0, feats, 512):
            at = pl.ds(start, min(512, feats - start))
            both = jnp.concatenate([a_ref[:, at], b_ref[:, at]], axis=0)
            rows = lax.dot_general(hot, both, (((0,), (0,)), ((), ())), preferred_element_type=F32)
            packed[:, at] = rows[: 2 * cap].astype(BF)
        acc[...] = jnp.zeros_like(acc)

    for block in range(chunk):
        row = step * chunk + block
        lhs = packed[:, pl.ds(pl.multiple_of(row * LANES, LANES), LANES)]
        rhs = jnp.concatenate([tiles_ref[block, j] for j in range(per_row)], axis=1)
        prods = jnp.dot(lhs, rhs, preferred_element_type=F32)
        at = [cols_ref[row * per_row + j] for j in range(per_row)]
        old = [acc[at[j]] for j in range(per_row)]
        for j in range(per_row):
            acc[at[j]] = old[j] + prods[:, j * LANES : (j + 1) * LANES]

    ncol = acc.shape[0]
    tiles = bw // LANES
    pairs = ncol // (2 * tiles)

    @pl.when(step == pl.num_programs(0) - 1)
    def _():
        if own:
            for n in range(ncol):
                got = acc[n].astype(F32)
                for g in range(2):
                    outs[g][:, n * LANES : (n + 1) * LANES] = got[g * cap : (g + 1) * cap].astype(BF)
        else:
            for n in range(tiles):
                at = slice(n * LANES, (n + 1) * LANES)
                outs[0][:, at] = acc[me * tiles + n].astype(BF)
                outs[1][:, at] = acc[(me + 1 - 2 * (me % 2)) * tiles + n].astype(BF)
            for e in range(1, pairs):
                first = lax.rem(chip + e, pairs) * 2 * tiles
                for n in range(2 * tiles):
                    got = acc[first + n]
                    to = (e - 1) * 2 * tiles + n
                    for g in range(2):
                        outs[2 + g][:, to * LANES : (to + 1) * LANES] = got[
                            g * cap : (g + 1) * cap
                        ].astype(BF)


def delta_of(own, cap, groups, width, meta, cols, a, b, tiles):
    nblk, per_row = tiles.shape[:2]
    feats = nblk * LANES
    bw = width // groups
    chunk = min(4, nblk)
    far = width - 2 * bw
    if own:
        shapes = [(cap, width)] * 2
    else:
        shapes = [(2 * cap, bw)] * 2 + [(cap, far)] * 2
    rows = 2 * cap
    full = lambda s: pl.BlockSpec(s, lambda i, *_: (0,) * len(s))
    return pl.pallas_call(
        functools.partial(delta_kernel, own, cap, bw, chunk),
        grid_spec=pltpu.PrefetchScalarGridSpec(
            num_scalar_prefetch=2,
            grid=(nblk // chunk,),
            in_specs=[
                full(a.shape),
                full(b.shape),
                pl.BlockSpec((chunk, per_row, LANES, LANES), lambda i, *_: (i, 0, 0, 0)),
            ],
            out_specs=[full(s) for s in shapes],
            scratch_shapes=[
                pltpu.VMEM((rows, feats), BF),
                pltpu.VMEM((width // LANES, rows, LANES), F32),
            ],
        ),
        out_shape=[jax.ShapeDtypeStruct(s, BF) for s in shapes],
        compiler_params=params(),
        name="delta_own" if own else "delta_far",
        cost_estimate=pl.CostEstimate(
            flops=2 * rows * nblk * per_row * LANES * LANES * 4,
            bytes_accessed=2 * tiles.size + 4 * a.size,
            transcendentals=0,
        ),
    )(meta, cols, a, b, tiles)


def base_kernel(merge, cap, meta_ref, a_ref, b_ref, w_ref, *rest):
    if merge:
        mine_ref, other_ref, ca_ref, cb_ref, both, hot = rest
    else:
        ca_ref, cb_ref, both = rest
    count = a_ref.shape[0]
    feats = w_ref.shape[0]

    @pl.when(pl.program_id(0) == 0)
    def _():
        both[:count] = a_ref[:, :feats]
        both[count:] = b_ref[:, :feats]
        if merge:
            me = meta_ref[0]
            mate = me + 1 - 2 * (me % 2)
            for g, ref in enumerate((a_ref, b_ref)):
                tenants = tenant_lanes(ref)
                mine = one_hot(slots_of(tenants, me), g * cap)
                other = one_hot(slots_of(tenants, mate), (1 - g) * cap)
                hot[0, g * count : (g + 1) * count] = mine
                hot[1, g * count : (g + 1) * count] = other

    total = jnp.dot(both[...], w_ref[...], preferred_element_type=F32)
    if merge:
        total += jnp.dot(hot[0][:, : 2 * cap], mine_ref[...], preferred_element_type=F32)
        total += jnp.dot(hot[1][:, : 2 * cap], other_ref[...], preferred_element_type=F32)
    ca_ref[...] = total[:count].astype(BF)
    cb_ref[...] = total[count:].astype(BF)


def base_of(cap, meta, a, b, weight, mine=None, other=None):
    count = a.shape[0]
    feats, bw = weight.shape
    bn = min(256, bw)
    merge = mine is not None
    full = lambda s: pl.BlockSpec(s, lambda i, *_: (0,) * len(s))
    scratch = [pltpu.VMEM((2 * count, feats), BF)]
    specs = [full(a.shape), full(b.shape), pl.BlockSpec((feats, bn), lambda i, *_: (0, i))]
    args = [a, b, weight]
    if merge:
        scratch.append(pltpu.VMEM((2, 2 * count, LANES), BF))
        specs += [pl.BlockSpec((2 * cap, bn), lambda i, *_: (0, i))] * 2
        args += [mine, other]
    return pl.pallas_call(
        functools.partial(base_kernel, merge, cap),
        grid_spec=pltpu.PrefetchScalarGridSpec(
            num_scalar_prefetch=1,
            grid=(bw // bn,),
            in_specs=specs,
            out_specs=[pl.BlockSpec((count, bn), lambda i, *_: (0, i))] * 2,
            scratch_shapes=scratch,
        ),
        out_shape=[jax.ShapeDtypeStruct((count, bw), BF)] * 2,
        compiler_params=params(),
        name="base_far" if merge else "base_own",
        cost_estimate=pl.CostEstimate(
            flops=4 * count * feats * bw, bytes_accessed=2 * weight.size + 4 * a.size, transcendentals=0
        ),
    )(meta, *args)


def merge_kernel(cap, groups, nz, meta_ref, own_ref, dself_ref, dmate_ref, cself_ref, cmate_ref, *rest):
    pairs = groups // 2
    far = rest[: 4 * (pairs - 1)]
    outs, acc = rest[4 * (pairs - 1) : -1], rest[-1]
    me, z = meta_ref[0], meta_ref[1]
    mate = me + 1 - 2 * (me % 2)
    chip = me // 2
    width = acc.shape[1]
    bw = width // groups
    tenants = tenant_lanes(own_ref)

    def hot(tenant, offset):
        return one_hot(slots_of(tenants, tenant), offset)

    near = (hot(me, 0) + hot(mate, cap))[:, : 2 * cap]
    step = min(512, bw)
    for start in range(0, width, step):
        at = pl.ds(start, step)
        rows = jnp.concatenate([dself_ref[:, at].astype(F32), dmate_ref[:, at].astype(F32)], axis=0)
        acc[:, at] = jnp.dot(near, rows.astype(BF), preferred_element_type=F32)

    def add(block, piece):
        at = pl.ds(pl.multiple_of(block * bw, LANES), bw)
        acc[:, at] += piece[...].astype(F32)

    add(me, cself_ref)
    add(mate, cmate_ref)
    for dx in range(1, pairs):
        c_same, c_diag, d_same, d_diag = far[4 * (dx - 1) : 4 * dx]
        source = lax.rem(chip + pairs - dx, pairs)
        same = 2 * source + me % 2
        diag = 2 * source + 1 - me % 2
        add(same, c_same)
        add(diag, c_diag)
        there = (hot(same, 0) + hot(diag, cap))[:, : 2 * cap]
        for e in range(1, pairs):
            target = lax.rem(source + e, pairs)
            for start in range(0, 2 * bw, step):
                at = pl.ds((e - 1) * 2 * bw + start, step)
                rows = jnp.concatenate([d_same[:, at].astype(F32), d_diag[:, at].astype(F32)], axis=0)
                to = pl.ds(pl.multiple_of(target * 2 * bw + start, LANES), step)
                acc[:, to] += jnp.dot(there, rows.astype(BF), preferred_element_type=F32)

    zw = width // nz
    if len(outs) == nz:
        for dz in range(nz):
            block = lax.rem(z + dz, nz)
            at = pl.ds(pl.multiple_of(block * zw, LANES), zw)
            outs[dz][...] = acc[:, at].astype(outs[dz].dtype)
    else:
        outs[0][...] = acc[...].astype(BF)


def merge_of(cap, groups, nz, direct, width, meta, own, *pieces):
    count = own.shape[0]
    zw = width // nz
    if direct:
        shapes = [jax.ShapeDtypeStruct((count, zw), F32 if dz == 0 else BF) for dz in range(nz)]
    else:
        shapes = [jax.ShapeDtypeStruct((count, width), BF)]
    return pl.pallas_call(
        functools.partial(merge_kernel, cap, groups, nz),
        out_shape=shapes,
        in_specs=[smem()] + [whole()] * (1 + len(pieces)),
        out_specs=[whole()] * len(shapes),
        scratch_shapes=[pltpu.VMEM((count, width), F32)],
        compiler_params=params(),
        name="merge",
        cost_estimate=pl.CostEstimate(
            flops=4 * count * width * LANES, bytes_accessed=8 * count * width, transcendentals=0
        ),
    )(meta, own, *pieces)


def shards(groups, nz, gate_in, up_in, down_weight, delta_tiles, delta_cols, tenant_of_row):
    count = gate_in.shape[0]
    pairs = groups // 2
    bw = down_weight.shape[1]
    width = bw * groups
    cap = -(-(count * 3 // (2 * groups)) // 8) * 8
    meta = jnp.stack([lax.axis_index("rows"), lax.axis_index("tensor")]).astype(jnp.int32)
    cols = delta_cols.reshape(-1)
    tiles = delta_tiles[0]

    def rows_to(pick):
        return [(2 * x + c, pick(x, c)) for x in range(pairs) for c in range(2)]

    swap = rows_to(lambda x, c: 2 * x + 1 - c)

    def back(dx):
        return rows_to(lambda x, c: 2 * ((x - dx) % pairs) + c)

    def ahead(dx, cross):
        return rows_to(lambda x, c: 2 * ((x + dx) % pairs) + (1 - c if cross else c))

    def permute(v, perm):
        return lax.ppermute(v, "rows", perm)

    own = hidden_of(gate_in, up_in, tenant_of_row)
    away = [permute(own, back(dx)) for dx in range(1, pairs)]
    mate = permute(own, swap)
    d_self, d_mate = delta_of(True, cap, groups, width, meta, cols, own, mate, tiles)
    d_near = permute(d_mate, swap)
    c_self, c_mate = base_of(cap, meta, own, mate, down_weight)
    c_near = permute(c_mate, swap)
    pieces = [d_self, d_near, c_self, c_near]
    for dx in range(1, pairs):
        same = away[dx - 1]
        diag = permute(same, swap)
        mine, other, d_same, d_diag = delta_of(
            False, cap, groups, width, meta, cols, same, diag, tiles
        )
        other = permute(other, swap)
        d_same = permute(d_same, ahead(dx, False))
        d_diag = permute(d_diag, ahead(dx, True))
        c_same, c_diag = base_of(cap, meta, same, diag, down_weight, mine, other)
        c_same = permute(c_same, ahead(dx, False))
        c_diag = permute(c_diag, ahead(dx, True))
        pieces += [c_same, c_diag, d_same, d_diag]
    direct = nz <= 4
    terms = merge_of(cap, groups, nz, direct, width, meta, own, *pieces)
    if not direct:
        return lax.psum_scatter(terms[0], "tensor", scatter_dimension=1, tiled=True)
    total = terms[0]
    for dz in range(1, nz):
        perm = [(z, (z + dz) % nz) for z in range(nz)]
        total = total + lax.ppermute(terms[dz], "tensor", perm).astype(F32)
    return total.astype(BF)


def solution(mesh):
    groups, nz = mesh.shape["rows"], mesh.shape["tensor"]
    return jax.shard_map(
        functools.partial(shards, groups, nz),
        mesh=mesh,
        in_specs=(
            P(("replica", "rows"), "tensor"),
            P(("replica", "rows"), "tensor"),
            P("tensor", "rows"),
            P("rows", "tensor", None, None, None),
            P("rows", "tensor", None),
            P(("replica", "rows"), None),
        ),
        out_specs=P(("replica", "rows"), "tensor"),
        check_vma=False,
    )
```

time: 147 us -> 106 us (0.72)
  the two profiles are of different devices: /device:TPU:0 before, /device:TPU:13 now
where the time goes in v1:
time: 106 us; the launch traced here: 105 us
  waiting for transfers between devices  51.7 us (49%)
  Pallas kernels  37 us (35%)
  starting transfers between devices  12.1 us (11%)
  local copies, waits for them, and re-layouts  3.69 us (3%)
    ppermute x10, waiting for transfers between devices, permute(): return lax.ppermute(v, 'rows', perm)  29.4 us
    ppermute x3, waiting for transfers between devices, shards(): total = total + lax.ppermute(terms[dz], 'tensor', perm).astype(F32)  22.2 us
    pallas_call x2, Pallas kernels, base_of(): pl.pallas_call(functools.partial(base_kernel, merge, cap), grid_spec=pltp...  20 us
    pallas_call x2, Pallas kernels, delta_of(): pl.pallas_call(functools.partial(delta_kernel, own, cap, bw, chunk), grid...  14.8 us
    ppermute x10, starting transfers between devices, permute(): return lax.ppermute(v, 'rows', perm)  8.2 us
    ppermute x3, starting transfers between devices, shards(): total = total + lax.ppermute(terms[dz], 'tensor', perm).astype(F32)  3.86 us
    unnamed x6, local copies, waits for them, and re-layouts  3.59 us
  transfers between devices with their start and end apart: 13, of which 6 were waited for; matrix products, arithmetic and copies ran while one was open for 1% of the time, Pallas kernels for 33%

profile of v1, /device:TPU:13, one launch (start us, length us, event | category | flops | bytes accessed | tf_op | source)
XLA Modules:
  0.0 105.4 jit_solution(14145782611940868857)
XLA Ops:
  0.0 0.7 copy.8.tenant_ref
  0.7 0.0 copy-start
  0.7 1.0 copy-done
  1.8 0.0 copy-start.1
  1.8 1.0 copy-done.1
  2.8 0.4 hidden.1.a_ref.own_ref
  3.2 1.3 %collective-permute-start.3 = (bf16[64,4224]{1,0:T(8,128)(2,1)S(1)}, bf16[64,4224]{1,0:T(8,128)(2,1)S(1)}, u32[]{:S(2)}, u32[]{:S(2)}) collective-permute-start(bf16[64,4224]{1,0:T(8,128)(2,1)S(1)} %hidden.1.a_ref.own_ref), channel_id=1, source_target_pairs={{0,8},{4,12},{8,0},{12,4},{1,9},{5,13},{9,1},{13,5},{2,10},{6,14},... | collective-permute-start | bytes 1622024 | tf_op jit(solution)/shard_map/ppermute | solution.py:330
  4.5 1.0 collective-permute-start
  5.5 11.0 %collective-permute-done.3.a_ref = bf16[64,4224]{1,0:T(8,128)(2,1)S(1)} collective-permute-done((bf16[64,4224]{1,0:T(8,128)(2,1)S(1)}, bf16[64,4224]{1,0:T(8,128)(2,1)S(1)}, u32[]{:S(2)}, u32[]{:S(2)}) %collective-permute-start.3) | collective-permute-done | bytes 540704 | tf_op jit(solution)/shard_map/ppermute | solution.py:330
  16.4 1.5 %collective-permute-start.4 = (bf16[64,4224]{1,0:T(8,128)(2,1)S(1)}, bf16[64,4224]{1,0:T(8,128)(2,1)S(1)}, u32[]{:S(2)}, u32[]{:S(2)}) collective-permute-start(bf16[64,4224]{1,0:T(8,128)(2,1)S(1)} %collective-permute-done.3.a_ref), channel_id=1, source_target_pairs={{0,4},{4,0},{8,12},{12,8},{1,5},{5,1},{9,13},{13,9},{2,6},{6,2},{1... | collective-permute-start | bytes 1622024 | tf_op jit(solution)/shard_map/ppermute | solution.py:330
  18.0 0.8 copy.9
  18.8 0.1 reshape.3.cols_ref
  18.9 0.1 pad_add_fusion.meta_ref
  18.9 0.0 collective-permute-done.b_ref
  18.9 7.4 %delta_own.1 = (bf16[24,8192]{1,0:T(8,128)(2,1)S(1)}, bf16[24,8192]{1,0:T(8,128)(2,1)S(1)}) custom-call(s32[2]{0:T(128)S(1)} %pad_add_fusion.meta_ref, s32[192]{0:T(256)S(1)} %reshape.3.cols_ref, bf16[64,4224]{1,0:T(8,128)(2,1)S(1)} %hidden.1.a_ref.own_ref, bf16[64,4224]{1,0:T(8,128)(2,1)S(1)} %collective-permute-done.b_ref, bf16[32,6,128,128]{3,2,1,0:T(8,128)(2,1)} %bitcast.3), custom_call_target="tpu_custom_call" | custom-call | flops 1207959552 | bytes 7372800 | tf_op jit(solution)/shard_map/delta_own/pallas_call | solution.py:146
  26.3 0.1 collective-permute-start.1
  26.4 0.0 collective-permute-done.4.b_ref
  26.4 7.4 %delta_far.1 = (bf16[48,2048]{1,0:T(8,128)(2,1)S(1)}, bf16[48,2048]{1,0:T(8,128)(2,1)S(1)}, bf16[24,4096]{1,0:T(8,128)(2,1)S(1)}, bf16[24,4096]{1,0:T(8,128)(2,1)S(1)}) custom-call(s32[2]{0:T(128)S(1)} %pad_add_fusion.meta_ref, s32[192]{0:T(256)S(1)} %reshape.3.cols_ref, bf16[64,4224]{1,0:T(8,128)(2,1)S(1)} %collective-permute-done.3.a_ref, ...), custom_call_target="tpu_custom_call" | custom-call | flops 1207959552 | bytes 7372800 | tf_op jit(solution)/shard_map/delta_far/pallas_call | solution.py:146
  33.8 0.6 collective-permute-start.5
  34.4 9.9 %base_own.1 = (bf16[64,2048]{1,0:T(8,128)(2,1)S(1)}, bf16[64,2048]{1,0:T(8,128)(2,1)S(1)}) custom-call(s32[2]{0:T(128)S(1)} %pad_add_fusion.meta_ref, bf16[64,4224]{1,0:T(8,128)(2,1)S(1)} %hidden.1.a_ref.own_ref, bf16[64,4224]{1,0:T(8,128)(2,1)S(1)} %collective-permute-done.b_ref, bf16[4096,2048]{1,0:T(8,128)(2,1)} %w_ref.3), custom_call_target="tpu_custom_call" | custom-call | flops 2147483648 | bytes 17858560 | tf_op jit(solution)/shard_map/base_own/pallas_call | solution.py:216
  44.3 0.1 collective-permute-start.2
  44.4 0.0 collective-permute-done.5.rest_1_
  44.4 10.1 %base_far.1 = (bf16[64,2048]{1,0:T(8,128)(2,1)S(1)}, bf16[64,2048]{1,0:T(8,128)(2,1)S(1)}) custom-call(s32[2]{0:T(128)S(1)} %pad_add_fusion.meta_ref, bf16[64,4224]{1,0:T(8,128)(2,1)S(1)} %collective-permute-done.3.a_ref, bf16[64,4224]{1,0:T(8,128)(2,1)S(1)} %collective-permute-done.4.b_ref, bf16[4096,2048]{1,0:T(8,128)(2,1)} %w_ref.3, ...), custom_call_target="tpu_custom_call" | custom-call | flops 2147483648 | bytes 17858560 | tf_op jit(solution)/shard_map/base_far/pallas_call | solution.py:216
  54.5 1.3 %collective-permute-start.6 = (bf16[64,2048]{1,0:T(8,128)(2,1)S(1)}, bf16[64,2048]{1,0:T(8,128)(2,1)S(1)}, u32[]{:S(2)}, u32[]{:S(2)}) collective-permute-start(bf16[64,2048]{1,0:T(8,128)(2,1)S(1)} %get-tuple-element.25), channel_id=1, source_target_pairs={{0,8},{4,12},{8,0},{12,4},{1,9},{5,13},{9,1},{13,5},{2,10},{6,14},... | collective-permute-start | bytes 786440 | tf_op jit(solution)/shard_map/ppermute | solution.py:330
  55.8 0.9 collective-permute-start.7
  56.7 1.2 %collective-permute-start.8 = (bf16[24,4096]{1,0:T(8,128)(2,1)S(1)}, bf16[24,4096]{1,0:T(8,128)(2,1)S(1)}, u32[]{:S(2)}, u32[]{:S(2)}) collective-permute-start(bf16[24,4096]{1,0:T(8,128)(2,1)S(1)} %get-tuple-element.27), channel_id=1, source_target_pairs={{0,8},{4,12},{8,0},{12,4},{1,9},{5,13},{9,1},{13,5},{2,10},{6,14},... | collective-permute-start | bytes 589832 | tf_op jit(solution)/shard_map/ppermute | solution.py:330
  57.9 0.0 collective-permute-done.2.cmate_ref
  57.9 0.3 collective-permute-start.9
  58.2 0.0 collective-permute-done.1.dmate_ref
  58.2 13.6 %collective-permute-done.8.rest_2_ = bf16[24,4096]{1,0:T(8,128)(2,1)S(1)} collective-permute-done((bf16[24,4096]{1,0:T(8,128)(2,1)S(1)}, bf16[24,4096]{1,0:T(8,128)(2,1)S(1)}, u32[]{:S(2)}, u32[]{:S(2)}) %collective-permute-start.8) | collective-permute-done | bytes 196640 | tf_op jit(solution)/shard_map/ppermute | solution.py:330
  71.8 4.9 %collective-permute-done.9.rest_3_ = bf16[24,4096]{1,0:T(8,128)(2,1)S(1)} collective-permute-done((bf16[24,4096]{1,0:T(8,128)(2,1)S(1)}, bf16[24,4096]{1,0:T(8,128)(2,1)S(1)}, u32[]{:S(2)}, u32[]{:S(2)}) %collective-permute-start.9) | collective-permute-done | bytes 196640 | tf_op jit(solution)/shard_map/ppermute | solution.py:330
  76.7 0.0 collective-permute-done.6.rest_0_
  76.7 0.0 collective-permute-done.7.rest_1_
  76.7 1.7 %merge.1 = (f32[64,2048]{1,0:T(8,128)S(1)}, bf16[64,2048]{1,0:T(8,128)(2,1)S(1)}, bf16[64,2048]{1,0:T(8,128)(2,1)S(1)}, bf16[64,2048]{1,0:T(8,128)(2,1)S(1)}) custom-call(s32[2]{0:T(128)S(1)} %pad_add_fusion.meta_ref, bf16[64,4224]{1,0:T(8,128)(2,1)S(1)} %hidden.1.a_ref.own_ref, bf16[24,8192]{1,0:T(8,128)(2,1)S(1)} %get-tuple-element.19.dself_ref, ...), custom_call_target="tpu_custom_call" | custom-call | flops 268435456 | bytes 4194304 | tf_op jit(solution)/shard_map/merge/pallas_call | solution.py:294
  78.4 1.4 %collective-permute-start.10 = (bf16[64,2048]{1,0:T(8,128)(2,1)S(1)}, bf16[64,2048]{1,0:T(8,128)(2,1)S(1)}, u32[]{:S(2)}, u32[]{:S(2)}) collective-permute-start(bf16[64,2048]{1,0:T(8,128)(2,1)S(1)} %get-tuple-element.30), channel_id=1, source_target_pairs={{0,1},{1,2},{2,3},{3,0},{4,5},{5,6},{6,7},{7,4},{8,9},{9,10},{10,1... | collective-permute-start | bytes 786440 | tf_op jit(solution)/shard_map/ppermute | solution.py:360
  79.8 1.1 %collective-permute-start.11 = (bf16[64,2048]{1,0:T(8,128)(2,1)S(1)}, bf16[64,2048]{1,0:T(8,128)(2,1)S(1)}, u32[]{:S(2)}, u32[]{:S(2)}) collective-permute-start(bf16[64,2048]{1,0:T(8,128)(2,1)S(1)} %get-tuple-element.31), channel_id=1, source_target_pairs={{0,2},{1,3},{2,0},{3,1},{4,6},{5,7},{6,4},{7,5},{8,10},{9,11},{10,... | collective-permute-start | bytes 786440 | tf_op jit(solution)/shard_map/ppermute | solution.py:360
  80.9 1.4 %collective-permute-start.12 = (bf16[64,2048]{1,0:T(8,128)(2,1)S(1)}, bf16[64,2048]{1,0:T(8,128)(2,1)S(1)}, u32[]{:S(2)}, u32[]{:S(2)}) collective-permute-start(bf16[64,2048]{1,0:T(8,128)(2,1)S(1)} %get-tuple-element.32), channel_id=1, source_target_pairs={{0,3},{1,0},{2,1},{3,2},{4,7},{5,4},{6,5},{7,6},{8,11},{9,8},{10,9... | collective-permute-start | bytes 786440 | tf_op jit(solution)/shard_map/ppermute | solution.py:360
  82.3 4.3 %collective-permute-done.10 = bf16[64,2048]{1,0:T(8,128)(2,1)S(1)} collective-permute-done((bf16[64,2048]{1,0:T(8,128)(2,1)S(1)}, bf16[64,2048]{1,0:T(8,128)(2,1)S(1)}, u32[]{:S(2)}, u32[]{:S(2)}) %collective-permute-start.10) | collective-permute-done | bytes 262176 | tf_op jit(solution)/shard_map/ppermute | solution.py:360
  86.6 16.0 %collective-permute-done.11 = bf16[64,2048]{1,0:T(8,128)(2,1)S(1)} collective-permute-done((bf16[64,2048]{1,0:T(8,128)(2,1)S(1)}, bf16[64,2048]{1,0:T(8,128)(2,1)S(1)}, u32[]{:S(2)}, u32[]{:S(2)}) %collective-permute-start.11) | collective-permute-done | bytes 262176 | tf_op jit(solution)/shard_map/ppermute | solution.py:360
  102.5 2.0 %collective-permute-done.12 = bf16[64,2048]{1,0:T(8,128)(2,1)S(1)} collective-permute-done((bf16[64,2048]{1,0:T(8,128)(2,1)S(1)}, bf16[64,2048]{1,0:T(8,128)(2,1)S(1)}, u32[]{:S(2)}, u32[]{:S(2)}) %collective-permute-start.12) | collective-permute-done | bytes 262176 | tf_op jit(solution)/shard_map/ppermute | solution.py:360
  104.5 0.8 add_convert_fusion
Async XLA Ops:
  0.7 1.0 copy-start
  1.8 1.0 copy-start.1
  3.2 13.2 %collective-permute-start.3 = (bf16[64,4224]{1,0:T(8,128)(2,1)S(1)}, bf16[64,4224]{1,0:T(8,128)(2,1)S(1)}, u32[]{:S(2)}, u32[]{:S(2)}) collective-permute-start(bf16[64,4224]{1,0:T(8,128)(2,1)S(1)} %hidden.1.a_ref.own_ref), channel_id=1, source_target_pairs={{0,8},{4,12},{8,0},{12,4},{1,9},{5,13},{9,1},{13,5},{2,10},{6,14},... | collective-permute-start | bytes 1622024 | tf_op jit(solution)/shard_map/ppermute | solution.py:330
  4.5 14.4 %collective-permute-start = (bf16[64,4224]{1,0:T(8,128)(2,1)S(1)}, bf16[64,4224]{1,0:T(8,128)(2,1)S(1)}, u32[]{:S(2)}, u32[]{:S(2)}) collective-permute-start(bf16[64,4224]{1,0:T(8,128)(2,1)S(1)} %hidden.1.a_ref.own_ref), channel_id=1, source_target_pairs={{0,4},{4,0},{8,12},{12,8},{1,5},{5,1},{9,13},{13,9},{2,6},{6,2},{1... | collective-permute-start | bytes 1622024 | tf_op jit(solution)/shard_map/ppermute | solution.py:330
  16.4 10.0 %collective-permute-start.4 = (bf16[64,4224]{1,0:T(8,128)(2,1)S(1)}, bf16[64,4224]{1,0:T(8,128)(2,1)S(1)}, u32[]{:S(2)}, u32[]{:S(2)}) collective-permute-start(bf16[64,4224]{1,0:T(8,128)(2,1)S(1)} %collective-permute-done.3.a_ref), channel_id=1, source_target_pairs={{0,4},{4,0},{8,12},{12,8},{1,5},{5,1},{9,13},{13,9},{2,6},{6,2},{1... | collective-permute-start | bytes 1622024 | tf_op jit(solution)/shard_map/ppermute | solution.py:330
  26.3 31.9 %collective-permute-start.1 = (bf16[24,8192]{1,0:T(8,128)(2,1)S(1)}, bf16[24,8192]{1,0:T(8,128)(2,1)S(1)}, u32[]{:S(2)}, u32[]{:S(2)}) collective-permute-start(bf16[24,8192]{1,0:T(8,128)(2,1)S(1)} %get-tuple-element.20), channel_id=1, source_target_pairs={{0,4},{4,0},{8,12},{12,8},{1,5},{5,1},{9,13},{13,9},{2,6},{6,2},{1... | collective-permute-start | bytes 1179656 | tf_op jit(solution)/shard_map/ppermute | solution.py:330
  33.8 10.6 %collective-permute-start.5 = (bf16[48,2048]{1,0:T(8,128)(2,1)S(1)}, bf16[48,2048]{1,0:T(8,128)(2,1)S(1)}, u32[]{:S(2)}, u32[]{:S(2)}) collective-permute-start(bf16[48,2048]{1,0:T(8,128)(2,1)S(1)} %get-tuple-element.24), channel_id=1, source_target_pairs={{0,4},{4,0},{8,12},{12,8},{1,5},{5,1},{9,13},{13,9},{2,6},{6,2},{1... | collective-permute-start | bytes 589832 | tf_op jit(solution)/shard_map/ppermute | solution.py:330
  44.3 13.6 %collective-permute-start.2 = (bf16[64,2048]{1,0:T(8,128)(2,1)S(1)}, bf16[64,2048]{1,0:T(8,128)(2,1)S(1)}, u32[]{:S(2)}, u32[]{:S(2)}) collective-permute-start(bf16[64,2048]{1,0:T(8,128)(2,1)S(1)} %get-tuple-element.22), channel_id=1, source_target_pairs={{0,4},{4,0},{8,12},{12,8},{1,5},{5,1},{9,13},{13,9},{2,6},{6,2},{1... | collective-permute-start | bytes 786440 | tf_op jit(solution)/shard_map/ppermute | solution.py:330
  54.5 22.1 %collective-permute-start.6 = (bf16[64,2048]{1,0:T(8,128)(2,1)S(1)}, bf16[64,2048]{1,0:T(8,128)(2,1)S(1)}, u32[]{:S(2)}, u32[]{:S(2)}) collective-permute-start(bf16[64,2048]{1,0:T(8,128)(2,1)S(1)} %get-tuple-element.25), channel_id=1, source_target_pairs={{0,8},{4,12},{8,0},{12,4},{1,9},{5,13},{9,1},{13,5},{2,10},{6,14},... | collective-permute-start | bytes 786440 | tf_op jit(solution)/shard_map/ppermute | solution.py:330
  55.8 20.9 %collective-permute-start.7 = (bf16[64,2048]{1,0:T(8,128)(2,1)S(1)}, bf16[64,2048]{1,0:T(8,128)(2,1)S(1)}, u32[]{:S(2)}, u32[]{:S(2)}) collective-permute-start(bf16[64,2048]{1,0:T(8,128)(2,1)S(1)} %get-tuple-element.26), channel_id=1, source_target_pairs={{0,12},{4,8},{8,4},{12,0},{1,13},{5,9},{9,5},{13,1},{2,14},{6,10},... | collective-permute-start | bytes 786440 | tf_op jit(solution)/shard_map/ppermute | solution.py:330
  56.7 15.1 %collective-permute-start.8 = (bf16[24,4096]{1,0:T(8,128)(2,1)S(1)}, bf16[24,4096]{1,0:T(8,128)(2,1)S(1)}, u32[]{:S(2)}, u32[]{:S(2)}) collective-permute-start(bf16[24,4096]{1,0:T(8,128)(2,1)S(1)} %get-tuple-element.27), channel_id=1, source_target_pairs={{0,8},{4,12},{8,0},{12,4},{1,9},{5,13},{9,1},{13,5},{2,10},{6,14},... | collective-permute-start | bytes 589832 | tf_op jit(solution)/shard_map/ppermute | solution.py:330
  57.9 18.7 %collective-permute-start.9 = (bf16[24,4096]{1,0:T(8,128)(2,1)S(1)}, bf16[24,4096]{1,0:T(8,128)(2,1)S(1)}, u32[]{:S(2)}, u32[]{:S(2)}) collective-permute-start(bf16[24,4096]{1,0:T(8,128)(2,1)S(1)} %get-tuple-element.28), channel_id=1, source_target_pairs={{0,12},{4,8},{8,4},{12,0},{1,13},{5,9},{9,5},{13,1},{2,14},{6,10},... | collective-permute-start | bytes 589832 | tf_op jit(solution)/shard_map/ppermute | solution.py:330
  78.4 8.2 %collective-permute-start.10 = (bf16[64,2048]{1,0:T(8,128)(2,1)S(1)}, bf16[64,2048]{1,0:T(8,128)(2,1)S(1)}, u32[]{:S(2)}, u32[]{:S(2)}) collective-permute-start(bf16[64,2048]{1,0:T(8,128)(2,1)S(1)} %get-tuple-element.30), channel_id=1, source_target_pairs={{0,1},{1,2},{2,3},{3,0},{4,5},{5,6},{6,7},{7,4},{8,9},{9,10},{10,1... | collective-permute-start | bytes 786440 | tf_op jit(solution)/shard_map/ppermute | solution.py:360
  79.8 22.7 %collective-permute-start.11 = (bf16[64,2048]{1,0:T(8,128)(2,1)S(1)}, bf16[64,2048]{1,0:T(8,128)(2,1)S(1)}, u32[]{:S(2)}, u32[]{:S(2)}) collective-permute-start(bf16[64,2048]{1,0:T(8,128)(2,1)S(1)} %get-tuple-element.31), channel_id=1, source_target_pairs={{0,2},{1,3},{2,0},{3,1},{4,6},{5,7},{6,4},{7,5},{8,10},{9,11},{10,... | collective-permute-start | bytes 786440 | tf_op jit(solution)/shard_map/ppermute | solution.py:360
  80.9 23.6 %collective-permute-start.12 = (bf16[64,2048]{1,0:T(8,128)(2,1)S(1)}, bf16[64,2048]{1,0:T(8,128)(2,1)S(1)}, u32[]{:S(2)}, u32[]{:S(2)}) collective-permute-start(bf16[64,2048]{1,0:T(8,128)(2,1)S(1)} %get-tuple-element.32), channel_id=1, source_target_pairs={{0,3},{1,0},{2,1},{3,2},{4,7},{5,4},{6,5},{7,6},{8,11},{9,8},{10,9... | collective-permute-start | bytes 786440 | tf_op jit(solution)/shard_map/ppermute | solution.py:360

commit v2 on v0

v2 whole, which is shorter than its diff:
```python
import functools

import jax
import jax.numpy as jnp
from jax import lax
from jax.experimental import pallas as pl
from jax.experimental.pallas import tpu as pltpu
from jax.sharding import PartitionSpec as P

BF = jnp.bfloat16
F32 = jnp.float32
LANES = 128
VMEM_LIMIT = 28 * 1024 * 1024
PARTS = 2


def params():
    return pltpu.CompilerParams(vmem_limit_bytes=VMEM_LIMIT)


def whole():
    return pl.BlockSpec(memory_space=pltpu.VMEM)


def smem():
    return pl.BlockSpec(memory_space=pltpu.SMEM)


def hidden_kernel(tenant_ref, gate_ref, up_ref, out_ref):
    width = gate_ref.shape[1]
    count, total = out_ref.shape
    step = pl.program_id(0)
    for start in range(0, width, 512):
        at = pl.ds(start, min(512, width - start))
        v = gate_ref[:, at].astype(F32)
        to = pl.ds(pl.multiple_of(step * width + start, LANES), min(512, width - start))
        out_ref[:, to] = (v / (1.0 + jnp.exp(-v)) * up_ref[:, at].astype(F32)).astype(BF)

    @pl.when(step == 0)
    def _():
        row = jnp.broadcast_to(tenant_ref[...].astype(F32), (count, count))
        diagonal = lax.broadcasted_iota(jnp.int32, (count, count), 0) == lax.broadcasted_iota(
            jnp.int32, (count, count), 1
        )
        column = jnp.sum(jnp.where(diagonal, row, 0.0), axis=1, keepdims=True)
        out_ref[:, total - LANES :] = jnp.broadcast_to(column, (count, LANES)).astype(BF)


def hidden_of(gate, up, tenant):
    count, feats = gate.shape
    steps = 4 if feats % (4 * LANES) == 0 else 1
    part = pl.BlockSpec((count, feats // steps), lambda i: (0, i))
    return pl.pallas_call(
        hidden_kernel,
        grid=(steps,),
        out_shape=jax.ShapeDtypeStruct((count, feats + LANES), BF),
        in_specs=[pl.BlockSpec((1, count), lambda i: (0, 0)), part, part],
        out_specs=pl.BlockSpec((count, feats + LANES), lambda i: (0, 0)),
        compiler_params=params(),
        name="hidden",
        cost_estimate=pl.CostEstimate(
            flops=6 * count * feats, bytes_accessed=6 * count * feats, transcendentals=count * feats
        ),
    )(tenant.reshape(1, count), gate, up)


def slots_of(tenants, tenant):
    count = tenants.shape[0]
    mine = tenants == tenant.astype(F32)
    ones = jnp.where(mine, 1.0, 0.0).astype(BF)
    above = lax.broadcasted_iota(jnp.int32, (count, count), 0) > lax.broadcasted_iota(
        jnp.int32, (count, count), 1
    )
    earlier = jnp.dot(jnp.where(above, 1.0, 0.0).astype(BF), ones, preferred_element_type=F32)
    return jnp.where(mine, earlier, -1024.0)


def one_hot(slots, offset):
    lanes = lax.broadcasted_iota(jnp.int32, slots.shape, 1).astype(F32)
    return jnp.where(slots + offset == lanes, 1.0, 0.0).astype(BF)


def tenant_lanes(hidden_ref):
    return hidden_ref[:, hidden_ref.shape[1] - LANES :].astype(F32)


def pack_rows(cap, me, a_ref, b_ref, packed):
    feats = packed.shape[1]
    hot = jnp.concatenate(
        [
            one_hot(slots_of(tenant_lanes(a_ref), me), 0),
            one_hot(slots_of(tenant_lanes(b_ref), me), cap),
        ],
        axis=0,
    )
    for start in range(0, feats, 512):
        at = pl.ds(start, min(512, feats - start))
        both = jnp.concatenate([a_ref[:, at], b_ref[:, at]], axis=0)
        rows = lax.dot_general(hot, both, (((0,), (0,)), ((), ())), preferred_element_type=F32)
        packed[:, at] = rows[: 2 * cap].astype(BF)


def add_tiles(first, last, cols_ref, packed, tiles_ref, acc):
    per_row = tiles_ref.shape[1]
    for row in range(first, last):
        lhs = packed[:, row * LANES : (row + 1) * LANES]
        rhs = jnp.concatenate([tiles_ref[row, j] for j in range(per_row)], axis=1)
        prods = jnp.dot(lhs, rhs, preferred_element_type=F32)
        at = [cols_ref[row * per_row + j] for j in range(per_row)]
        old = [acc[at[j]] for j in range(per_row)]
        for j in range(per_row):
            acc[at[j]] = old[j] + prods[:, j * LANES : (j + 1) * LANES]


def near_kernel(cap, nt, nw, *refs):
    meta_ref, cols_ref, a_ref, b_ref, tiles_ref, w_ref = refs[:6]
    da_ref, db_ref, ca_ref, cb_ref, tv_ref, wv_ref = refs[6:12]
    packed, acc, both, tsem, wsem = refs[12:]
    count = a_ref.shape[0]
    feats, bw = w_ref.shape
    nblk = tiles_ref.shape[0]
    tpart, wpart = nblk // nt, bw // nw
    tcopies = [
        pltpu.make_async_copy(
            tiles_ref.at[pl.ds(i * tpart, tpart)], tv_ref.at[pl.ds(i * tpart, tpart)], tsem.at[i]
        )
        for i in range(nt)
    ]
    wcopies = [
        pltpu.make_async_copy(
            w_ref.at[:, pl.ds(i * wpart, wpart)], wv_ref.at[:, pl.ds(i * wpart, wpart)], wsem.at[i]
        )
        for i in range(nw)
    ]
    for copy in tcopies + wcopies:
        copy.start()
    pack_rows(cap, meta_ref[0], a_ref, b_ref, packed)
    acc[...] = jnp.zeros_like(acc)
    both[:count] = a_ref[:, :feats]
    both[count:] = b_ref[:, :feats]
    for i in range(nt):
        tcopies[i].wait()
        add_tiles(i * tpart, (i + 1) * tpart, cols_ref, packed, tv_ref, acc)
    for n in range(acc.shape[0]):
        got = acc[n]
        da_ref[:, n * LANES : (n + 1) * LANES] = got[:cap].astype(BF)
        db_ref[:, n * LANES : (n + 1) * LANES] = got[cap:].astype(BF)
    for i in range(nw):
        at = slice(i * wpart, (i + 1) * wpart)
        wcopies[i].wait()
        total = jnp.dot(both[...], wv_ref[:, at], preferred_element_type=F32)
        ca_ref[:, at] = total[:count].astype(BF)
        cb_ref[:, at] = total[count:].astype(BF)


def near_of(cap, width, meta, cols, a, b, tiles, weight):
    count = a.shape[0]
    feats, bw = weight.shape
    nblk = tiles.shape[0]
    nt, nw = (4 if nblk % 4 == 0 else 1), max(1, bw // 512)
    any_space = pl.BlockSpec(memory_space=pl.ANY)
    return pl.pallas_call(
        functools.partial(near_kernel, cap, nt, nw),
        in_specs=[smem(), smem(), whole(), whole(), any_space, any_space],
        out_specs=[whole()] * 6,
        out_shape=[
            jax.ShapeDtypeStruct((cap, width), BF),
            jax.ShapeDtypeStruct((cap, width), BF),
            jax.ShapeDtypeStruct((count, bw), BF),
            jax.ShapeDtypeStruct((count, bw), BF),
            pltpu.VMEM(tiles.shape, BF),
            pltpu.VMEM(weight.shape, BF),
        ],
        scratch_shapes=[
            pltpu.VMEM((2 * cap, feats), BF),
            pltpu.VMEM((width // LANES, 2 * cap, LANES), F32),
            pltpu.VMEM((2 * count, feats), BF),
            pltpu.SemaphoreType.DMA((nt,)),
            pltpu.SemaphoreType.DMA((nw,)),
        ],
        compiler_params=params(),
        name="near",
        cost_estimate=pl.CostEstimate(
            flops=4 * count * feats * bw,
            bytes_accessed=4 * weight.size + 4 * tiles.size,
            transcendentals=0,
        ),
    )(meta, cols, a, b, tiles, weight)


def far_kernel(cap, bw, *refs):
    meta_ref, cols_ref, a_ref, b_ref, tiles_ref, own_ref, mate_ref, da_ref, db_ref, packed, acc = refs
    me = meta_ref[0]
    chip = me // 2
    ncol = acc.shape[0]
    tiles = bw // LANES
    pairs = ncol // (2 * tiles)
    pack_rows(cap, me, a_ref, b_ref, packed)
    acc[...] = jnp.zeros_like(acc)
    add_tiles(0, tiles_ref.shape[0], cols_ref, packed, tiles_ref, acc)
    for n in range(tiles):
        at = slice(n * LANES, (n + 1) * LANES)
        mate_ref[:, at] = acc[(me + 1 - 2 * (me % 2)) * tiles + n].astype(BF)
        own_ref[:, at] = acc[me * tiles + n].astype(BF)
        got = []
        for e in range(1, pairs):
            first = lax.rem(chip + e, pairs) * 2 * tiles
            got += [acc[first + n], acc[first + tiles + n]]
        da_ref[:, at] = jnp.concatenate([v[:cap] for v in got], axis=0).astype(BF)
        db_ref[:, at] = jnp.concatenate([v[cap:] for v in got], axis=0).astype(BF)


def far_of(cap, groups, width, meta, cols, a, b, tiles):
    feats = tiles.shape[0] * LANES
    bw = width // groups
    away = (groups - 2) * cap
    return pl.pallas_call(
        functools.partial(far_kernel, cap, bw),
        in_specs=[smem(), smem(), whole(), whole(), whole()],
        out_specs=[whole()] * 4,
        out_shape=[jax.ShapeDtypeStruct((rows, bw), BF) for rows in (2 * cap, 2 * cap, away, away)],
        scratch_shapes=[
            pltpu.VMEM((2 * cap, feats), BF),
            pltpu.VMEM((width // LANES, 2 * cap, LANES), F32),
        ],
        compiler_params=params(),
        name="far",
        cost_estimate=pl.CostEstimate(
            flops=16 * cap * tiles.size, bytes_accessed=2 * tiles.size, transcendentals=0
        ),
    )(meta, cols, a, b, tiles)


def send_kernel(cap, start, *refs):
    meta_ref, a_ref, b_ref, w_ref, mine_ref, other_ref, da_ref, db_ref, ma_ref, mb_ref, both = refs
    count = a_ref.shape[0]
    feats = w_ref.shape[0]
    sub = ma_ref.shape[1]
    both[:count] = a_ref[:, :feats]
    both[count:] = b_ref[:, :feats]
    me = meta_ref[0]
    mate = me + 1 - 2 * (me % 2)
    mine, other = [], []
    for g, ref in enumerate((a_ref, b_ref)):
        tenants = tenant_lanes(ref)
        mine.append(one_hot(slots_of(tenants, me), g * cap)[:, : 2 * cap])
        other.append(one_hot(slots_of(tenants, mate), (1 - g) * cap)[:, : 2 * cap])
    mine, other = jnp.concatenate(mine, axis=0), jnp.concatenate(other, axis=0)
    step = min(256, sub)
    for n in range(0, sub, step):
        at, to = pl.ds(start + n, step), pl.ds(n, step)
        total = jnp.dot(both[...], w_ref[:, at], preferred_element_type=F32)
        total += jnp.dot(mine, mine_ref[:, at], preferred_element_type=F32)
        total += jnp.dot(other, other_ref[:, at], preferred_element_type=F32)
        ma_ref[:count, to] = total[:count].astype(BF)
        mb_ref[:count, to] = total[count:].astype(BF)
    ma_ref[count:] = da_ref[:, pl.ds(start, sub)]
    mb_ref[count:] = db_ref[:, pl.ds(start, sub)]


def send_of(cap, start, sub, meta, a, b, weight, mine, other, da, db):
    count = a.shape[0]
    feats = weight.shape[0]
    rows = count + da.shape[0]
    return pl.pallas_call(
        functools.partial(send_kernel, cap, start),
        in_specs=[smem()] + [whole()] * 7,
        out_specs=[whole()] * 2,
        out_shape=[jax.ShapeDtypeStruct((rows, sub), BF)] * 2,
        scratch_shapes=[pltpu.VMEM((2 * count, feats), BF)],
        compiler_params=params(),
        name="send",
        cost_estimate=pl.CostEstimate(
            flops=4 * count * feats * sub, bytes_accessed=2 * feats * sub, transcendentals=0
        ),
    )(meta, a, b, weight, mine, other, da, db)


def merge_kernel(cap, groups, nz, bw, start, *refs):
    meta_ref, own_ref, dself_ref, dmate_ref, cself_ref, cmate_ref = refs[:6]
    pairs = groups // 2
    far = refs[6 : 6 + 2 * (pairs - 1)]
    outs, acc = refs[6 + 2 * (pairs - 1) : -1], refs[-1]
    sub = acc.shape[2]
    me, z = meta_ref[0], meta_ref[1]
    mate = me + 1 - 2 * (me % 2)
    chip = me // 2
    count = own_ref.shape[0]
    tenants = tenant_lanes(own_ref)
    near = one_hot(slots_of(tenants, me), 0) + one_hot(slots_of(tenants, mate), cap)
    near = near[:, : 2 * cap]
    for block in range(groups):
        at = pl.ds(block * bw + start, sub)
        rows = jnp.concatenate([dself_ref[:, at].astype(F32), dmate_ref[:, at].astype(F32)], axis=0)
        acc[block] = jnp.dot(near, rows.astype(BF), preferred_element_type=F32)
    acc[me] += cself_ref[:, start : start + sub].astype(F32)
    acc[mate] += cmate_ref[:, start : start + sub].astype(F32)
    for dx in range(1, pairs):
        source = lax.rem(chip + pairs - dx, pairs)
        for k, owner in enumerate((2 * source + me % 2, 2 * source + 1 - me % 2)):
            got = far[2 * (dx - 1) + k]
            acc[owner] += got[:count].astype(F32)
            slots = slots_of(tenants, owner)
            delta = got[count:]
            for e in range(1, pairs):
                target = lax.rem(source + e, pairs)
                for half in range(2):
                    row = (2 * (e - 1) + half) * cap
                    hot = one_hot(slots, row)[:, : delta.shape[0]]
                    acc[2 * target + half] += jnp.dot(hot, delta, preferred_element_type=F32)
    if len(outs) == nz:
        for dz in range(nz):
            outs[dz][...] = acc[lax.rem(z + dz, nz)].astype(outs[dz].dtype)
    else:
        for block in range(groups):
            outs[0][:, block * bw : (block + 1) * bw] = acc[block].astype(BF)


def merge_of(cap, groups, nz, direct, bw, start, sub, meta, own, *pieces):
    count = own.shape[0]
    if direct:
        shapes = [jax.ShapeDtypeStruct((count, sub), F32 if dz == 0 else BF) for dz in range(nz)]
    else:
        shapes = [jax.ShapeDtypeStruct((count, groups * bw), BF)]
    return pl.pallas_call(
        functools.partial(merge_kernel, cap, groups, nz, bw, start),
        out_shape=shapes,
        in_specs=[smem()] + [whole()] * (1 + len(pieces)),
        out_specs=[whole()] * len(shapes),
        scratch_shapes=[pltpu.VMEM((groups, count, sub), F32)],
        compiler_params=params(),
        name="merge",
        cost_estimate=pl.CostEstimate(
            flops=4 * count * groups * sub * LANES, bytes_accessed=8 * count * groups * sub, transcendentals=0
        ),
    )(meta, own, *pieces)


def shards(groups, nz, gate_in, up_in, down_weight, delta_tiles, delta_cols, tenant_of_row):
    count = gate_in.shape[0]
    pairs = groups // 2
    bw = down_weight.shape[1]
    width = bw * groups
    cap = -(-(count * 3 // (2 * groups)) // 8) * 8
    direct = nz == groups and nz <= 4
    parts = PARTS if direct else 1
    sub = bw // parts
    meta = jnp.stack([lax.axis_index("rows"), lax.axis_index("tensor")]).astype(jnp.int32)
    cols = delta_cols.reshape(-1)
    tiles = delta_tiles[0]

    def rows_to(pick):
        return [(2 * x + c, pick(x, c)) for x in range(pairs) for c in range(2)]

    swap = rows_to(lambda x, c: 2 * x + 1 - c)

    def back(dx):
        return rows_to(lambda x, c: 2 * ((x - dx) % pairs) + c)

    def ahead(dx, cross):
        return rows_to(lambda x, c: 2 * ((x + dx) % pairs) + (1 - c if cross else c))

    def permute(v, perm):
        return lax.ppermute(v, "rows", perm)

    own = hidden_of(gate_in, up_in, tenant_of_row)
    away = [permute(own, back(dx)) for dx in range(1, pairs)]
    mate = permute(own, swap)
    d_self, d_mate, c_self, c_mate, tiles, weight = near_of(
        cap, width, meta, cols, own, mate, tiles, down_weight
    )
    away, c_self = lax.optimization_barrier((away, c_self))
    d_near = permute(d_mate, swap)
    c_near = permute(c_mate, swap)
    messages = [[] for _ in range(parts)]
    for dx in range(1, pairs):
        same = away[dx - 1]
        diag = permute(same, swap)
        mine, other, d_same, d_diag = far_of(cap, groups, width, meta, cols, same, diag, tiles)
        other = permute(other, swap)
        for part in range(parts):
            m_same, m_diag = send_of(
                cap, part * sub, sub, meta, same, diag, weight, mine, other, d_same, d_diag
            )
            messages[part] += [permute(m_same, ahead(dx, False)), permute(m_diag, ahead(dx, True))]
    out = []
    for part in range(parts):
        terms = merge_of(
            cap, groups, nz, direct, bw, part * sub, sub, meta, own,
            d_self, d_near, c_self, c_near, *messages[part],
        )
        if not direct:
            return lax.psum_scatter(terms[0], "tensor", scatter_dimension=1, tiled=True)
        total = terms[0]
        for dz in range(1, nz):
            perm = [(z, (z + dz) % nz) for z in range(nz)]
            total = total + lax.ppermute(terms[dz], "tensor", perm).astype(F32)
        out.append(total.astype(BF))
    return jnp.concatenate(out, axis=1)


def solution(mesh):
    groups, nz = mesh.shape["rows"], mesh.shape["tensor"]
    return jax.shard_map(
        functools.partial(shards, groups, nz),
        mesh=mesh,
        in_specs=(
            P(("replica", "rows"), "tensor"),
            P(("replica", "rows"), "tensor"),
            P("tensor", "rows"),
            P("rows", "tensor", None, None, None),
            P("rows", "tensor", None),
            P(("replica", "rows"), None),
        ),
        out_specs=P(("replica", "rows"), "tensor"),
        check_vma=False,
    )
```

time: 147 us -> 67.9 us (0.46)
  blocking collectives: 56.3 us -> 0 us
  matrix products: 26.7 us -> 0 us
  Pallas kernels: 0 us -> 20.5 us
  waiting for transfers between devices: 39.7 us -> 23.2 us
  starting transfers between devices: 4.25 us -> 18.8 us
  between operations: 13.5 us -> 0.09 us
  other arithmetic: 4.07 us -> 0.92 us
  local copies, waits for them, and re-layouts: 2.04 us -> 3.6 us
    all_to_all x3 -> x0, blocking collectives: 56.3 us -> none  [the longest x1 22.5 us: shards(): lax.all_to_all(answer, 'rows', split_axis=0, concat_axis=0, tiled=True)]
    reduce_scatter x1 -> x0, waiting for transfers between devices: 28.1 us -> none  [shards(): lax.psum_scatter(term.astype(jnp.float32).astype(jnp.bfloat16), 'tensor',...]
    dot_general x5 -> x0, matrix products: 26.7 us -> none  [the longest x1 10.9 us: shards(): jnp.dot(lax.all_gather(hidden, 'rows', axis=0, tiled=True), down_weight,...]
    ppermute x0 -> x16, waiting for transfers between devices: none -> 23.2 us  [the longest x10 13 us: permute(): return lax.ppermute(v, 'rows', perm)]
    pallas_call x0 -> x7, Pallas kernels: none -> 20.5 us  [the longest x1 10.5 us: near_of(): pl.pallas_call(functools.partial(near_kernel, cap, nt, nw), in_specs=[sme...]
    ppermute x0 -> x16, starting transfers between devices: none -> 18.8 us  [the longest x6 11.3 us: shards(): total = total + lax.ppermute(terms[dz], 'tensor', perm).astype(F32)]
    all_to_all x1 -> x0, waiting for transfers between devices: 10.9 us -> none  [shards(): lax.all_to_all(outgoing, 'rows', split_axis=0, concat_axis=0, tiled=True)]
    all_to_all x1 -> x0, starting transfers between devices: 4.21 us -> none  [shards(): lax.all_to_all(outgoing, 'rows', split_axis=0, concat_axis=0, tiled=True)]
  transfers between devices with their start and end apart: 3 -> 16, of which waited for: 2 -> 8; matrix products, arithmetic and copies ran while one was open for 11% -> 1% of each run, Pallas kernels for 0% -> 20%
where the time goes in v2:
time: 67.9 us; the launch traced here: 67.1 us
  waiting for transfers between devices  23.2 us (34%)
  Pallas kernels  20.5 us (30%)
  starting transfers between devices  18.8 us (28%)
  local copies, waits for them, and re-layouts  3.6 us (5%)
  other arithmetic  0.92 us (1%)
    ppermute x10, waiting for transfers between devices, permute(): return lax.ppermute(v, 'rows', perm)  13 us
    ppermute x6, starting transfers between devices, shards(): total = total + lax.ppermute(terms[dz], 'tensor', perm).astype(F32)  11.3 us
    pallas_call x1, Pallas kernels, near_of(): pl.pallas_call(functools.partial(near_kernel, cap, nt, nw), in_specs=[sme...  10.5 us
    ppermute x6, waiting for transfers between devices, shards(): total = total + lax.ppermute(terms[dz], 'tensor', perm).astype(F32)  10.2 us
    ppermute x10, starting transfers between devices, permute(): return lax.ppermute(v, 'rows', perm)  7.51 us
    pallas_call x2, Pallas kernels, send_of(): pl.pallas_call(functools.partial(send_kernel, cap, start), in_specs=[smem...  4.09 us
    unnamed x7, local copies, waits for them, and re-layouts  3.5 us
    pallas_call x2, Pallas kernels, merge_of(): pl.pallas_call(functools.partial(merge_kernel, cap, groups, nz, bw, start...  2.97 us
  transfers between devices with their start and end apart: 16, of which 8 were waited for; matrix products, arithmetic and copies ran while one was open for 1% of the time, Pallas kernels for 20%

profile of v2, /device:TPU:0, one launch (start us, length us, event | category | flops | bytes accessed | tf_op | source)
XLA Modules:
  0.0 67.1 jit_solution(14174206125537367985)
XLA Ops:
  0.0 0.0 copy-start
  0.0 1.0 %copy-done = bf16[64,4096]{1,0:T(8,128)(2,1)S(1)} copy-done((bf16[64,4096]{1,0:T(8,128)(2,1)S(1)}, bf16[64,4096]{1,0:T(8,128)(2,1)}, u32[]{:S(2)}) %copy-start) | copy-done | bytes 524312
  1.0 0.0 copy-start.1
  1.0 1.0 %copy-done.1 = bf16[64,4096]{1,0:T(8,128)(2,1)S(1)} copy-done((bf16[64,4096]{1,0:T(8,128)(2,1)S(1)}, bf16[64,4096]{1,0:T(8,128)(2,1)}, u32[]{:S(2)}) %copy-start.1) | copy-done | bytes 524312
  2.1 0.0 copy-start.2
  2.1 0.7 copy-done.2
  2.7 0.6 hidden.1.refs_2_.refs_1_
  3.3 0.5 collective-permute-start
  3.9 2.6 %collective-permute-start.2 = (bf16[64,4224]{1,0:T(8,128)(2,1)S(1)}, bf16[64,4224]{1,0:T(8,128)(2,1)S(1)}, u32[]{:S(2)}, u32[]{:S(2)}) collective-permute-start(bf16[64,4224]{1,0:T(8,128)(2,1)S(1)} %hidden.1.refs_2_.refs_1_), channel_id=1, source_target_pairs={{0,8},{4,12},{8,0},{12,4},{1,9},{5,13},{9,1},{13,5},{2,10},{6,14},... | collective-permute-start | bytes 1622024 | tf_op jit(solution)/shard_map/ppermute | solution.py:364
  6.4 0.8 %copy.7 = s32[1,32,6]{2,1,0:T(8,128)S(1)} copy(s32[1,32,6]{1,0,2:T(1,128)} %param.10) | data formatting | bytes 1536 | tf_op args[4]
  7.2 0.1 reshape.7.refs_1_
  7.3 0.1 pad_add_fusion.refs_0_
  7.4 0.0 collective-permute-done.refs_3_
  7.4 10.5 %near.1 = (bf16[24,8192]{1,0:T(8,128)(2,1)S(1)}, bf16[24,8192]{1,0:T(8,128)(2,1)S(1)}, bf16[64,2048]{1,0:T(8,128)(2,1)S(1)}, bf16[64,2048]{1,0:T(8,128)(2,1)S(1)...) custom-call(s32[2]{0:T(128)S(1)} %pad_add_fusion.refs_0_, s32[192]{0:T(256)S(1)} %reshape.7.refs_1_, ...), custom_call_target="tpu_custom_call" | custom-call | flops 2147483648 | bytes 46137344 | tf_op jit(solution)/shard_map/near/pallas_call | solution.py:162
  17.9 1.4 %collective-permute-done.2.refs_2_.refs_1_ = bf16[64,4224]{1,0:T(8,128)(2,1)S(1)} collective-permute-done((bf16[64,4224]{1,0:T(8,128)(2,1)S(1)}, bf16[64,4224]{1,0:T(8,128)(2,1)S(1)}, u32[]{:S(2)}, u32[]{:S(2)}) %collective-permute-start.2) | collective-permute-done | bytes 540704 | tf_op jit(solution)/shard_map/ppermute | solution.py:364
  19.3 0.0 collective-permute-start.4
  19.3 1.9 %collective-permute-done.4.refs_3_.refs_2_ = bf16[64,4224]{1,0:T(8,128)(2,1)S(1)} collective-permute-done((bf16[64,4224]{1,0:T(8,128)(2,1)S(1)}, bf16[64,4224]{1,0:T(8,128)(2,1)S(1)}, u32[]{:S(2)}, u32[]{:S(2)}) %collective-permute-start.4) | collective-permute-done | bytes 540704 | tf_op jit(solution)/shard_map/ppermute | solution.py:364
  21.2 2.3 %far.1 = (bf16[48,2048]{1,0:T(8,128)(2,1)S(1)}, bf16[48,2048]{1,0:T(8,128)(2,1)S(1)}, bf16[48,2048]{1,0:T(8,128)(2,1)S(1)}, bf16[48,2048]{1,0:T(8,128)(2,1)S(1)}) custom-call(s32[2]{0:T(128)S(1)} %pad_add_fusion.refs_0_, s32[192]{0:T(256)S(1)} %reshape.7.refs_1_, bf16[64,4224]{1,0:T(8,128)(2,1)S(1)} %collective-permute-done.2.refs_2_.refs_1_, ...), custom_call_target="tpu_custom_call" | custom-call | flops 1207959552 | bytes 6291456 | tf_op jit(solution)/shard_map/far/pallas_call | solution.py:217
  23.5 0.2 collective-permute-start.5
  23.7 0.4 collective-permute-start.1
  24.1 0.1 collective-permute-start.3
  24.2 0.8 %collective-permute-done.5.refs_5_ = bf16[48,2048]{1,0:T(8,128)(2,1)S(1)} collective-permute-done((bf16[48,2048]{1,0:T(8,128)(2,1)S(1)}, bf16[48,2048]{1,0:T(8,128)(2,1)S(1)}, u32[]{:S(2)}, u32[]{:S(2)}) %collective-permute-start.5) | collective-permute-done | bytes 196640 | tf_op jit(solution)/shard_map/ppermute | solution.py:364
  25.0 2.0 %send.3 = (bf16[112,1024]{1,0:T(8,128)(2,1)S(1)}, bf16[112,1024]{1,0:T(8,128)(2,1)S(1)}) custom-call(s32[2]{0:T(128)S(1)} %pad_add_fusion.refs_0_, bf16[64,4224]{1,0:T(8,128)(2,1)S(1)} %collective-permute-done.2.refs_2_.refs_1_, bf16[64,4224]{1,0:T(8,128)(2,1)S(1)} %collective-permute-done.4.refs_3_.refs_2_, ...), custom_call_target="tpu_custom_call" | custom-call | flops 1073741824 | bytes 8388608 | tf_op jit(solution)/shard_map/send/pallas_call | solution.py:265
  27.1 1.8 %collective-permute-start.11 = (bf16[112,1024]{1,0:T(8,128)(2,1)S(1)}, bf16[112,1024]{1,0:T(8,128)(2,1)S(1)}, u32[]{:S(2)}, u32[]{:S(2)}) collective-permute-start(bf16[112,1024]{1,0:T(8,128)(2,1)S(1)} %get-tuple-element.47), channel_id=1, source_target_pairs={{0,8},{4,12},{8,0},{12,4},{1,9},{5,13},{9,1},{13,5},{2,10},{6,14},... | collective-permute-start | bytes 688136 | tf_op jit(solution)/shard_map/ppermute | solution.py:364
  28.9 0.0 collective-permute-start.12
  28.9 2.0 %send.2 = (bf16[112,1024]{1,0:T(8,128)(2,1)S(1)}, bf16[112,1024]{1,0:T(8,128)(2,1)S(1)}) custom-call(s32[2]{0:T(128)S(1)} %pad_add_fusion.refs_0_, bf16[64,4224]{1,0:T(8,128)(2,1)S(1)} %collective-permute-done.2.refs_2_.refs_1_, bf16[64,4224]{1,0:T(8,128)(2,1)S(1)} %collective-permute-done.4.refs_3_.refs_2_, ...), custom_call_target="tpu_custom_call" | custom-call | flops 1073741824 | bytes 8388608 | tf_op jit(solution)/shard_map/send/pallas_call | solution.py:265
  31.0 1.6 %collective-permute-start.6 = (bf16[112,1024]{1,0:T(8,128)(2,1)S(1)}, bf16[112,1024]{1,0:T(8,128)(2,1)S(1)}, u32[]{:S(2)}, u32[]{:S(2)}) collective-permute-start(bf16[112,1024]{1,0:T(8,128)(2,1)S(1)} %get-tuple-element.41), channel_id=1, source_target_pairs={{0,8},{4,12},{8,0},{12,4},{1,9},{5,13},{9,1},{13,5},{2,10},{6,14},... | collective-permute-start | bytes 688136 | tf_op jit(solution)/shard_map/ppermute | solution.py:364
  32.5 0.0 collective-permute-done.3.refs_5_
  32.5 0.3 collective-permute-start.7
  32.9 0.0 collective-permute-done.1.refs_3_
  32.9 2.7 %collective-permute-done.11.refs_6_ = bf16[112,1024]{1,0:T(8,128)(2,1)S(1)} collective-permute-done((bf16[112,1024]{1,0:T(8,128)(2,1)S(1)}, bf16[112,1024]{1,0:T(8,128)(2,1)S(1)}, u32[]{:S(2)}, u32[]{:S(2)}) %collective-permute-start.11) | collective-permute-done | bytes 229408 | tf_op jit(solution)/shard_map/ppermute | solution.py:364
  35.6 4.2 %collective-permute-done.12.refs_7_ = bf16[112,1024]{1,0:T(8,128)(2,1)S(1)} collective-permute-done((bf16[112,1024]{1,0:T(8,128)(2,1)S(1)}, bf16[112,1024]{1,0:T(8,128)(2,1)S(1)}, u32[]{:S(2)}, u32[]{:S(2)}) %collective-permute-start.12) | collective-permute-done | bytes 229408 | tf_op jit(solution)/shard_map/ppermute | solution.py:364
  39.8 1.5 %merge.3 = (f32[64,1024]{1,0:T(8,128)S(1)}, bf16[64,1024]{1,0:T(8,128)(2,1)S(1)}, bf16[64,1024]{1,0:T(8,128)(2,1)S(1)}, bf16[64,1024]{1,0:T(8,128)(2,1)S(1)}) custom-call(s32[2]{0:T(128)S(1)} %pad_add_fusion.refs_0_, bf16[64,4224]{1,0:T(8,128)(2,1)S(1)} %hidden.1.refs_2_.refs_1_, bf16[24,8192]{1,0:T(8,128)(2,1)S(1)} %get-tuple-element.29.refs_2_, ...), custom_call_target="tpu_custom_call" | custom-call | flops 134217728 | bytes 2097152 | tf_op jit(solution)/shard_map/merge/pallas_call | solution.py:325
  41.3 1.7 %collective-permute-start.13 = (bf16[64,1024]{1,0:T(8,128)(2,1)S(1)}, bf16[64,1024]{1,0:T(8,128)(2,1)S(1)}, u32[]{:S(2)}, u32[]{:S(2)}) collective-permute-start(bf16[64,1024]{1,0:T(8,128)(2,1)S(1)} %get-tuple-element.50), channel_id=1, source_target_pairs={{0,1},{1,2},{2,3},{3,0},{4,5},{5,6},{6,7},{7,4},{8,9},{9,10},{10,1... | collective-permute-start | bytes 393224 | tf_op jit(solution)/shard_map/ppermute | solution.py:397
  43.0 2.6 %collective-permute-start.14 = (bf16[64,1024]{1,0:T(8,128)(2,1)S(1)}, bf16[64,1024]{1,0:T(8,128)(2,1)S(1)}, u32[]{:S(2)}, u32[]{:S(2)}) collective-permute-start(bf16[64,1024]{1,0:T(8,128)(2,1)S(1)} %get-tuple-element.51), channel_id=1, source_target_pairs={{0,2},{1,3},{2,0},{3,1},{4,6},{5,7},{6,4},{7,5},{8,10},{9,11},{10,... | collective-permute-start | bytes 393224 | tf_op jit(solution)/shard_map/ppermute | solution.py:397
  45.6 1.3 %collective-permute-start.15 = (bf16[64,1024]{1,0:T(8,128)(2,1)S(1)}, bf16[64,1024]{1,0:T(8,128)(2,1)S(1)}, u32[]{:S(2)}, u32[]{:S(2)}) collective-permute-start(bf16[64,1024]{1,0:T(8,128)(2,1)S(1)} %get-tuple-element.52), channel_id=1, source_target_pairs={{0,3},{1,0},{2,1},{3,2},{4,7},{5,4},{6,5},{7,6},{8,11},{9,8},{10,9... | collective-permute-start | bytes 393224 | tf_op jit(solution)/shard_map/ppermute | solution.py:397
  46.9 0.0 collective-permute-done.6.refs_6_
  46.9 2.0 %collective-permute-done.7.refs_7_ = bf16[112,1024]{1,0:T(8,128)(2,1)S(1)} collective-permute-done((bf16[112,1024]{1,0:T(8,128)(2,1)S(1)}, bf16[112,1024]{1,0:T(8,128)(2,1)S(1)}, u32[]{:S(2)}, u32[]{:S(2)}) %collective-permute-start.7) | collective-permute-done | bytes 229408 | tf_op jit(solution)/shard_map/ppermute | solution.py:364
  48.8 1.5 %merge.2 = (f32[64,1024]{1,0:T(8,128)S(1)}, bf16[64,1024]{1,0:T(8,128)(2,1)S(1)}, bf16[64,1024]{1,0:T(8,128)(2,1)S(1)}, bf16[64,1024]{1,0:T(8,128)(2,1)S(1)}) custom-call(s32[2]{0:T(128)S(1)} %pad_add_fusion.refs_0_, bf16[64,4224]{1,0:T(8,128)(2,1)S(1)} %hidden.1.refs_2_.refs_1_, bf16[24,8192]{1,0:T(8,128)(2,1)S(1)} %get-tuple-element.29.refs_2_, ...), custom_call_target="tpu_custom_call" | custom-call | flops 134217728 | bytes 2097152 | tf_op jit(solution)/shard_map/merge/pallas_call | solution.py:325
  50.3 1.8 %collective-permute-start.8 = (bf16[64,1024]{1,0:T(8,128)(2,1)S(1)}, bf16[64,1024]{1,0:T(8,128)(2,1)S(1)}, u32[]{:S(2)}, u32[]{:S(2)}) collective-permute-start(bf16[64,1024]{1,0:T(8,128)(2,1)S(1)} %get-tuple-element.44), channel_id=1, source_target_pairs={{0,1},{1,2},{2,3},{3,0},{4,5},{5,6},{6,7},{7,4},{8,9},{9,10},{10,1... | collective-permute-start | bytes 393224 | tf_op jit(solution)/shard_map/ppermute | solution.py:397
  52.1 2.6 %collective-permute-start.9 = (bf16[64,1024]{1,0:T(8,128)(2,1)S(1)}, bf16[64,1024]{1,0:T(8,128)(2,1)S(1)}, u32[]{:S(2)}, u32[]{:S(2)}) collective-permute-start(bf16[64,1024]{1,0:T(8,128)(2,1)S(1)} %get-tuple-element.45), channel_id=1, source_target_pairs={{0,2},{1,3},{2,0},{3,1},{4,6},{5,7},{6,4},{7,5},{8,10},{9,11},{10,... | collective-permute-start | bytes 393224 | tf_op jit(solution)/shard_map/ppermute | solution.py:397
  54.7 0.0 collective-permute-done.13
  54.7 1.4 %collective-permute-start.10 = (bf16[64,1024]{1,0:T(8,128)(2,1)S(1)}, bf16[64,1024]{1,0:T(8,128)(2,1)S(1)}, u32[]{:S(2)}, u32[]{:S(2)}) collective-permute-start(bf16[64,1024]{1,0:T(8,128)(2,1)S(1)} %get-tuple-element.46), channel_id=1, source_target_pairs={{0,3},{1,0},{2,1},{3,2},{4,7},{5,4},{6,5},{7,6},{8,11},{9,8},{10,9... | collective-permute-start | bytes 393224 | tf_op jit(solution)/shard_map/ppermute | solution.py:397
  56.1 0.0 collective-permute-done.14
  56.1 0.0 collective-permute-done.15
  56.1 0.1 add_convert_fusion
  56.2 2.5 %collective-permute-done.8 = bf16[64,1024]{1,0:T(8,128)(2,1)S(1)} collective-permute-done((bf16[64,1024]{1,0:T(8,128)(2,1)S(1)}, bf16[64,1024]{1,0:T(8,128)(2,1)S(1)}, u32[]{:S(2)}, u32[]{:S(2)}) %collective-permute-start.8) | collective-permute-done | bytes 131104 | tf_op jit(solution)/shard_map/ppermute | solution.py:397
  58.7 7.7 %collective-permute-done.9 = bf16[64,1024]{1,0:T(8,128)(2,1)S(1)} collective-permute-done((bf16[64,1024]{1,0:T(8,128)(2,1)S(1)}, bf16[64,1024]{1,0:T(8,128)(2,1)S(1)}, u32[]{:S(2)}, u32[]{:S(2)}) %collective-permute-start.9) | collective-permute-done | bytes 131104 | tf_op jit(solution)/shard_map/ppermute | solution.py:397
  66.3 0.0 collective-permute-done.10
  66.3 0.1 add_convert_fusion.1
  66.4 0.7 %pad_maximum_fusion = bf16[64,2048]{1,0:T(8,128)(2,1)} fusion(bf16[64,1024]{1,0:T(8,128)(2,1)S(1)} %add_convert_fusion, bf16[64,1024]{1,0:T(8,128)(2,1)S(1)} %add_convert_fusion.1), kind=kLoop, calls=%fused_computation | loop fusion | flops 524288 | bytes 524288 | tf_op jit(solution)/shard_map/concatenate | solution.py:399
Async XLA Ops:
  0.0 1.0 %copy-start = (bf16[64,4096]{1,0:T(8,128)(2,1)S(1)}, bf16[64,4096]{1,0:T(8,128)(2,1)}, u32[]{:S(2)}) copy-start(bf16[64,4096]{1,0:T(8,128)(2,1)} %gate_ref.1) | copy-start | bytes 1572868
  1.0 1.0 %copy-start.1 = (bf16[64,4096]{1,0:T(8,128)(2,1)S(1)}, bf16[64,4096]{1,0:T(8,128)(2,1)}, u32[]{:S(2)}) copy-start(bf16[64,4096]{1,0:T(8,128)(2,1)} %up_ref.1) | copy-start | bytes 1572868
  2.1 0.7 copy-start.2
  3.3 4.0 %collective-permute-start = (bf16[64,4224]{1,0:T(8,128)(2,1)S(1)}, bf16[64,4224]{1,0:T(8,128)(2,1)S(1)}, u32[]{:S(2)}, u32[]{:S(2)}) collective-permute-start(bf16[64,4224]{1,0:T(8,128)(2,1)S(1)} %hidden.1.refs_2_.refs_1_), channel_id=1, source_target_pairs={{0,4},{4,0},{8,12},{12,8},{1,5},{5,1},{9,13},{13,9},{2,6},{6,2},{1... | collective-permute-start | bytes 1622024 | tf_op jit(solution)/shard_map/ppermute | solution.py:364
  3.9 15.4 %collective-permute-start.2 = (bf16[64,4224]{1,0:T(8,128)(2,1)S(1)}, bf16[64,4224]{1,0:T(8,128)(2,1)S(1)}, u32[]{:S(2)}, u32[]{:S(2)}) collective-permute-start(bf16[64,4224]{1,0:T(8,128)(2,1)S(1)} %hidden.1.refs_2_.refs_1_), channel_id=1, source_target_pairs={{0,8},{4,12},{8,0},{12,4},{1,9},{5,13},{9,1},{13,5},{2,10},{6,14},... | collective-permute-start | bytes 1622024 | tf_op jit(solution)/shard_map/ppermute | solution.py:364
  19.3 1.9 %collective-permute-start.4 = (bf16[64,4224]{1,0:T(8,128)(2,1)S(1)}, bf16[64,4224]{1,0:T(8,128)(2,1)S(1)}, u32[]{:S(2)}, u32[]{:S(2)}) collective-permute-start(bf16[64,4224]{1,0:T(8,128)(2,1)S(1)} %collective-permute-done.2.refs_2_.refs_1_), channel_id=1, source_target_pairs={{0,4},{4,0},{8,12},{12,8},{1,5},{5,1},{9,13},{13,9},{2,6},{6,2},{1... | collective-permute-start | bytes 1622024 | tf_op jit(solution)/shard_map/ppermute | solution.py:364
  23.5 1.5 %collective-permute-start.5 = (bf16[48,2048]{1,0:T(8,128)(2,1)S(1)}, bf16[48,2048]{1,0:T(8,128)(2,1)S(1)}, u32[]{:S(2)}, u32[]{:S(2)}) collective-permute-start(bf16[48,2048]{1,0:T(8,128)(2,1)S(1)} %get-tuple-element.38), channel_id=1, source_target_pairs={{0,4},{4,0},{8,12},{12,8},{1,5},{5,1},{9,13},{13,9},{2,6},{6,2},{1... | collective-permute-start | bytes 589832 | tf_op jit(solution)/shard_map/ppermute | solution.py:364
  23.7 9.1 %collective-permute-start.1 = (bf16[24,8192]{1,0:T(8,128)(2,1)S(1)}, bf16[24,8192]{1,0:T(8,128)(2,1)S(1)}, u32[]{:S(2)}, u32[]{:S(2)}) collective-permute-start(bf16[24,8192]{1,0:T(8,128)(2,1)S(1)} %get-tuple-element.30), channel_id=1, source_target_pairs={{0,4},{4,0},{8,12},{12,8},{1,5},{5,1},{9,13},{13,9},{2,6},{6,2},{1... | collective-permute-start | bytes 1179656 | tf_op jit(solution)/shard_map/ppermute | solution.py:364
  24.1 8.4 %collective-permute-start.3 = (bf16[64,2048]{1,0:T(8,128)(2,1)S(1)}, bf16[64,2048]{1,0:T(8,128)(2,1)S(1)}, u32[]{:S(2)}, u32[]{:S(2)}) collective-permute-start(bf16[64,2048]{1,0:T(8,128)(2,1)S(1)} %get-tuple-element.33), channel_id=1, source_target_pairs={{0,4},{4,0},{8,12},{12,8},{1,5},{5,1},{9,13},{13,9},{2,6},{6,2},{1... | collective-permute-start | bytes 786440 | tf_op jit(solution)/shard_map/ppermute | solution.py:364
  27.1 8.5 %collective-permute-start.11 = (bf16[112,1024]{1,0:T(8,128)(2,1)S(1)}, bf16[112,1024]{1,0:T(8,128)(2,1)S(1)}, u32[]{:S(2)}, u32[]{:S(2)}) collective-permute-start(bf16[112,1024]{1,0:T(8,128)(2,1)S(1)} %get-tuple-element.47), channel_id=1, source_target_pairs={{0,8},{4,12},{8,0},{12,4},{1,9},{5,13},{9,1},{13,5},{2,10},{6,14},... | collective-permute-start | bytes 688136 | tf_op jit(solution)/shard_map/ppermute | solution.py:364
  28.9 10.9 %collective-permute-start.12 = (bf16[112,1024]{1,0:T(8,128)(2,1)S(1)}, bf16[112,1024]{1,0:T(8,128)(2,1)S(1)}, u32[]{:S(2)}, u32[]{:S(2)}) collective-permute-start(bf16[112,1024]{1,0:T(8,128)(2,1)S(1)} %get-tuple-element.48), channel_id=1, source_target_pairs={{0,12},{4,8},{8,4},{12,0},{1,13},{5,9},{9,5},{13,1},{2,14},{6,10},... | collective-permute-start | bytes 688136 | tf_op jit(solution)/shard_map/ppermute | solution.py:364
  31.0 15.9 %collective-permute-start.6 = (bf16[112,1024]{1,0:T(8,128)(2,1)S(1)}, bf16[112,1024]{1,0:T(8,128)(2,1)S(1)}, u32[]{:S(2)}, u32[]{:S(2)}) collective-permute-start(bf16[112,1024]{1,0:T(8,128)(2,1)S(1)} %get-tuple-element.41), channel_id=1, source_target_pairs={{0,8},{4,12},{8,0},{12,4},{1,9},{5,13},{9,1},{13,5},{2,10},{6,14},... | collective-permute-start | bytes 688136 | tf_op jit(solution)/shard_map/ppermute | solution.py:364
  32.5 16.3 %collective-permute-start.7 = (bf16[112,1024]{1,0:T(8,128)(2,1)S(1)}, bf16[112,1024]{1,0:T(8,128)(2,1)S(1)}, u32[]{:S(2)}, u32[]{:S(2)}) collective-permute-start(bf16[112,1024]{1,0:T(8,128)(2,1)S(1)} %get-tuple-element.42), channel_id=1, source_target_pairs={{0,12},{4,8},{8,4},{12,0},{1,13},{5,9},{9,5},{13,1},{2,14},{6,10},... | collective-permute-start | bytes 688136 | tf_op jit(solution)/shard_map/ppermute | solution.py:364
  41.3 13.4 %collective-permute-start.13 = (bf16[64,1024]{1,0:T(8,128)(2,1)S(1)}, bf16[64,1024]{1,0:T(8,128)(2,1)S(1)}, u32[]{:S(2)}, u32[]{:S(2)}) collective-permute-start(bf16[64,1024]{1,0:T(8,128)(2,1)S(1)} %get-tuple-element.50), channel_id=1, source_target_pairs={{0,1},{1,2},{2,3},{3,0},{4,5},{5,6},{6,7},{7,4},{8,9},{9,10},{10,1... | collective-permute-start | bytes 393224 | tf_op jit(solution)/shard_map/ppermute | solution.py:397
  43.0 13.1 %collective-permute-start.14 = (bf16[64,1024]{1,0:T(8,128)(2,1)S(1)}, bf16[64,1024]{1,0:T(8,128)(2,1)S(1)}, u32[]{:S(2)}, u32[]{:S(2)}) collective-permute-start(bf16[64,1024]{1,0:T(8,128)(2,1)S(1)} %get-tuple-element.51), channel_id=1, source_target_pairs={{0,2},{1,3},{2,0},{3,1},{4,6},{5,7},{6,4},{7,5},{8,10},{9,11},{10,... | collective-permute-start | bytes 393224 | tf_op jit(solution)/shard_map/ppermute | solution.py:397
  45.6 10.5 %collective-permute-start.15 = (bf16[64,1024]{1,0:T(8,128)(2,1)S(1)}, bf16[64,1024]{1,0:T(8,128)(2,1)S(1)}, u32[]{:S(2)}, u32[]{:S(2)}) collective-permute-start(bf16[64,1024]{1,0:T(8,128)(2,1)S(1)} %get-tuple-element.52), channel_id=1, source_target_pairs={{0,3},{1,0},{2,1},{3,2},{4,7},{5,4},{6,5},{7,6},{8,11},{9,8},{10,9... | collective-permute-start | bytes 393224 | tf_op jit(solution)/shard_map/ppermute | solution.py:397
  50.3 8.3 %collective-permute-start.8 = (bf16[64,1024]{1,0:T(8,128)(2,1)S(1)}, bf16[64,1024]{1,0:T(8,128)(2,1)S(1)}, u32[]{:S(2)}, u32[]{:S(2)}) collective-permute-start(bf16[64,1024]{1,0:T(8,128)(2,1)S(1)} %get-tuple-element.44), channel_id=1, source_target_pairs={{0,1},{1,2},{2,3},{3,0},{4,5},{5,6},{6,7},{7,4},{8,9},{9,10},{10,1... | collective-permute-start | bytes 393224 | tf_op jit(solution)/shard_map/ppermute | solution.py:397
  52.1 14.2 %collective-permute-start.9 = (bf16[64,1024]{1,0:T(8,128)(2,1)S(1)}, bf16[64,1024]{1,0:T(8,128)(2,1)S(1)}, u32[]{:S(2)}, u32[]{:S(2)}) collective-permute-start(bf16[64,1024]{1,0:T(8,128)(2,1)S(1)} %get-tuple-element.45), channel_id=1, source_target_pairs={{0,2},{1,3},{2,0},{3,1},{4,6},{5,7},{6,4},{7,5},{8,10},{9,11},{10,... | collective-permute-start | bytes 393224 | tf_op jit(solution)/shard_map/ppermute | solution.py:397
  54.7 11.6 %collective-permute-start.10 = (bf16[64,1024]{1,0:T(8,128)(2,1)S(1)}, bf16[64,1024]{1,0:T(8,128)(2,1)S(1)}, u32[]{:S(2)}, u32[]{:S(2)}) collective-permute-start(bf16[64,1024]{1,0:T(8,128)(2,1)S(1)} %get-tuple-element.46), channel_id=1, source_target_pairs={{0,3},{1,0},{2,1},{3,2},{4,7},{5,4},{6,5},{7,6},{8,11},{9,8},{10,9... | collective-permute-start | bytes 393224 | tf_op jit(solution)/shard_map/ppermute | solution.py:397

commit v3 on v2

--- a/solution.py
+++ b/solution.py
@@ -10,8 +10,8 @@
 BF = jnp.bfloat16
 F32 = jnp.float32
 LANES = 128
-VMEM_LIMIT = 28 * 1024 * 1024
-PARTS = 2
+VMEM_LIMIT = 16 * 1024 * 1024
+PARTS = (6, 5, 5)
 
 
 def params():
@@ -26,42 +26,53 @@
     return pl.BlockSpec(memory_space=pltpu.SMEM)
 
 
-def hidden_kernel(tenant_ref, gate_ref, up_ref, out_ref):
-    width = gate_ref.shape[1]
-    count, total = out_ref.shape
-    step = pl.program_id(0)
-    for start in range(0, width, 512):
-        at = pl.ds(start, min(512, width - start))
-        v = gate_ref[:, at].astype(F32)
-        to = pl.ds(pl.multiple_of(step * width + start, LANES), min(512, width - start))
-        out_ref[:, to] = (v / (1.0 + jnp.exp(-v)) * up_ref[:, at].astype(F32)).astype(BF)
-
-    @pl.when(step == 0)
-    def _():
-        row = jnp.broadcast_to(tenant_ref[...].astype(F32), (count, count))
-        diagonal = lax.broadcasted_iota(jnp.int32, (count, count), 0) == lax.broadcasted_iota(
-            jnp.int32, (count, count), 1
-        )
-        column = jnp.sum(jnp.where(diagonal, row, 0.0), axis=1, keepdims=True)
-        out_ref[:, total - LANES :] = jnp.broadcast_to(column, (count, LANES)).astype(BF)
+def hidden_kernel(chunks, tenant_hbm, gate_hbm, up_hbm, out_ref, tenant_ref, gate_ref, up_ref, sem):
+    count, feats = gate_ref.shape
+    rows = count // chunks
+    copies = [pltpu.make_async_copy(tenant_hbm, tenant_ref, sem.at[2 * chunks])]
+    for i in range(chunks):
+        at = pl.ds(i * rows, rows)
+        copies.append(pltpu.make_async_copy(gate_hbm.at[at], gate_ref.at[at], sem.at[2 * i]))
+        copies.append(pltpu.make_async_copy(up_hbm.at[at], up_ref.at[at], sem.at[2 * i + 1]))
+    for copy in copies:
+        copy.start()
+    copies[0].wait()
+    row = jnp.broadcast_to(tenant_ref[...].astype(F32), (count, count))
+    diagonal = lax.broadcasted_iota(jnp.int32, (count, count), 0) == lax.broadcasted_iota(
+        jnp.int32, (count, count), 1
+    )
+    column = jnp.sum(jnp.where(diagonal, row, 0.0), axis=1, keepdims=True)
+    out_ref[:, feats:] = jnp.broadcast_to(column, (count, LANES)).astype(BF)
+    for i in range(chunks):
+        copies[2 * i + 1].wait()
+        copies[2 * i + 2].wait()
+        at = pl.ds(i * rows, rows)
+        for start in range(0, feats, 512):
+            to = pl.ds(start, min(512, feats - start))
+            v = gate_ref[at, to].astype(F32)
+            out_ref[at, to] = (v / (1.0 + jnp.exp(-v)) * up_ref[at, to].astype(F32)).astype(BF)
 
 
 def hidden_of(gate, up, tenant):
     count, feats = gate.shape
-    steps = 4 if feats % (4 * LANES) == 0 else 1
-    part = pl.BlockSpec((count, feats // steps), lambda i: (0, i))
+    chunks = 4 if count % 64 == 0 else 1
     return pl.pallas_call(
-        hidden_kernel,
-        grid=(steps,),
+        functools.partial(hidden_kernel, chunks),
         out_shape=jax.ShapeDtypeStruct((count, feats + LANES), BF),
-        in_specs=[pl.BlockSpec((1, count), lambda i: (0, 0)), part, part],
-        out_specs=pl.BlockSpec((count, feats + LANES), lambda i: (0, 0)),
+        in_specs=[pl.BlockSpec(memory_space=pltpu.HBM)] * 3,
+        out_specs=whole(),
+        scratch_shapes=[
+            pltpu.VMEM((1, count), jnp.int32),
+            pltpu.VMEM((count, feats), BF),
+            pltpu.VMEM((count, feats), BF),
+            pltpu.SemaphoreType.DMA((2 * chunks + 1,)),
+        ],
         compiler_params=params(),
         name="hidden",
         cost_estimate=pl.CostEstimate(
             flops=6 * count * feats, bytes_accessed=6 * count * feats, transcendentals=count * feats
         ),
-    )(tenant.reshape(1, count), gate, up)
+    )(tenant, gate, up)
 
 
 def slots_of(tenants, tenant):
@@ -106,7 +117,7 @@
         lhs = packed[:, row * LANES : (row + 1) * LANES]
         rhs = jnp.concatenate([tiles_ref[row, j] for j in range(per_row)], axis=1)
         prods = jnp.dot(lhs, rhs, preferred_element_type=F32)
-        at = [cols_ref[row * per_row + j] for j in range(per_row)]
+        at = [cols_ref[j, row] for j in range(per_row)]
         old = [acc[at[j]] for j in range(per_row)]
         for j in range(per_row):
             acc[at[j]] = old[j] + prods[:, j * LANES : (j + 1) * LANES]
@@ -158,7 +169,7 @@
     feats, bw = weight.shape
     nblk = tiles.shape[0]
     nt, nw = (4 if nblk % 4 == 0 else 1), max(1, bw // 512)
-    any_space = pl.BlockSpec(memory_space=pl.ANY)
+    any_space = pl.BlockSpec(memory_space=pltpu.HBM)
     return pl.pallas_call(
         functools.partial(near_kernel, cap, nt, nw),
         in_specs=[smem(), smem(), whole(), whole(), any_space, any_space],
@@ -189,7 +200,10 @@
 
 
 def far_kernel(cap, bw, *refs):
-    meta_ref, cols_ref, a_ref, b_ref, tiles_ref, own_ref, mate_ref, da_ref, db_ref, packed, acc = refs
+    meta_ref, cols_ref, a_ref, b_ref, tiles_ref, own_ref, mate_ref, da_ref, db_ref, both_ref, packed, acc = refs
+    count, feats = a_ref.shape[0], packed.shape[1]
+    both_ref[:count] = a_ref[:, :feats]
+    both_ref[count:] = b_ref[:, :feats]
     me = meta_ref[0]
     chip = me // 2
     ncol = acc.shape[0]
@@ -217,8 +231,9 @@
     return pl.pallas_call(
         functools.partial(far_kernel, cap, bw),
         in_specs=[smem(), smem(), whole(), whole(), whole()],
-        out_specs=[whole()] * 4,
-        out_shape=[jax.ShapeDtypeStruct((rows, bw), BF) for rows in (2 * cap, 2 * cap, away, away)],
+        out_specs=[whole()] * 5,
+        out_shape=[jax.ShapeDtypeStruct((rows, bw), BF) for rows in (2 * cap, 2 * cap, away, away)]
+        + [jax.ShapeDtypeStruct((2 * a.shape[0], feats), BF)],
         scratch_shapes=[
             pltpu.VMEM((2 * cap, feats), BF),
             pltpu.VMEM((width // LANES, 2 * cap, LANES), F32),
@@ -232,21 +247,18 @@
 
 
 def send_kernel(cap, start, *refs):
-    meta_ref, a_ref, b_ref, w_ref, mine_ref, other_ref, da_ref, db_ref, ma_ref, mb_ref, both = refs
-    count = a_ref.shape[0]
-    feats = w_ref.shape[0]
+    meta_ref, ta_ref, tb_ref, both, w_ref, mine_ref, other_ref, da_ref, db_ref, ma_ref, mb_ref = refs
+    count = ta_ref.shape[0]
     sub = ma_ref.shape[1]
-    both[:count] = a_ref[:, :feats]
-    both[count:] = b_ref[:, :feats]
     me = meta_ref[0]
     mate = me + 1 - 2 * (me % 2)
     mine, other = [], []
-    for g, ref in enumerate((a_ref, b_ref)):
+    for g, ref in enumerate((ta_ref, tb_ref)):
         tenants = tenant_lanes(ref)
         mine.append(one_hot(slots_of(tenants, me), g * cap)[:, : 2 * cap])
         other.append(one_hot(slots_of(tenants, mate), (1 - g) * cap)[:, : 2 * cap])
     mine, other = jnp.concatenate(mine, axis=0), jnp.concatenate(other, axis=0)
-    step = min(256, sub)
+    step = 256 if sub % 256 == 0 else LANES
     for n in range(0, sub, step):
         at, to = pl.ds(start + n, step), pl.ds(n, step)
         total = jnp.dot(both[...], w_ref[:, at], preferred_element_type=F32)
@@ -258,22 +270,21 @@
     mb_ref[count:] = db_ref[:, pl.ds(start, sub)]
 
 
-def send_of(cap, start, sub, meta, a, b, weight, mine, other, da, db):
+def send_of(cap, start, sub, meta, a, b, both, weight, mine, other, da, db):
     count = a.shape[0]
     feats = weight.shape[0]
     rows = count + da.shape[0]
     return pl.pallas_call(
         functools.partial(send_kernel, cap, start),
-        in_specs=[smem()] + [whole()] * 7,
+        in_specs=[smem()] + [whole()] * 8,
         out_specs=[whole()] * 2,
         out_shape=[jax.ShapeDtypeStruct((rows, sub), BF)] * 2,
-        scratch_shapes=[pltpu.VMEM((2 * count, feats), BF)],
         compiler_params=params(),
         name="send",
         cost_estimate=pl.CostEstimate(
             flops=4 * count * feats * sub, bytes_accessed=2 * feats * sub, transcendentals=0
         ),
-    )(meta, a, b, weight, mine, other, da, db)
+    )(meta, a, b, both, weight, mine, other, da, db)
 
 
 def merge_kernel(cap, groups, nz, bw, start, *refs):
@@ -308,9 +319,12 @@
                     row = (2 * (e - 1) + half) * cap
                     hot = one_hot(slots, row)[:, : delta.shape[0]]
                     acc[2 * target + half] += jnp.dot(hot, delta, preferred_element_type=F32)
-    if len(outs) == nz:
-        for dz in range(nz):
-            outs[dz][...] = acc[lax.rem(z + dz, nz)].astype(outs[dz].dtype)
+    if len(outs) == 3:
+        near_z = z + 1 - 2 * lax.rem(z, 2)
+        outs[0][:count] = acc[near_z].astype(BF)
+        outs[0][count:] = acc[lax.rem(near_z + 2, nz)].astype(BF)
+        outs[1][...] = acc[z]
+        outs[2][...] = acc[lax.rem(z + 2, nz)]
     else:
         for block in range(groups):
             outs[0][:, block * bw : (block + 1) * bw] = acc[block].astype(BF)
@@ -319,7 +333,7 @@
 def merge_of(cap, groups, nz, direct, bw, start, sub, meta, own, *pieces):
     count = own.shape[0]
     if direct:
-        shapes = [jax.ShapeDtypeStruct((count, sub), F32 if dz == 0 else BF) for dz in range(nz)]
+        shapes = [jax.ShapeDtypeStruct((2 * count, sub), BF)] + [jax.ShapeDtypeStruct((count, sub), F32)] * 2
     else:
         shapes = [jax.ShapeDtypeStruct((count, groups * bw), BF)]
     return pl.pallas_call(
@@ -342,11 +356,11 @@
     bw = down_weight.shape[1]
     width = bw * groups
     cap = -(-(count * 3 // (2 * groups)) // 8) * 8
-    direct = nz == groups and nz <= 4
-    parts = PARTS if direct else 1
-    sub = bw // parts
+    direct = nz == groups == 4 and bw % (LANES * sum(PARTS)) == 0
+    cuts = [bw * p // sum(PARTS) for p in PARTS] if direct else [bw]
+    starts = [sum(cuts[:i]) for i in range(len(cuts))]
     meta = jnp.stack([lax.axis_index("rows"), lax.axis_index("tensor")]).astype(jnp.int32)
-    cols = delta_cols.reshape(-1)
+    cols = delta_cols[0].T
     tiles = delta_tiles[0]
 
     def rows_to(pick):
@@ -363,38 +377,52 @@
     def permute(v, perm):
         return lax.ppermute(v, "rows", perm)
 
-    own = hidden_of(gate_in, up_in, tenant_of_row)
+    stay = lambda v: pltpu.with_memory_space_constraint(v, pltpu.HBM)
+    own = hidden_of(stay(gate_in), stay(up_in), stay(tenant_of_row.reshape(1, count)))
     away = [permute(own, back(dx)) for dx in range(1, pairs)]
     mate = permute(own, swap)
     d_self, d_mate, c_self, c_mate, tiles, weight = near_of(
-        cap, width, meta, cols, own, mate, tiles, down_weight
+        cap, width, meta, cols, own, mate, stay(tiles), stay(down_weight)
     )
-    away, c_self = lax.optimization_barrier((away, c_self))
     d_near = permute(d_mate, swap)
     c_near = permute(c_mate, swap)
-    messages = [[] for _ in range(parts)]
+    away, d_near, c_near = lax.optimization_barrier((away, d_near, c_near))
+    sent = []
+
+    def send(message, perm):
+        if len(sent) >= 2:
+            message, sent[-2] = lax.optimization_barrier((message, sent[-2]))
+        sent.append(permute(message, perm))
+
     for dx in range(1, pairs):
         same = away[dx - 1]
         diag = permute(same, swap)
-        mine, other, d_same, d_diag = far_of(cap, groups, width, meta, cols, same, diag, tiles)
+        mine, other, d_same, d_diag, both = far_of(
+            cap, groups, width, meta, cols, same, diag, tiles
+        )
         other = permute(other, swap)
-        for part in range(parts):
+        for part, (start, sub) in enumerate(zip(starts, cuts)):
             m_same, m_diag = send_of(
-                cap, part * sub, sub, meta, same, diag, weight, mine, other, d_same, d_diag
+                cap, start, sub, meta, same, diag, both, weight, mine, other, d_same, d_diag
             )
-            messages[part] += [permute(m_same, ahead(dx, False)), permute(m_diag, ahead(dx, True))]
+            send(m_same, ahead(dx, False))
+            send(m_diag, ahead(dx, True))
     out = []
-    for part in range(parts):
+    for part, (start, sub) in enumerate(zip(starts, cuts)):
+        got = []
+        for dx in range(1, pairs):
+            first = 2 * ((dx - 1) * len(cuts) + part)
+            got += sent[first : first + 2]
         terms = merge_of(
-            cap, groups, nz, direct, bw, part * sub, sub, meta, own,
-            d_self, d_near, c_self, c_near, *messages[part],
+            cap, groups, nz, direct, bw, start, sub, meta, own,
+            d_self, d_near, c_self, c_near, *got,
         )
         if not direct:
             return lax.psum_scatter(terms[0], "tensor", scatter_dimension=1, tiled=True)
-        total = terms[0]
-        for dz in range(1, nz):
-            perm = [(z, (z + dz) % nz) for z in range(nz)]
-            total = total + lax.ppermute(terms[dz], "tensor", perm).astype(F32)
+        pair = lax.ppermute(terms[0], "tensor", [(z, z ^ 1) for z in range(nz)])
+        passed = (terms[2] + pair[count:].astype(F32)).astype(BF)
+        passed = lax.ppermute(passed, "tensor", [(z, z ^ 2) for z in range(nz)])
+        total = terms[1] + pair[:count].astype(F32) + passed.astype(F32)
         out.append(total.astype(BF))
     return jnp.concatenate(out, axis=1)
 

time: 67.9 us -> 70.3 us (1.035)
  Pallas kernels: 20.5 us -> 25.5 us
  local copies, waits for them, and re-layouts: 3.6 us -> 0.68 us
  waiting for transfers between devices: 23.2 us -> 25.8 us
  starting transfers between devices: 18.8 us -> 17 us
    ppermute x6, starting transfers between devices: 11.3 us -> 7.02 us  [the longest x3 3.82 us: shards(): pair = lax.ppermute(terms[0], 'tensor', [(z, z ^ 1) for z in range(nz)])]
    pallas_call x2 -> x3, Pallas kernels: 4.09 us -> 7.01 us  [send_of(): pl.pallas_call(functools.partial(send_kernel, cap, start), in_specs=[smem...]
    unnamed x7 -> x1, local copies, waits for them, and re-layouts: 3.5 us -> 0.68 us
    ppermute x6, waiting for transfers between devices: 10.2 us -> 12.8 us  [the longest x3 7.45 us: shards(): pair = lax.ppermute(terms[0], 'tensor', [(z, z ^ 1) for z in range(nz)])]
    ppermute x10 -> x12, starting transfers between devices: 7.51 us -> 9.99 us  [permute(): return lax.ppermute(v, 'rows', perm)]
    pallas_call x2 -> x3, Pallas kernels: 2.97 us -> 4.07 us  [merge_of(): pl.pallas_call(functools.partial(merge_kernel, cap, groups, nz, bw, start...]
    pallas_call x1, Pallas kernels: 0.6 us -> 1.48 us  [hidden_of(): pl.pallas_call(functools.partial(hidden_kernel, chunks), out_shape=jax.Sh...]
    ppermute x10 -> x12, waiting for transfers between devices: 13 us -> 13 us  [permute(): return lax.ppermute(v, 'rows', perm)]
  transfers between devices with their start and end apart: 16 -> 18, of which waited for: 8 -> 12; matrix products, arithmetic and copies ran while one was open for 1% -> 1% of each run, Pallas kernels for 20% -> 19%
where the time goes in v3:
time: 70.3 us; the launch traced here: 70.1 us
  waiting for transfers between devices  25.8 us (37%)
  Pallas kernels  25.5 us (36%)
  starting transfers between devices  17 us (24%)
  other arithmetic  0.96 us (1%)
    ppermute x12, waiting for transfers between devices, permute(): return lax.ppermute(v, 'rows', perm)  13 us
    pallas_call x1, Pallas kernels, near_of(): pl.pallas_call(functools.partial(near_kernel, cap, nt, nw), in_specs=[sme...  10.6 us
    ppermute x12, starting transfers between devices, permute(): return lax.ppermute(v, 'rows', perm)  9.99 us
    ppermute x3, waiting for transfers between devices, shards(): pair = lax.ppermute(terms[0], 'tensor', [(z, z ^ 1) for z in range(nz)])  7.45 us
    pallas_call x3, Pallas kernels, send_of(): pl.pallas_call(functools.partial(send_kernel, cap, start), in_specs=[smem...  7.01 us
    ppermute x3, waiting for transfers between devices, shards(): passed = lax.ppermute(passed, 'tensor', [(z, z ^ 2) for z in range(nz)])  5.34 us
    pallas_call x3, Pallas kernels, merge_of(): pl.pallas_call(functools.partial(merge_kernel, cap, groups, nz, bw, start...  4.07 us
    ppermute x3, starting transfers between devices, shards(): pair = lax.ppermute(terms[0], 'tensor', [(z, z ^ 1) for z in range(nz)])  3.82 us
  transfers between devices with their start and end apart: 18, of which 12 were waited for; matrix products, arithmetic and copies ran while one was open for 1% of the time, Pallas kernels for 19%

profile of v3, /device:TPU:0, one launch (start us, length us, event | category | flops | bytes accessed | tf_op | source)
XLA Modules:
  0.0 70.1 jit_solution(8415020796079141441)
XLA Ops:
  0.0 1.5 %hidden.1.refs_2_.refs_1_ = bf16[64,4224]{1,0:T(8,128)(2,1)S(1)} custom-call(s32[1,64]{1,0:T(1,128)} %bitcast.12, bf16[64,4096]{1,0:T(8,128)(2,1)} %gate_hbm.1, bf16[64,4096]{1,0:T(8,128)(2,1)} %up_hbm.1), custom_call_target="tpu_custom_call" | custom-call | flops 1572864 | bytes 1572864 | tf_op jit(solution)/shard_map/hidden/pallas_call | solution.py:59
  1.5 0.5 collective-permute-start
  2.0 2.6 %collective-permute-start.1 = (bf16[64,4224]{1,0:T(8,128)(2,1)S(1)}, bf16[64,4224]{1,0:T(8,128)(2,1)S(1)}, u32[]{:S(2)}, u32[]{:S(2)}) collective-permute-start(bf16[64,4224]{1,0:T(8,128)(2,1)S(1)} %hidden.1.refs_2_.refs_1_), channel_id=1, source_target_pairs={{0,8},{4,12},{8,0},{12,4},{1,9},{5,13},{9,1},{13,5},{2,10},{6,14},... | collective-permute-start | bytes 1622024 | tf_op jit(solution)/shard_map/ppermute | solution.py:378
  4.6 0.7 copy.9
  5.3 0.1 pad_add_fusion.refs_0_
  5.3 0.0 collective-permute-done.refs_3_
  5.3 10.6 %near.1 = (bf16[24,8192]{1,0:T(8,128)(2,1)S(1)}, bf16[24,8192]{1,0:T(8,128)(2,1)S(1)}, bf16[64,2048]{1,0:T(8,128)(2,1)S(1)}, bf16[64,2048]{1,0:T(8,128)(2,1)S(1)...) custom-call(s32[2]{0:T(128)S(1)} %pad_add_fusion.refs_0_, s32[6,32]{1,0:T(8,128)S(1)} %bitcast.9, ...), custom_call_target="tpu_custom_call" | custom-call | flops 2147483648 | bytes 46137344 | tf_op jit(solution)/shard_map/near/pallas_call | solution.py:173
  15.9 0.2 collective-permute-start.2
  16.2 0.3 collective-permute-start.3
  16.5 0.9 %collective-permute-done.1.refs_2_.refs_1_ = bf16[64,4224]{1,0:T(8,128)(2,1)S(1)} collective-permute-done((bf16[64,4224]{1,0:T(8,128)(2,1)S(1)}, bf16[64,4224]{1,0:T(8,128)(2,1)S(1)}, u32[]{:S(2)}, u32[]{:S(2)}) %collective-permute-start.1) | collective-permute-done | bytes 540704 | tf_op jit(solution)/shard_map/ppermute | solution.py:378
  17.4 0.7 collective-permute-done.3.refs_5_
  18.1 0.0 collective-permute-done.2.refs_3_
  18.1 0.2 collective-permute-start.4
  18.3 1.8 %collective-permute-done.4.refs_3_.refs_2_ = bf16[64,4224]{1,0:T(8,128)(2,1)S(1)} collective-permute-done((bf16[64,4224]{1,0:T(8,128)(2,1)S(1)}, bf16[64,4224]{1,0:T(8,128)(2,1)S(1)}, u32[]{:S(2)}, u32[]{:S(2)}) %collective-permute-start.4) | collective-permute-done | bytes 540704 | tf_op jit(solution)/shard_map/ppermute | solution.py:378
  20.0 2.4 %far.1 = (bf16[48,2048]{1,0:T(8,128)(2,1)S(1)}, bf16[48,2048]{1,0:T(8,128)(2,1)S(1)}, bf16[48,2048]{1,0:T(8,128)(2,1)S(1)}, bf16[48,2048]{1,0:T(8,128)(2,1)S(1)}, bf16[128,4096]{1,0:T(8,128)(2,1)S(1)}) custom-call(s32[2]{0:T(128)S(1)} %pad_add_fusion.refs_0_, s32[6,32]{1,0:T(8,128)S(1)} %bitcast.10, ...), custom_call_target="tpu_custom_call" | custom-call | flops 1207959552 | bytes 6291456 | tf_op jit(solution)/shard_map/far/pallas_call | solution.py:231
  22.4 0.2 collective-permute-start.5
  22.6 1.3 %collective-permute-done.5.refs_6_ = bf16[48,2048]{1,0:T(8,128)(2,1)S(1)} collective-permute-done((bf16[48,2048]{1,0:T(8,128)(2,1)S(1)}, bf16[48,2048]{1,0:T(8,128)(2,1)S(1)}, u32[]{:S(2)}, u32[]{:S(2)}) %collective-permute-start.5) | collective-permute-done | bytes 196640 | tf_op jit(solution)/shard_map/ppermute | solution.py:378
  23.9 1.8 %send.4 = (bf16[112,768]{1,0:T(8,128)(2,1)S(1)}, bf16[112,768]{1,0:T(8,128)(2,1)S(1)}) custom-call(s32[2]{0:T(128)S(1)} %pad_add_fusion.refs_0_, bf16[64,4224]{1,0:T(8,128)(2,1)S(1)} %collective-permute-done.1.refs_2_.refs_1_, bf16[64,4224]{1,0:T(8,128)(2,1)S(1)} %collective-permute-done.4.refs_3_.refs_2_, bf16[128,4096]{1,0:T(8,128)(2,1)S(1)} %get-tuple-element.50.refs_3_, ...), custom_call_target="tpu_custom_call" | custom-call | flops 805306368 | bytes 6291456 | tf_op jit(solution)/shard_map/send/pallas_call | solution.py:277
  25.8 1.2 %collective-permute-start.6 = (bf16[112,768]{1,0:T(8,128)(2,1)S(1)}, bf16[112,768]{1,0:T(8,128)(2,1)S(1)}, u32[]{:S(2)}, u32[]{:S(2)}) collective-permute-start(bf16[112,768]{1,0:T(8,128)(2,1)S(1)} %get-tuple-element.57), channel_id=1, source_target_pairs={{0,8},{4,12},{8,0},{12,4},{1,9},{5,13},{9,1},{13,5},{2,10},{6,14},... | collective-permute-start | bytes 516104 | tf_op jit(solution)/shard_map/ppermute | solution.py:378
  26.9 0.4 collective-permute-start.7
  27.3 2.6 %send.3 = (bf16[112,640]{1,0:T(8,128)(2,1)S(1)}, bf16[112,640]{1,0:T(8,128)(2,1)S(1)}) custom-call(s32[2]{0:T(128)S(1)} %pad_add_fusion.refs_0_, bf16[64,4224]{1,0:T(8,128)(2,1)S(1)} %collective-permute-done.1.refs_2_.refs_1_, bf16[64,4224]{1,0:T(8,128)(2,1)S(1)} %collective-permute-done.4.refs_3_.refs_2_, bf16[128,4096]{1,0:T(8,128)(2,1)S(1)} %get-tuple-element.50.refs_3_, ...), custom_call_target="tpu_custom_call" | custom-call | flops 671088640 | bytes 5242880 | tf_op jit(solution)/shard_map/send/pallas_call | solution.py:277
  29.9 3.1 %collective-permute-done.6.refs_6_ = bf16[112,768]{1,0:T(8,128)(2,1)S(1)} collective-permute-done((bf16[112,768]{1,0:T(8,128)(2,1)S(1)}, bf16[112,768]{1,0:T(8,128)(2,1)S(1)}, u32[]{:S(2)}, u32[]{:S(2)}) %collective-permute-start.6) | collective-permute-done | bytes 172064 | tf_op jit(solution)/shard_map/ppermute | solution.py:378
  33.0 2.1 %collective-permute-done.7.refs_7_ = bf16[112,768]{1,0:T(8,128)(2,1)S(1)} collective-permute-done((bf16[112,768]{1,0:T(8,128)(2,1)S(1)}, bf16[112,768]{1,0:T(8,128)(2,1)S(1)}, u32[]{:S(2)}, u32[]{:S(2)}) %collective-permute-start.7) | collective-permute-done | bytes 172064 | tf_op jit(solution)/shard_map/ppermute | solution.py:378
  35.2 1.4 %merge.3 = (bf16[128,768]{1,0:T(8,128)(2,1)S(1)}, f32[64,768]{1,0:T(8,128)S(1)}, f32[64,768]{1,0:T(8,128)S(1)}) custom-call(s32[2]{0:T(128)S(1)} %pad_add_fusion.refs_0_, bf16[64,4224]{1,0:T(8,128)(2,1)S(1)} %hidden.1.refs_2_.refs_1_, bf16[24,8192]{1,0:T(8,128)(2,1)S(1)} %get-tuple-element.42.refs_2_, bf16[24,8192]{1,0:T(8,128)(2,1)S(1)} %collective-permute-done.2.refs_3_, ...), custom_call_target="tpu_custom_call" | custom-call | flops 100663296 | bytes 1572864 | tf_op jit(solution)/shard_map/merge/pallas_call | solution.py:339
  36.6 1.7 %collective-permute-start.8 = (bf16[128,768]{1,0:T(8,128)(2,1)S(1)}, bf16[128,768]{1,0:T(8,128)(2,1)S(1)}, u32[]{:S(2)}, u32[]{:S(2)}) collective-permute-start(bf16[128,768]{1,0:T(8,128)(2,1)S(1)} %get-tuple-element.63), channel_id=1, source_target_pairs={{0,1},{1,0},{2,3},{3,2},{4,5},{5,4},{6,7},{7,6},{8,9},{9,8},{10,11... | collective-permute-start | bytes 589832 | tf_op jit(solution)/shard_map/ppermute | solution.py:422
  38.2 1.0 %collective-permute-start.10 = (bf16[112,640]{1,0:T(8,128)(2,1)S(1)}, bf16[112,640]{1,0:T(8,128)(2,1)S(1)}, u32[]{:S(2)}, u32[]{:S(2)}) collective-permute-start(bf16[112,640]{1,0:T(8,128)(2,1)S(1)} %get-tuple-element.66), channel_id=1, source_target_pairs={{0,8},{4,12},{8,0},{12,4},{1,9},{5,13},{9,1},{13,5},{2,10},{6,14},... | collective-permute-start | bytes 430088 | tf_op jit(solution)/shard_map/ppermute | solution.py:378
  39.3 0.6 collective-permute-start.11
  39.9 2.6 %send.5 = (bf16[112,640]{1,0:T(8,128)(2,1)S(1)}, bf16[112,640]{1,0:T(8,128)(2,1)S(1)}) custom-call(s32[2]{0:T(128)S(1)} %pad_add_fusion.refs_0_, bf16[64,4224]{1,0:T(8,128)(2,1)S(1)} %collective-permute-done.1.refs_2_.refs_1_, bf16[64,4224]{1,0:T(8,128)(2,1)S(1)} %collective-permute-done.4.refs_3_.refs_2_, bf16[128,4096]{1,0:T(8,128)(2,1)S(1)} %get-tuple-element.50.refs_3_, ...), custom_call_target="tpu_custom_call" | custom-call | flops 671088640 | bytes 5242880 | tf_op jit(solution)/shard_map/send/pallas_call | solution.py:277
  42.5 2.3 %collective-permute-done.10.refs_6_ = bf16[112,640]{1,0:T(8,128)(2,1)S(1)} collective-permute-done((bf16[112,640]{1,0:T(8,128)(2,1)S(1)}, bf16[112,640]{1,0:T(8,128)(2,1)S(1)}, u32[]{:S(2)}, u32[]{:S(2)}) %collective-permute-start.10) | collective-permute-done | bytes 143392 | tf_op jit(solution)/shard_map/ppermute | solution.py:378
  44.8 1.0 %collective-permute-start.14 = (bf16[112,640]{1,0:T(8,128)(2,1)S(1)}, bf16[112,640]{1,0:T(8,128)(2,1)S(1)}, u32[]{:S(2)}, u32[]{:S(2)}) collective-permute-start(bf16[112,640]{1,0:T(8,128)(2,1)S(1)} %get-tuple-element.74), channel_id=1, source_target_pairs={{0,8},{4,12},{8,0},{12,4},{1,9},{5,13},{9,1},{13,5},{2,10},{6,14},... | collective-permute-start | bytes 430088 | tf_op jit(solution)/shard_map/ppermute | solution.py:378
  45.9 0.8 %collective-permute-done.11.refs_7_ = bf16[112,640]{1,0:T(8,128)(2,1)S(1)} collective-permute-done((bf16[112,640]{1,0:T(8,128)(2,1)S(1)}, bf16[112,640]{1,0:T(8,128)(2,1)S(1)}, u32[]{:S(2)}, u32[]{:S(2)}) %collective-permute-start.11) | collective-permute-done | bytes 143392 | tf_op jit(solution)/shard_map/ppermute | solution.py:378
  46.7 1.7 %collective-permute-start.15 = (bf16[112,640]{1,0:T(8,128)(2,1)S(1)}, bf16[112,640]{1,0:T(8,128)(2,1)S(1)}, u32[]{:S(2)}, u32[]{:S(2)}) collective-permute-start(bf16[112,640]{1,0:T(8,128)(2,1)S(1)} %get-tuple-element.75), channel_id=1, source_target_pairs={{0,12},{4,8},{8,4},{12,0},{1,13},{5,9},{9,5},{13,1},{2,14},{6,10},... | collective-permute-start | bytes 430088 | tf_op jit(solution)/shard_map/ppermute | solution.py:378
  48.3 0.0 collective-permute-done.8
  48.4 2.7 %collective-permute-start.9 = (bf16[64,768]{1,0:T(8,128)(2,1)S(1)}, bf16[64,768]{1,0:T(8,128)(2,1)S(1)}, u32[]{:S(2)}, u32[]{:S(2)}) collective-permute-start(bf16[64,768]{1,0:T(8,128)(2,1)S(1)} %add_convert_fusion.1), channel_id=1, source_target_pairs={{0,2},{1,3},{2,0},{3,1},{4,6},{5,7},{6,4},{7,5},{8,10},{9,11},{10,... | collective-permute-start | bytes 294920 | tf_op jit(solution)/shard_map/ppermute | solution.py:424
  51.0 1.3 %merge.4 = (bf16[128,640]{1,0:T(8,128)(2,1)S(1)}, f32[64,640]{1,0:T(8,128)S(1)}, f32[64,640]{1,0:T(8,128)S(1)}) custom-call(s32[2]{0:T(128)S(1)} %pad_add_fusion.refs_0_, bf16[64,4224]{1,0:T(8,128)(2,1)S(1)} %hidden.1.refs_2_.refs_1_, bf16[24,8192]{1,0:T(8,128)(2,1)S(1)} %get-tuple-element.42.refs_2_, bf16[24,8192]{1,0:T(8,128)(2,1)S(1)} %collective-permute-done.2.refs_3_, ...), custom_call_target="tpu_custom_call" | custom-call | flops 83886080 | bytes 1310720 | tf_op jit(solution)/shard_map/merge/pallas_call | solution.py:339
  52.4 0.5 collective-permute-start.12
  52.9 0.0 collective-permute-done.14.refs_6_
  52.9 0.0 collective-permute-done.15.refs_7_
  52.9 1.3 %merge.5 = (bf16[128,640]{1,0:T(8,128)(2,1)S(1)}, f32[64,640]{1,0:T(8,128)S(1)}, f32[64,640]{1,0:T(8,128)S(1)}) custom-call(s32[2]{0:T(128)S(1)} %pad_add_fusion.refs_0_, bf16[64,4224]{1,0:T(8,128)(2,1)S(1)} %hidden.1.refs_2_.refs_1_, bf16[24,8192]{1,0:T(8,128)(2,1)S(1)} %get-tuple-element.42.refs_2_, bf16[24,8192]{1,0:T(8,128)(2,1)S(1)} %collective-permute-done.2.refs_3_, ...), custom_call_target="tpu_custom_call" | custom-call | flops 83886080 | bytes 1310720 | tf_op jit(solution)/shard_map/merge/pallas_call | solution.py:339
  54.2 1.7 %collective-permute-start.16 = (bf16[128,640]{1,0:T(8,128)(2,1)S(1)}, bf16[128,640]{1,0:T(8,128)(2,1)S(1)}, u32[]{:S(2)}, u32[]{:S(2)}) collective-permute-start(bf16[128,640]{1,0:T(8,128)(2,1)S(1)} %get-tuple-element.77), channel_id=1, source_target_pairs={{0,1},{1,0},{2,3},{3,2},{4,5},{5,4},{6,7},{7,6},{8,9},{9,8},{10,11... | collective-permute-start | bytes 491528 | tf_op jit(solution)/shard_map/ppermute | solution.py:422
  55.9 0.0 collective-permute-done.9
  55.9 3.6 %collective-permute-done.12 = bf16[128,640]{1,0:T(8,128)(2,1)S(1)} collective-permute-done((bf16[128,640]{1,0:T(8,128)(2,1)S(1)}, bf16[128,640]{1,0:T(8,128)(2,1)S(1)}, u32[]{:S(2)}, u32[]{:S(2)}) %collective-permute-start.12) | collective-permute-done | bytes 163872 | tf_op jit(solution)/shard_map/ppermute | solution.py:422
  59.6 0.1 collective-permute-start.13
  59.7 3.8 %collective-permute-done.16 = bf16[128,640]{1,0:T(8,128)(2,1)S(1)} collective-permute-done((bf16[128,640]{1,0:T(8,128)(2,1)S(1)}, bf16[128,640]{1,0:T(8,128)(2,1)S(1)}, u32[]{:S(2)}, u32[]{:S(2)}) %collective-permute-start.16) | collective-permute-done | bytes 163872 | tf_op jit(solution)/shard_map/ppermute | solution.py:422
  63.5 0.5 collective-permute-start.17
  64.0 3.2 %collective-permute-done.13 = bf16[64,640]{1,0:T(8,128)(2,1)S(1)} collective-permute-done((bf16[64,640]{1,0:T(8,128)(2,1)S(1)}, bf16[64,640]{1,0:T(8,128)(2,1)S(1)}, u32[]{:S(2)}, u32[]{:S(2)}) %collective-permute-start.13) | collective-permute-done | bytes 81952 | tf_op jit(solution)/shard_map/ppermute | solution.py:424
  67.2 2.1 %collective-permute-done.17 = bf16[64,640]{1,0:T(8,128)(2,1)S(1)} collective-permute-done((bf16[64,640]{1,0:T(8,128)(2,1)S(1)}, bf16[64,640]{1,0:T(8,128)(2,1)S(1)}, u32[]{:S(2)}, u32[]{:S(2)}) %collective-permute-start.17) | collective-permute-done | bytes 81952 | tf_op jit(solution)/shard_map/ppermute | solution.py:424
  69.4 0.7 %pad_maximum_fusion = bf16[64,2048]{1,0:T(8,128)(2,1)} fusion(bf16[64,640]{1,0:T(8,128)(2,1)S(1)} %add_convert_fusion.2, bf16[64,640]{1,0:T(8,128)(2,1)S(1)} %add_convert_fusion.4, bf16[64,768]{1,0:T(8,128)(2,1)S(1)} %add_convert_fusion), kind=kLoop, calls=%fused_computation | loop fusion | flops 786432 | bytes 524288 | tf_op jit(solution)/shard_map/concatenate | solution.py:427
  (6 shorter events, 0.2 us)
Async XLA Ops:
  1.5 3.8 %collective-permute-start = (bf16[64,4224]{1,0:T(8,128)(2,1)S(1)}, bf16[64,4224]{1,0:T(8,128)(2,1)S(1)}, u32[]{:S(2)}, u32[]{:S(2)}) collective-permute-start(bf16[64,4224]{1,0:T(8,128)(2,1)S(1)} %hidden.1.refs_2_.refs_1_), channel_id=1, source_target_pairs={{0,4},{4,0},{8,12},{12,8},{1,5},{5,1},{9,13},{13,9},{2,6},{6,2},{1... | collective-permute-start | bytes 1622024 | tf_op jit(solution)/shard_map/ppermute | solution.py:378
  2.0 15.4 %collective-permute-start.1 = (bf16[64,4224]{1,0:T(8,128)(2,1)S(1)}, bf16[64,4224]{1,0:T(8,128)(2,1)S(1)}, u32[]{:S(2)}, u32[]{:S(2)}) collective-permute-start(bf16[64,4224]{1,0:T(8,128)(2,1)S(1)} %hidden.1.refs_2_.refs_1_), channel_id=1, source_target_pairs={{0,8},{4,12},{8,0},{12,4},{1,9},{5,13},{9,1},{13,5},{2,10},{6,14},... | collective-permute-start | bytes 1622024 | tf_op jit(solution)/shard_map/ppermute | solution.py:378
  15.9 2.2 %collective-permute-start.2 = (bf16[24,8192]{1,0:T(8,128)(2,1)S(1)}, bf16[24,8192]{1,0:T(8,128)(2,1)S(1)}, u32[]{:S(2)}, u32[]{:S(2)}) collective-permute-start(bf16[24,8192]{1,0:T(8,128)(2,1)S(1)} %get-tuple-element.43), channel_id=1, source_target_pairs={{0,4},{4,0},{8,12},{12,8},{1,5},{5,1},{9,13},{13,9},{2,6},{6,2},{1... | collective-permute-start | bytes 1179656 | tf_op jit(solution)/shard_map/ppermute | solution.py:378
  16.2 1.9 %collective-permute-start.3 = (bf16[64,2048]{1,0:T(8,128)(2,1)S(1)}, bf16[64,2048]{1,0:T(8,128)(2,1)S(1)}, u32[]{:S(2)}, u32[]{:S(2)}) collective-permute-start(bf16[64,2048]{1,0:T(8,128)(2,1)S(1)} %get-tuple-element.44), channel_id=1, source_target_pairs={{0,4},{4,0},{8,12},{12,8},{1,5},{5,1},{9,13},{13,9},{2,6},{6,2},{1... | collective-permute-start | bytes 786440 | tf_op jit(solution)/shard_map/ppermute | solution.py:378
  18.1 1.9 %collective-permute-start.4 = (bf16[64,4224]{1,0:T(8,128)(2,1)S(1)}, bf16[64,4224]{1,0:T(8,128)(2,1)S(1)}, u32[]{:S(2)}, u32[]{:S(2)}) collective-permute-start(bf16[64,4224]{1,0:T(8,128)(2,1)S(1)} %collective-permute-done.1.refs_2_.refs_1_), channel_id=1, source_target_pairs={{0,4},{4,0},{8,12},{12,8},{1,5},{5,1},{9,13},{13,9},{2,6},{6,2},{1... | collective-permute-start | bytes 1622024 | tf_op jit(solution)/shard_map/ppermute | solution.py:378
  22.4 1.5 %collective-permute-start.5 = (bf16[48,2048]{1,0:T(8,128)(2,1)S(1)}, bf16[48,2048]{1,0:T(8,128)(2,1)S(1)}, u32[]{:S(2)}, u32[]{:S(2)}) collective-permute-start(bf16[48,2048]{1,0:T(8,128)(2,1)S(1)} %get-tuple-element.53), channel_id=1, source_target_pairs={{0,4},{4,0},{8,12},{12,8},{1,5},{5,1},{9,13},{13,9},{2,6},{6,2},{1... | collective-permute-start | bytes 589832 | tf_op jit(solution)/shard_map/ppermute | solution.py:378
  25.8 7.3 %collective-permute-start.6 = (bf16[112,768]{1,0:T(8,128)(2,1)S(1)}, bf16[112,768]{1,0:T(8,128)(2,1)S(1)}, u32[]{:S(2)}, u32[]{:S(2)}) collective-permute-start(bf16[112,768]{1,0:T(8,128)(2,1)S(1)} %get-tuple-element.57), channel_id=1, source_target_pairs={{0,8},{4,12},{8,0},{12,4},{1,9},{5,13},{9,1},{13,5},{2,10},{6,14},... | collective-permute-start | bytes 516104 | tf_op jit(solution)/shard_map/ppermute | solution.py:378
  26.9 8.2 %collective-permute-start.7 = (bf16[112,768]{1,0:T(8,128)(2,1)S(1)}, bf16[112,768]{1,0:T(8,128)(2,1)S(1)}, u32[]{:S(2)}, u32[]{:S(2)}) collective-permute-start(bf16[112,768]{1,0:T(8,128)(2,1)S(1)} %get-tuple-element.60), channel_id=1, source_target_pairs={{0,12},{4,8},{8,4},{12,0},{1,13},{5,9},{9,5},{13,1},{2,14},{6,10},... | collective-permute-start | bytes 516104 | tf_op jit(solution)/shard_map/ppermute | solution.py:378
  36.6 11.8 %collective-permute-start.8 = (bf16[128,768]{1,0:T(8,128)(2,1)S(1)}, bf16[128,768]{1,0:T(8,128)(2,1)S(1)}, u32[]{:S(2)}, u32[]{:S(2)}) collective-permute-start(bf16[128,768]{1,0:T(8,128)(2,1)S(1)} %get-tuple-element.63), channel_id=1, source_target_pairs={{0,1},{1,0},{2,3},{3,2},{4,5},{5,4},{6,7},{7,6},{8,9},{9,8},{10,11... | collective-permute-start | bytes 589832 | tf_op jit(solution)/shard_map/ppermute | solution.py:422
  38.2 6.6 %collective-permute-start.10 = (bf16[112,640]{1,0:T(8,128)(2,1)S(1)}, bf16[112,640]{1,0:T(8,128)(2,1)S(1)}, u32[]{:S(2)}, u32[]{:S(2)}) collective-permute-start(bf16[112,640]{1,0:T(8,128)(2,1)S(1)} %get-tuple-element.66), channel_id=1, source_target_pairs={{0,8},{4,12},{8,0},{12,4},{1,9},{5,13},{9,1},{13,5},{2,10},{6,14},... | collective-permute-start | bytes 430088 | tf_op jit(solution)/shard_map/ppermute | solution.py:378
  39.3 7.4 %collective-permute-start.11 = (bf16[112,640]{1,0:T(8,128)(2,1)S(1)}, bf16[112,640]{1,0:T(8,128)(2,1)S(1)}, u32[]{:S(2)}, u32[]{:S(2)}) collective-permute-start(bf16[112,640]{1,0:T(8,128)(2,1)S(1)} %get-tuple-element.69), channel_id=1, source_target_pairs={{0,12},{4,8},{8,4},{12,0},{1,13},{5,9},{9,5},{13,1},{2,14},{6,10},... | collective-permute-start | bytes 430088 | tf_op jit(solution)/shard_map/ppermute | solution.py:378
  44.8 8.1 %collective-permute-start.14 = (bf16[112,640]{1,0:T(8,128)(2,1)S(1)}, bf16[112,640]{1,0:T(8,128)(2,1)S(1)}, u32[]{:S(2)}, u32[]{:S(2)}) collective-permute-start(bf16[112,640]{1,0:T(8,128)(2,1)S(1)} %get-tuple-element.74), channel_id=1, source_target_pairs={{0,8},{4,12},{8,0},{12,4},{1,9},{5,13},{9,1},{13,5},{2,10},{6,14},... | collective-permute-start | bytes 430088 | tf_op jit(solution)/shard_map/ppermute | solution.py:378
  46.7 6.2 %collective-permute-start.15 = (bf16[112,640]{1,0:T(8,128)(2,1)S(1)}, bf16[112,640]{1,0:T(8,128)(2,1)S(1)}, u32[]{:S(2)}, u32[]{:S(2)}) collective-permute-start(bf16[112,640]{1,0:T(8,128)(2,1)S(1)} %get-tuple-element.75), channel_id=1, source_target_pairs={{0,12},{4,8},{8,4},{12,0},{1,13},{5,9},{9,5},{13,1},{2,14},{6,10},... | collective-permute-start | bytes 430088 | tf_op jit(solution)/shard_map/ppermute | solution.py:378
  48.4 7.5 %collective-permute-start.9 = (bf16[64,768]{1,0:T(8,128)(2,1)S(1)}, bf16[64,768]{1,0:T(8,128)(2,1)S(1)}, u32[]{:S(2)}, u32[]{:S(2)}) collective-permute-start(bf16[64,768]{1,0:T(8,128)(2,1)S(1)} %add_convert_fusion.1), channel_id=1, source_target_pairs={{0,2},{1,3},{2,0},{3,1},{4,6},{5,7},{6,4},{7,5},{8,10},{9,11},{10,... | collective-permute-start | bytes 294920 | tf_op jit(solution)/shard_map/ppermute | solution.py:424
  52.4 7.2 %collective-permute-start.12 = (bf16[128,640]{1,0:T(8,128)(2,1)S(1)}, bf16[128,640]{1,0:T(8,128)(2,1)S(1)}, u32[]{:S(2)}, u32[]{:S(2)}) collective-permute-start(bf16[128,640]{1,0:T(8,128)(2,1)S(1)} %get-tuple-element.72), channel_id=1, source_target_pairs={{0,1},{1,0},{2,3},{3,2},{4,5},{5,4},{6,7},{7,6},{8,9},{9,8},{10,11... | collective-permute-start | bytes 491528 | tf_op jit(solution)/shard_map/ppermute | solution.py:422
  54.2 9.2 %collective-permute-start.16 = (bf16[128,640]{1,0:T(8,128)(2,1)S(1)}, bf16[128,640]{1,0:T(8,128)(2,1)S(1)}, u32[]{:S(2)}, u32[]{:S(2)}) collective-permute-start(bf16[128,640]{1,0:T(8,128)(2,1)S(1)} %get-tuple-element.77), channel_id=1, source_target_pairs={{0,1},{1,0},{2,3},{3,2},{4,5},{5,4},{6,7},{7,6},{8,9},{9,8},{10,11... | collective-permute-start | bytes 491528 | tf_op jit(solution)/shard_map/ppermute | solution.py:422
  59.6 7.6 %collective-permute-start.13 = (bf16[64,640]{1,0:T(8,128)(2,1)S(1)}, bf16[64,640]{1,0:T(8,128)(2,1)S(1)}, u32[]{:S(2)}, u32[]{:S(2)}) collective-permute-start(bf16[64,640]{1,0:T(8,128)(2,1)S(1)} %add_convert_fusion.5), channel_id=1, source_target_pairs={{0,2},{1,3},{2,0},{3,1},{4,6},{5,7},{6,4},{7,5},{8,10},{9,11},{10,... | collective-permute-start | bytes 245768 | tf_op jit(solution)/shard_map/ppermute | solution.py:424
  63.5 5.8 %collective-permute-start.17 = (bf16[64,640]{1,0:T(8,128)(2,1)S(1)}, bf16[64,640]{1,0:T(8,128)(2,1)S(1)}, u32[]{:S(2)}, u32[]{:S(2)}) collective-permute-start(bf16[64,640]{1,0:T(8,128)(2,1)S(1)} %add_convert_fusion.3), channel_id=1, source_target_pairs={{0,2},{1,3},{2,0},{3,1},{4,6},{5,7},{6,4},{7,5},{8,10},{9,11},{10,... | collective-permute-start | bytes 245768 | tf_op jit(solution)/shard_map/ppermute | solution.py:424

commit v4 on v3

--- a/solution.py
+++ b/solution.py
@@ -11,7 +11,9 @@
 F32 = jnp.float32
 LANES = 128
 VMEM_LIMIT = 16 * 1024 * 1024
-PARTS = (6, 5, 5)
+PARTS = (6, 6, 4)
+LAG = 4
+ORDER = (1, 2, 3)
 
 
 def params():
@@ -123,14 +125,28 @@
             acc[at[j]] = old[j] + prods[:, j * LANES : (j + 1) * LANES]
 
 
+def owner_hots(cap, pairs, me, own_ref, hot_ref):
+    tenants = tenant_lanes(own_ref)
+    mate = me + 1 - 2 * (me % 2)
+    hot_ref[0] = one_hot(slots_of(tenants, me), 0) + one_hot(slots_of(tenants, mate), cap)
+    away = 2 * (pairs - 1)
+    for dx in range(1, pairs):
+        source = lax.rem(me // 2 + pairs - dx, pairs)
+        for k, owner in enumerate((2 * source + me % 2, 2 * source + 1 - me % 2)):
+            slots = slots_of(tenants, owner)
+            for block in range(away):
+                hot_ref[1 + (2 * (dx - 1) + k) * away + block] = one_hot(slots, block * cap)
+
+
 def near_kernel(cap, nt, nw, *refs):
     meta_ref, cols_ref, a_ref, b_ref, tiles_ref, w_ref = refs[:6]
-    da_ref, db_ref, ca_ref, cb_ref, tv_ref, wv_ref = refs[6:12]
-    packed, acc, both, tsem, wsem = refs[12:]
+    da_ref, db_ref, ca_ref, cb_ref, tv_ref, wv_ref, hot_ref = refs[6:13]
+    packed, acc, both, tsem, wsem = refs[13:]
     count = a_ref.shape[0]
     feats, bw = w_ref.shape
     nblk = tiles_ref.shape[0]
     tpart, wpart = nblk // nt, bw // nw
+    width_pairs = da_ref.shape[1] // (2 * bw)
     tcopies = [
         pltpu.make_async_copy(
             tiles_ref.at[pl.ds(i * tpart, tpart)], tv_ref.at[pl.ds(i * tpart, tpart)], tsem.at[i]
@@ -149,6 +165,7 @@
     acc[...] = jnp.zeros_like(acc)
     both[:count] = a_ref[:, :feats]
     both[count:] = b_ref[:, :feats]
+    owner_hots(cap, width_pairs, meta_ref[0], a_ref, hot_ref)
     for i in range(nt):
         tcopies[i].wait()
         add_tiles(i * tpart, (i + 1) * tpart, cols_ref, packed, tv_ref, acc)
@@ -169,11 +186,12 @@
     feats, bw = weight.shape
     nblk = tiles.shape[0]
     nt, nw = (4 if nblk % 4 == 0 else 1), max(1, bw // 512)
+    hots = 1 + (width // bw - 2) ** 2
     any_space = pl.BlockSpec(memory_space=pltpu.HBM)
     return pl.pallas_call(
         functools.partial(near_kernel, cap, nt, nw),
         in_specs=[smem(), smem(), whole(), whole(), any_space, any_space],
-        out_specs=[whole()] * 6,
+        out_specs=[whole()] * 7,
         out_shape=[
             jax.ShapeDtypeStruct((cap, width), BF),
             jax.ShapeDtypeStruct((cap, width), BF),
@@ -181,6 +199,7 @@
             jax.ShapeDtypeStruct((count, bw), BF),
             pltpu.VMEM(tiles.shape, BF),
             pltpu.VMEM(weight.shape, BF),
+            jax.ShapeDtypeStruct((hots, count, LANES), BF),
         ],
         scratch_shapes=[
             pltpu.VMEM((2 * cap, feats), BF),
@@ -200,7 +219,7 @@
 
 
 def far_kernel(cap, bw, *refs):
-    meta_ref, cols_ref, a_ref, b_ref, tiles_ref, own_ref, mate_ref, da_ref, db_ref, both_ref, packed, acc = refs
+    meta_ref, cols_ref, a_ref, b_ref, tiles_ref, own_ref, mate_ref, da_ref, db_ref, both_ref, hot_ref, packed, acc = refs
     count, feats = a_ref.shape[0], packed.shape[1]
     both_ref[:count] = a_ref[:, :feats]
     both_ref[count:] = b_ref[:, :feats]
@@ -209,6 +228,12 @@
     ncol = acc.shape[0]
     tiles = bw // LANES
     pairs = ncol // (2 * tiles)
+    mate = me + 1 - 2 * (me % 2)
+    for g, ref in enumerate((a_ref, b_ref)):
+        tenants = tenant_lanes(ref)
+        hot_ref[g * count : (g + 1) * count] = one_hot(slots_of(tenants, me), g * cap) + one_hot(
+            slots_of(tenants, mate), (3 - g) * cap
+        )
     pack_rows(cap, me, a_ref, b_ref, packed)
     acc[...] = jnp.zeros_like(acc)
     add_tiles(0, tiles_ref.shape[0], cols_ref, packed, tiles_ref, acc)
@@ -231,9 +256,9 @@
     return pl.pallas_call(
         functools.partial(far_kernel, cap, bw),
         in_specs=[smem(), smem(), whole(), whole(), whole()],
-        out_specs=[whole()] * 5,
+        out_specs=[whole()] * 6,
         out_shape=[jax.ShapeDtypeStruct((rows, bw), BF) for rows in (2 * cap, 2 * cap, away, away)]
-        + [jax.ShapeDtypeStruct((2 * a.shape[0], feats), BF)],
+        + [jax.ShapeDtypeStruct((2 * a.shape[0], n), BF) for n in (feats, LANES)],
         scratch_shapes=[
             pltpu.VMEM((2 * cap, feats), BF),
             pltpu.VMEM((width // LANES, 2 * cap, LANES), F32),
@@ -247,36 +272,29 @@
 
 
 def send_kernel(cap, start, *refs):
-    meta_ref, ta_ref, tb_ref, both, w_ref, mine_ref, other_ref, da_ref, db_ref, ma_ref, mb_ref = refs
-    count = ta_ref.shape[0]
+    hot_ref, both, w_ref, mine_ref, other_ref, da_ref, db_ref, ma_ref, mb_ref = refs
+    count = both.shape[0] // 2
     sub = ma_ref.shape[1]
-    me = meta_ref[0]
-    mate = me + 1 - 2 * (me % 2)
-    mine, other = [], []
-    for g, ref in enumerate((ta_ref, tb_ref)):
-        tenants = tenant_lanes(ref)
-        mine.append(one_hot(slots_of(tenants, me), g * cap)[:, : 2 * cap])
-        other.append(one_hot(slots_of(tenants, mate), (1 - g) * cap)[:, : 2 * cap])
-    mine, other = jnp.concatenate(mine, axis=0), jnp.concatenate(other, axis=0)
+    hot = hot_ref[:, : 4 * cap]
     step = 256 if sub % 256 == 0 else LANES
     for n in range(0, sub, step):
         at, to = pl.ds(start + n, step), pl.ds(n, step)
         total = jnp.dot(both[...], w_ref[:, at], preferred_element_type=F32)
-        total += jnp.dot(mine, mine_ref[:, at], preferred_element_type=F32)
-        total += jnp.dot(other, other_ref[:, at], preferred_element_type=F32)
+        rows = jnp.concatenate([mine_ref[:, at], other_ref[:, at]], axis=0)
+        total += jnp.dot(hot, rows, preferred_element_type=F32)
         ma_ref[:count, to] = total[:count].astype(BF)
         mb_ref[:count, to] = total[count:].astype(BF)
     ma_ref[count:] = da_ref[:, pl.ds(start, sub)]
     mb_ref[count:] = db_ref[:, pl.ds(start, sub)]
 
 
-def send_of(cap, start, sub, meta, a, b, both, weight, mine, other, da, db):
-    count = a.shape[0]
+def send_of(cap, start, sub, hot, both, weight, mine, other, da, db):
+    count = both.shape[0] // 2
     feats = weight.shape[0]
     rows = count + da.shape[0]
     return pl.pallas_call(
         functools.partial(send_kernel, cap, start),
-        in_specs=[smem()] + [whole()] * 8,
+        in_specs=[whole()] * 7,
         out_specs=[whole()] * 2,
         out_shape=[jax.ShapeDtypeStruct((rows, sub), BF)] * 2,
         compiler_params=params(),
@@ -284,11 +302,11 @@
         cost_estimate=pl.CostEstimate(
             flops=4 * count * feats * sub, bytes_accessed=2 * feats * sub, transcendentals=0
         ),
-    )(meta, a, b, both, weight, mine, other, da, db)
+    )(hot, both, weight, mine, other, da, db)
 
 
 def merge_kernel(cap, groups, nz, bw, start, *refs):
-    meta_ref, own_ref, dself_ref, dmate_ref, cself_ref, cmate_ref = refs[:6]
+    meta_ref, hot_ref, dself_ref, dmate_ref, cself_ref, cmate_ref = refs[:6]
     pairs = groups // 2
     far = refs[6 : 6 + 2 * (pairs - 1)]
     outs, acc = refs[6 + 2 * (pairs - 1) : -1], refs[-1]
@@ -296,44 +314,39 @@
     me, z = meta_ref[0], meta_ref[1]
     mate = me + 1 - 2 * (me % 2)
     chip = me // 2
-    count = own_ref.shape[0]
-    tenants = tenant_lanes(own_ref)
-    near = one_hot(slots_of(tenants, me), 0) + one_hot(slots_of(tenants, mate), cap)
-    near = near[:, : 2 * cap]
+    count = acc.shape[1]
+    near = hot_ref[0][:, : 2 * cap]
     for block in range(groups):
         at = pl.ds(block * bw + start, sub)
         rows = jnp.concatenate([dself_ref[:, at].astype(F32), dmate_ref[:, at].astype(F32)], axis=0)
         acc[block] = jnp.dot(near, rows.astype(BF), preferred_element_type=F32)
     acc[me] += cself_ref[:, start : start + sub].astype(F32)
     acc[mate] += cmate_ref[:, start : start + sub].astype(F32)
+    away = groups - 2
     for dx in range(1, pairs):
         source = lax.rem(chip + pairs - dx, pairs)
         for k, owner in enumerate((2 * source + me % 2, 2 * source + 1 - me % 2)):
             got = far[2 * (dx - 1) + k]
             acc[owner] += got[:count].astype(F32)
-            slots = slots_of(tenants, owner)
             delta = got[count:]
             for e in range(1, pairs):
                 target = lax.rem(source + e, pairs)
                 for half in range(2):
-                    row = (2 * (e - 1) + half) * cap
-                    hot = one_hot(slots, row)[:, : delta.shape[0]]
+                    block = 2 * (e - 1) + half
+                    hot = hot_ref[1 + (2 * (dx - 1) + k) * away + block][:, : delta.shape[0]]
                     acc[2 * target + half] += jnp.dot(hot, delta, preferred_element_type=F32)
-    if len(outs) == 3:
-        near_z = z + 1 - 2 * lax.rem(z, 2)
-        outs[0][:count] = acc[near_z].astype(BF)
-        outs[0][count:] = acc[lax.rem(near_z + 2, nz)].astype(BF)
-        outs[1][...] = acc[z]
-        outs[2][...] = acc[lax.rem(z + 2, nz)]
+    if len(outs) == nz:
+        for dz in range(nz):
+            outs[dz][...] = acc[lax.rem(z + dz, nz)].astype(outs[dz].dtype)
     else:
         for block in range(groups):
             outs[0][:, block * bw : (block + 1) * bw] = acc[block].astype(BF)
 
 
-def merge_of(cap, groups, nz, direct, bw, start, sub, meta, own, *pieces):
-    count = own.shape[0]
+def merge_of(cap, groups, nz, direct, bw, start, sub, meta, hot, *pieces):
+    count = hot.shape[1]
     if direct:
-        shapes = [jax.ShapeDtypeStruct((2 * count, sub), BF)] + [jax.ShapeDtypeStruct((count, sub), F32)] * 2
+        shapes = [jax.ShapeDtypeStruct((count, sub), F32 if dz == 0 else BF) for dz in range(nz)]
     else:
         shapes = [jax.ShapeDtypeStruct((count, groups * bw), BF)]
     return pl.pallas_call(
@@ -347,7 +360,7 @@
         cost_estimate=pl.CostEstimate(
             flops=4 * count * groups * sub * LANES, bytes_accessed=8 * count * groups * sub, transcendentals=0
         ),
-    )(meta, own, *pieces)
+    )(meta, hot, *pieces)
 
 
 def shards(groups, nz, gate_in, up_in, down_weight, delta_tiles, delta_cols, tenant_of_row):
@@ -381,29 +394,29 @@
     own = hidden_of(stay(gate_in), stay(up_in), stay(tenant_of_row.reshape(1, count)))
     away = [permute(own, back(dx)) for dx in range(1, pairs)]
     mate = permute(own, swap)
-    d_self, d_mate, c_self, c_mate, tiles, weight = near_of(
+    d_self, d_mate, c_self, c_mate, tiles, weight, hot = near_of(
         cap, width, meta, cols, own, mate, stay(tiles), stay(down_weight)
     )
     d_near = permute(d_mate, swap)
     c_near = permute(c_mate, swap)
-    away, d_near, c_near = lax.optimization_barrier((away, d_near, c_near))
+    away, c_self = lax.optimization_barrier((away, c_self))
     sent = []
 
     def send(message, perm):
-        if len(sent) >= 2:
-            message, sent[-2] = lax.optimization_barrier((message, sent[-2]))
+        if len(sent) >= LAG:
+            message, sent[-LAG] = lax.optimization_barrier((message, sent[-LAG]))
         sent.append(permute(message, perm))
 
     for dx in range(1, pairs):
         same = away[dx - 1]
         diag = permute(same, swap)
-        mine, other, d_same, d_diag, both = far_of(
+        mine, other, d_same, d_diag, both, far_hot = far_of(
             cap, groups, width, meta, cols, same, diag, tiles
         )
         other = permute(other, swap)
         for part, (start, sub) in enumerate(zip(starts, cuts)):
             m_same, m_diag = send_of(
-                cap, start, sub, meta, same, diag, both, weight, mine, other, d_same, d_diag
+                cap, start, sub, far_hot, both, weight, mine, other, d_same, d_diag
             )
             send(m_same, ahead(dx, False))
             send(m_diag, ahead(dx, True))
@@ -414,15 +427,15 @@
             first = 2 * ((dx - 1) * len(cuts) + part)
             got += sent[first : first + 2]
         terms = merge_of(
-            cap, groups, nz, direct, bw, start, sub, meta, own,
+            cap, groups, nz, direct, bw, start, sub, meta, hot,
             d_self, d_near, c_self, c_near, *got,
         )
         if not direct:
             return lax.psum_scatter(terms[0], "tensor", scatter_dimension=1, tiled=True)
-        pair = lax.ppermute(terms[0], "tensor", [(z, z ^ 1) for z in range(nz)])
-        passed = (terms[2] + pair[count:].astype(F32)).astype(BF)
-        passed = lax.ppermute(passed, "tensor", [(z, z ^ 2) for z in range(nz)])
-        total = terms[1] + pair[:count].astype(F32) + passed.astype(F32)
+        total = terms[0]
+        for dz in ORDER:
+            perm = [(z, (z + dz) % nz) for z in range(nz)]
+            total = total + lax.ppermute(terms[dz], "tensor", perm).astype(F32)
         out.append(total.astype(BF))
     return jnp.concatenate(out, axis=1)
 

time: 70.3 us -> 63.3 us (0.900)
  waiting for transfers between devices: 25.8 us -> 16 us
  starting transfers between devices: 17 us -> 25 us
  Pallas kernels: 25.5 us -> 20.3 us
    ppermute x6 -> x9, starting transfers between devices: 7.02 us -> 16 us  [shards(): total = total + lax.ppermute(terms[dz], 'tensor', perm).astype(F32)]
    ppermute x6 -> x9, waiting for transfers between devices: 12.8 us -> 6.47 us  [shards(): total = total + lax.ppermute(terms[dz], 'tensor', perm).astype(F32)]
    pallas_call x3, Pallas kernels: 7.01 us -> 2.8 us  [send_of(): pl.pallas_call(functools.partial(send_kernel, cap, start), in_specs=[whol...]
    ppermute x12, waiting for transfers between devices: 13 us -> 9.57 us  [permute(): return lax.ppermute(v, 'rows', perm)]
    pallas_call x3, Pallas kernels: 4.07 us -> 2.84 us  [merge_of(): pl.pallas_call(functools.partial(merge_kernel, cap, groups, nz, bw, start...]
    ppermute x12, starting transfers between devices: 9.99 us -> 8.97 us  [permute(): return lax.ppermute(v, 'rows', perm)]
  transfers between devices with their start and end apart: 18 -> 21, of which waited for: 12 -> 8; matrix products, arithmetic and copies ran while one was open for 1% -> 1% of each run, Pallas kernels for 19% -> 22%
where the time goes in v4:
time: 63.3 us; the launch traced here: 63.1 us
  starting transfers between devices  25 us (39%)
  Pallas kernels  20.3 us (32%)
  waiting for transfers between devices  16 us (25%)
  other arithmetic  0.93 us (1%)
  local copies, waits for them, and re-layouts  0.68 us (1%)
    ppermute x9, starting transfers between devices, shards(): total = total + lax.ppermute(terms[dz], 'tensor', perm).astype(F32)  16 us
    pallas_call x1, Pallas kernels, near_of(): pl.pallas_call(functools.partial(near_kernel, cap, nt, nw), in_specs=[sme...  10.7 us
    ppermute x12, waiting for transfers between devices, permute(): return lax.ppermute(v, 'rows', perm)  9.57 us
    ppermute x12, starting transfers between devices, permute(): return lax.ppermute(v, 'rows', perm)  8.97 us
    ppermute x9, waiting for transfers between devices, shards(): total = total + lax.ppermute(terms[dz], 'tensor', perm).astype(F32)  6.47 us
    pallas_call x3, Pallas kernels, merge_of(): pl.pallas_call(functools.partial(merge_kernel, cap, groups, nz, bw, start...  2.84 us
    pallas_call x3, Pallas kernels, send_of(): pl.pallas_call(functools.partial(send_kernel, cap, start), in_specs=[whol...  2.8 us
    pallas_call x1, Pallas kernels, far_of(): pl.pallas_call(functools.partial(far_kernel, cap, bw), in_specs=[smem(),...  2.45 us
  transfers between devices with their start and end apart: 21, of which 8 were waited for; matrix products, arithmetic and copies ran while one was open for 1% of the time, Pallas kernels for 22%

profile of v4, /device:TPU:0, one launch (start us, length us, event | category | flops | bytes accessed | tf_op | source)
XLA Modules:
  0.0 63.1 jit_solution(14972648747991450615)
XLA Ops:
  0.0 1.5 %hidden.1.refs_2_ = bf16[64,4224]{1,0:T(8,128)(2,1)S(1)} custom-call(s32[1,64]{1,0:T(1,128)} %bitcast.12, bf16[64,4096]{1,0:T(8,128)(2,1)} %gate_hbm.1, bf16[64,4096]{1,0:T(8,128)(2,1)} %up_hbm.1), custom_call_target="tpu_custom_call" | custom-call | flops 1572864 | bytes 1572864 | tf_op jit(solution)/shard_map/hidden/pallas_call | solution.py:61
  1.5 0.5 collective-permute-start
  2.0 2.6 %collective-permute-start.2 = (bf16[64,4224]{1,0:T(8,128)(2,1)S(1)}, bf16[64,4224]{1,0:T(8,128)(2,1)S(1)}, u32[]{:S(2)}, u32[]{:S(2)}) collective-permute-start(bf16[64,4224]{1,0:T(8,128)(2,1)S(1)} %hidden.1.refs_2_), channel_id=1, source_target_pairs={{0,8},{4,12},{8,0},{12,4},{1,9},{5,13},{9,1},{13,5},{2,10},{6,14},... | collective-permute-start | bytes 1622024 | tf_op jit(solution)/shard_map/ppermute | solution.py:391
  4.6 0.7 %copy.9 = s32[1,32,6]{1,2,0:T(8,128)S(1)} copy(s32[1,32,6]{1,0,2:T(1,128)} %param.10) | data formatting | bytes 1536
  5.3 0.1 pad_add_fusion.refs_0_
  5.3 0.0 collective-permute-done.refs_3_
  5.3 10.7 %near.1 = (bf16[24,8192]{1,0:T(8,128)(2,1)S(1)}, bf16[24,8192]{1,0:T(8,128)(2,1)S(1)}, bf16[64,2048]{1,0:T(8,128)(2,1)S(1)}, bf16[64,2048]{1,0:T(8,128)(2,1)S(1)...) custom-call(s32[2]{0:T(128)S(1)} %pad_add_fusion.refs_0_, ...), custom_call_target="tpu_custom_call" | custom-call | flops 2147483648 | bytes 46137344 | tf_op jit(solution)/shard_map/near/pallas_call | solution.py:191
  16.1 1.3 %collective-permute-done.2.refs_2_ = bf16[64,4224]{1,0:T(8,128)(2,1)S(1)} collective-permute-done((bf16[64,4224]{1,0:T(8,128)(2,1)S(1)}, bf16[64,4224]{1,0:T(8,128)(2,1)S(1)}, u32[]{:S(2)}, u32[]{:S(2)}) %collective-permute-start.2) | collective-permute-done | bytes 540704 | tf_op jit(solution)/shard_map/ppermute | solution.py:391
  17.4 0.0 collective-permute-start.4
  17.4 1.9 %collective-permute-done.4.refs_3_ = bf16[64,4224]{1,0:T(8,128)(2,1)S(1)} collective-permute-done((bf16[64,4224]{1,0:T(8,128)(2,1)S(1)}, bf16[64,4224]{1,0:T(8,128)(2,1)S(1)}, u32[]{:S(2)}, u32[]{:S(2)}) %collective-permute-start.4) | collective-permute-done | bytes 540704 | tf_op jit(solution)/shard_map/ppermute | solution.py:391
  19.4 2.5 %far.1 = (bf16[48,2048]{1,0:T(8,128)(2,1)S(1)}, bf16[48,2048]{1,0:T(8,128)(2,1)S(1)}, bf16[48,2048]{1,0:T(8,128)(2,1)S(1)}, bf16[48,2048]{1,0:T(8,128)(2,1)S(1)}...) custom-call(s32[2]{0:T(128)S(1)} %pad_add_fusion.refs_0_, s32[6,32]{1,0:T(8,128)S(1)} %bitcast.10, ...), custom_call_target="tpu_custom_call" | custom-call | flops 1207959552 | bytes 6291456 | tf_op jit(solution)/shard_map/far/pallas_call | solution.py:256
  21.8 0.2 collective-permute-start.5
  22.0 0.4 collective-permute-start.1
  22.4 0.1 collective-permute-start.3
  22.5 0.8 %collective-permute-done.5.refs_4_ = bf16[48,2048]{1,0:T(8,128)(2,1)S(1)} collective-permute-done((bf16[48,2048]{1,0:T(8,128)(2,1)S(1)}, bf16[48,2048]{1,0:T(8,128)(2,1)S(1)}, u32[]{:S(2)}, u32[]{:S(2)}) %collective-permute-start.5) | collective-permute-done | bytes 196640 | tf_op jit(solution)/shard_map/ppermute | solution.py:391
  23.3 1.0 %send.5 = (bf16[112,768]{1,0:T(8,128)(2,1)S(1)}, bf16[112,768]{1,0:T(8,128)(2,1)S(1)}) custom-call(bf16[128,128]{1,0:T(8,128)(2,1)S(1)} %get-tuple-element.50.refs_0_, bf16[128,4096]{1,0:T(8,128)(2,1)S(1)} %get-tuple-element.51.refs_1_, bf16[4096,2048]{1,0:T(8,128)(2,1)S(1)} %get-tuple-element.52.refs_2_, bf16[48,2048]{1,0:T(8,128)(2,1)S(1)} %get-tuple-element.53.refs_3_, ...), custom_call_target="tpu_custom_call" | custom-call | flops 805306368 | bytes 6291456 | tf_op jit(solution)/shard_map/send/pallas_call | solution.py:295
  24.4 1.8 %collective-permute-start.11 = (bf16[112,768]{1,0:T(8,128)(2,1)S(1)}, bf16[112,768]{1,0:T(8,128)(2,1)S(1)}, u32[]{:S(2)}, u32[]{:S(2)}) collective-permute-start(bf16[112,768]{1,0:T(8,128)(2,1)S(1)} %get-tuple-element.67), channel_id=1, source_target_pairs={{0,8},{4,12},{8,0},{12,4},{1,9},{5,13},{9,1},{13,5},{2,10},{6,14},... | collective-permute-start | bytes 516104 | tf_op jit(solution)/shard_map/ppermute | solution.py:391
  26.2 0.0 collective-permute-start.12
  26.2 1.0 %send.4 = (bf16[112,768]{1,0:T(8,128)(2,1)S(1)}, bf16[112,768]{1,0:T(8,128)(2,1)S(1)}) custom-call(bf16[128,128]{1,0:T(8,128)(2,1)S(1)} %get-tuple-element.50.refs_0_, bf16[128,4096]{1,0:T(8,128)(2,1)S(1)} %get-tuple-element.51.refs_1_, bf16[4096,2048]{1,0:T(8,128)(2,1)S(1)} %get-tuple-element.52.refs_2_, bf16[48,2048]{1,0:T(8,128)(2,1)S(1)} %get-tuple-element.53.refs_3_, ...), custom_call_target="tpu_custom_call" | custom-call | flops 805306368 | bytes 6291456 | tf_op jit(solution)/shard_map/send/pallas_call | solution.py:295
  27.2 1.6 %collective-permute-start.6 = (bf16[112,768]{1,0:T(8,128)(2,1)S(1)}, bf16[112,768]{1,0:T(8,128)(2,1)S(1)}, u32[]{:S(2)}, u32[]{:S(2)}) collective-permute-start(bf16[112,768]{1,0:T(8,128)(2,1)S(1)} %get-tuple-element.58), channel_id=1, source_target_pairs={{0,8},{4,12},{8,0},{12,4},{1,9},{5,13},{9,1},{13,5},{2,10},{6,14},... | collective-permute-start | bytes 516104 | tf_op jit(solution)/shard_map/ppermute | solution.py:391
  28.8 0.0 collective-permute-done.3.refs_5_
  28.8 0.3 collective-permute-start.7
  29.1 0.0 collective-permute-done.1.refs_3_
  29.1 2.5 %collective-permute-done.11.refs_6_ = bf16[112,768]{1,0:T(8,128)(2,1)S(1)} collective-permute-done((bf16[112,768]{1,0:T(8,128)(2,1)S(1)}, bf16[112,768]{1,0:T(8,128)(2,1)S(1)}, u32[]{:S(2)}, u32[]{:S(2)}) %collective-permute-start.11) | collective-permute-done | bytes 172064 | tf_op jit(solution)/shard_map/ppermute | solution.py:391
  31.7 3.0 %collective-permute-done.12.refs_7_ = bf16[112,768]{1,0:T(8,128)(2,1)S(1)} collective-permute-done((bf16[112,768]{1,0:T(8,128)(2,1)S(1)}, bf16[112,768]{1,0:T(8,128)(2,1)S(1)}, u32[]{:S(2)}, u32[]{:S(2)}) %collective-permute-start.12) | collective-permute-done | bytes 172064 | tf_op jit(solution)/shard_map/ppermute | solution.py:391
  34.6 1.0 %merge.4 = (f32[64,768]{1,0:T(8,128)S(1)}, bf16[64,768]{1,0:T(8,128)(2,1)S(1)}, bf16[64,768]{1,0:T(8,128)(2,1)S(1)}, bf16[64,768]{1,0:T(8,128)(2,1)S(1)}) custom-call(s32[2]{0:T(128)S(1)} %pad_add_fusion.refs_0_, bf16[5,64,128]{2,1,0:T(8,128)(2,1)S(1)} %get-tuple-element.42.refs_1_, bf16[24,8192]{1,0:T(8,128)(2,1)S(1)} %get-tuple-element.43.refs_2_, ...), custom_call_target="tpu_custom_call" | custom-call | flops 100663296 | bytes 1572864 | tf_op jit(solution)/shard_map/merge/pallas_call | solution.py:352
  35.6 1.7 %collective-permute-start.13 = (bf16[64,768]{1,0:T(8,128)(2,1)S(1)}, bf16[64,768]{1,0:T(8,128)(2,1)S(1)}, u32[]{:S(2)}, u32[]{:S(2)}) collective-permute-start(bf16[64,768]{1,0:T(8,128)(2,1)S(1)} %get-tuple-element.70), channel_id=1, source_target_pairs={{0,1},{1,2},{2,3},{3,0},{4,5},{5,6},{6,7},{7,4},{8,9},{9,10},{10,1... | collective-permute-start | bytes 294920 | tf_op jit(solution)/shard_map/ppermute | solution.py:438
  37.3 2.5 %collective-permute-start.14 = (bf16[64,768]{1,0:T(8,128)(2,1)S(1)}, bf16[64,768]{1,0:T(8,128)(2,1)S(1)}, u32[]{:S(2)}, u32[]{:S(2)}) collective-permute-start(bf16[64,768]{1,0:T(8,128)(2,1)S(1)} %get-tuple-element.71), channel_id=1, source_target_pairs={{0,2},{1,3},{2,0},{3,1},{4,6},{5,7},{6,4},{7,5},{8,10},{9,11},{10,... | collective-permute-start | bytes 294920 | tf_op jit(solution)/shard_map/ppermute | solution.py:438
  39.8 1.4 %collective-permute-start.15 = (bf16[64,768]{1,0:T(8,128)(2,1)S(1)}, bf16[64,768]{1,0:T(8,128)(2,1)S(1)}, u32[]{:S(2)}, u32[]{:S(2)}) collective-permute-start(bf16[64,768]{1,0:T(8,128)(2,1)S(1)} %get-tuple-element.72), channel_id=1, source_target_pairs={{0,3},{1,0},{2,1},{3,2},{4,7},{5,4},{6,5},{7,6},{8,11},{9,8},{10,9... | collective-permute-start | bytes 294920 | tf_op jit(solution)/shard_map/ppermute | solution.py:438
  41.2 0.7 %send.3 = (bf16[112,512]{1,0:T(8,128)(2,1)S(1)}, bf16[112,512]{1,0:T(8,128)(2,1)S(1)}) custom-call(bf16[128,128]{1,0:T(8,128)(2,1)S(1)} %get-tuple-element.50.refs_0_, bf16[128,4096]{1,0:T(8,128)(2,1)S(1)} %get-tuple-element.51.refs_1_, bf16[4096,2048]{1,0:T(8,128)(2,1)S(1)} %get-tuple-element.52.refs_2_, bf16[48,2048]{1,0:T(8,128)(2,1)S(1)} %get-tuple-element.53.refs_3_, ...), custom_call_target="tpu_custom_call" | custom-call | flops 536870912 | bytes 4194304 | tf_op jit(solution)/shard_map/send/pallas_call | solution.py:295
  41.9 0.0 collective-permute-done.6.refs_6_
  41.9 0.9 %collective-permute-start.16 = (bf16[112,512]{1,0:T(8,128)(2,1)S(1)}, bf16[112,512]{1,0:T(8,128)(2,1)S(1)}, u32[]{:S(2)}, u32[]{:S(2)}) collective-permute-start(bf16[112,512]{1,0:T(8,128)(2,1)S(1)} %get-tuple-element.73), channel_id=1, source_target_pairs={{0,8},{4,12},{8,0},{12,4},{1,9},{5,13},{9,1},{13,5},{2,10},{6,14},... | collective-permute-start | bytes 344072 | tf_op jit(solution)/shard_map/ppermute | solution.py:391
  42.9 0.0 collective-permute-done.7.refs_7_
  42.9 0.5 collective-permute-start.17
  43.4 1.0 %merge.3 = (f32[64,768]{1,0:T(8,128)S(1)}, bf16[64,768]{1,0:T(8,128)(2,1)S(1)}, bf16[64,768]{1,0:T(8,128)(2,1)S(1)}, bf16[64,768]{1,0:T(8,128)(2,1)S(1)}) custom-call(s32[2]{0:T(128)S(1)} %pad_add_fusion.refs_0_, bf16[5,64,128]{2,1,0:T(8,128)(2,1)S(1)} %get-tuple-element.42.refs_1_, bf16[24,8192]{1,0:T(8,128)(2,1)S(1)} %get-tuple-element.43.refs_2_, ...), custom_call_target="tpu_custom_call" | custom-call | flops 100663296 | bytes 1572864 | tf_op jit(solution)/shard_map/merge/pallas_call | solution.py:352
  44.4 0.0 collective-permute-done.13
  44.4 1.6 %collective-permute-start.8 = (bf16[64,768]{1,0:T(8,128)(2,1)S(1)}, bf16[64,768]{1,0:T(8,128)(2,1)S(1)}, u32[]{:S(2)}, u32[]{:S(2)}) collective-permute-start(bf16[64,768]{1,0:T(8,128)(2,1)S(1)} %get-tuple-element.64), channel_id=1, source_target_pairs={{0,1},{1,2},{2,3},{3,0},{4,5},{5,6},{6,7},{7,4},{8,9},{9,10},{10,1... | collective-permute-start | bytes 294920 | tf_op jit(solution)/shard_map/ppermute | solution.py:438
  46.0 1.3 %collective-permute-done.14 = bf16[64,768]{1,0:T(8,128)(2,1)S(1)} collective-permute-done((bf16[64,768]{1,0:T(8,128)(2,1)S(1)}, bf16[64,768]{1,0:T(8,128)(2,1)S(1)}, u32[]{:S(2)}, u32[]{:S(2)}) %collective-permute-start.14) | collective-permute-done | bytes 98336 | tf_op jit(solution)/shard_map/ppermute | solution.py:438
  47.3 2.0 %collective-permute-start.9 = (bf16[64,768]{1,0:T(8,128)(2,1)S(1)}, bf16[64,768]{1,0:T(8,128)(2,1)S(1)}, u32[]{:S(2)}, u32[]{:S(2)}) collective-permute-start(bf16[64,768]{1,0:T(8,128)(2,1)S(1)} %get-tuple-element.65), channel_id=1, source_target_pairs={{0,2},{1,3},{2,0},{3,1},{4,6},{5,7},{6,4},{7,5},{8,10},{9,11},{10,... | collective-permute-start | bytes 294920 | tf_op jit(solution)/shard_map/ppermute | solution.py:438
  49.3 0.0 collective-permute-done.15
  49.3 1.9 %collective-permute-start.10 = (bf16[64,768]{1,0:T(8,128)(2,1)S(1)}, bf16[64,768]{1,0:T(8,128)(2,1)S(1)}, u32[]{:S(2)}, u32[]{:S(2)}) collective-permute-start(bf16[64,768]{1,0:T(8,128)(2,1)S(1)} %get-tuple-element.66), channel_id=1, source_target_pairs={{0,3},{1,0},{2,1},{3,2},{4,7},{5,4},{6,5},{7,6},{8,11},{9,8},{10,9... | collective-permute-start | bytes 294920 | tf_op jit(solution)/shard_map/ppermute | solution.py:438
  51.2 0.0 collective-permute-done.16.refs_6_
  51.2 0.0 collective-permute-done.17.refs_7_
  51.2 0.9 %merge.5 = (f32[64,512]{1,0:T(8,128)S(1)}, bf16[64,512]{1,0:T(8,128)(2,1)S(1)}, bf16[64,512]{1,0:T(8,128)(2,1)S(1)}, bf16[64,512]{1,0:T(8,128)(2,1)S(1)}) custom-call(s32[2]{0:T(128)S(1)} %pad_add_fusion.refs_0_, bf16[5,64,128]{2,1,0:T(8,128)(2,1)S(1)} %get-tuple-element.42.refs_1_, bf16[24,8192]{1,0:T(8,128)(2,1)S(1)} %get-tuple-element.43.refs_2_, ...), custom_call_target="tpu_custom_call" | custom-call | flops 67108864 | bytes 1048576 | tf_op jit(solution)/shard_map/merge/pallas_call | solution.py:352
  52.1 0.6 collective-permute-start.18
  52.7 1.5 %collective-permute-start.19 = (bf16[64,512]{1,0:T(8,128)(2,1)S(1)}, bf16[64,512]{1,0:T(8,128)(2,1)S(1)}, u32[]{:S(2)}, u32[]{:S(2)}) collective-permute-start(bf16[64,512]{1,0:T(8,128)(2,1)S(1)} %get-tuple-element.77), channel_id=1, source_target_pairs={{0,2},{1,3},{2,0},{3,1},{4,6},{5,7},{6,4},{7,5},{8,10},{9,11},{10,... | collective-permute-start | bytes 196616 | tf_op jit(solution)/shard_map/ppermute | solution.py:438
  54.2 0.0 collective-permute-done.8
  54.3 2.8 %collective-permute-start.20 = (bf16[64,512]{1,0:T(8,128)(2,1)S(1)}, bf16[64,512]{1,0:T(8,128)(2,1)S(1)}, u32[]{:S(2)}, u32[]{:S(2)}) collective-permute-start(bf16[64,512]{1,0:T(8,128)(2,1)S(1)} %get-tuple-element.78), channel_id=1, source_target_pairs={{0,3},{1,0},{2,1},{3,2},{4,7},{5,4},{6,5},{7,6},{8,11},{9,8},{10,9... | collective-permute-start | bytes 196616 | tf_op jit(solution)/shard_map/ppermute | solution.py:438
  57.1 0.0 collective-permute-done.9
  57.1 0.0 collective-permute-done.10
  57.1 0.1 add_convert_fusion.1
  57.2 1.8 %collective-permute-done.18 = bf16[64,512]{1,0:T(8,128)(2,1)S(1)} collective-permute-done((bf16[64,512]{1,0:T(8,128)(2,1)S(1)}, bf16[64,512]{1,0:T(8,128)(2,1)S(1)}, u32[]{:S(2)}, u32[]{:S(2)}) %collective-permute-start.18) | collective-permute-done | bytes 65568 | tf_op jit(solution)/shard_map/ppermute | solution.py:438
  58.9 3.4 %collective-permute-done.19 = bf16[64,512]{1,0:T(8,128)(2,1)S(1)} collective-permute-done((bf16[64,512]{1,0:T(8,128)(2,1)S(1)}, bf16[64,512]{1,0:T(8,128)(2,1)S(1)}, u32[]{:S(2)}, u32[]{:S(2)}) %collective-permute-start.19) | collective-permute-done | bytes 65568 | tf_op jit(solution)/shard_map/ppermute | solution.py:438
  62.3 0.0 collective-permute-done.20
  62.4 0.7 %pad_maximum_fusion = bf16[64,2048]{1,0:T(8,128)(2,1)} fusion(bf16[64,512]{1,0:T(8,128)(2,1)S(1)} %add_convert_fusion.2, bf16[64,768]{1,0:T(8,128)(2,1)S(1)} %add_convert_fusion, bf16[64,768]{1,0:T(8,128)(2,1)S(1)} %add_convert_fusion.1), kind=kLoop, calls=%fused_computation | loop fusion | flops 786432 | bytes 524288 | tf_op jit(solution)/shard_map/concatenate | solution.py:440
  (2 shorter events, 0.1 us)
Async XLA Ops:
  1.5 3.8 %collective-permute-start = (bf16[64,4224]{1,0:T(8,128)(2,1)S(1)}, bf16[64,4224]{1,0:T(8,128)(2,1)S(1)}, u32[]{:S(2)}, u32[]{:S(2)}) collective-permute-start(bf16[64,4224]{1,0:T(8,128)(2,1)S(1)} %hidden.1.refs_2_), channel_id=1, source_target_pairs={{0,4},{4,0},{8,12},{12,8},{1,5},{5,1},{9,13},{13,9},{2,6},{6,2},{1... | collective-permute-start | bytes 1622024 | tf_op jit(solution)/shard_map/ppermute | solution.py:391
  2.0 15.4 %collective-permute-start.2 = (bf16[64,4224]{1,0:T(8,128)(2,1)S(1)}, bf16[64,4224]{1,0:T(8,128)(2,1)S(1)}, u32[]{:S(2)}, u32[]{:S(2)}) collective-permute-start(bf16[64,4224]{1,0:T(8,128)(2,1)S(1)} %hidden.1.refs_2_), channel_id=1, source_target_pairs={{0,8},{4,12},{8,0},{12,4},{1,9},{5,13},{9,1},{13,5},{2,10},{6,14},... | collective-permute-start | bytes 1622024 | tf_op jit(solution)/shard_map/ppermute | solution.py:391
  17.4 1.9 %collective-permute-start.4 = (bf16[64,4224]{1,0:T(8,128)(2,1)S(1)}, bf16[64,4224]{1,0:T(8,128)(2,1)S(1)}, u32[]{:S(2)}, u32[]{:S(2)}) collective-permute-start(bf16[64,4224]{1,0:T(8,128)(2,1)S(1)} %collective-permute-done.2.refs_2_), channel_id=1, source_target_pairs={{0,4},{4,0},{8,12},{12,8},{1,5},{5,1},{9,13},{13,9},{2,6},{6,2},{1... | collective-permute-start | bytes 1622024 | tf_op jit(solution)/shard_map/ppermute | solution.py:391
  21.8 1.5 %collective-permute-start.5 = (bf16[48,2048]{1,0:T(8,128)(2,1)S(1)}, bf16[48,2048]{1,0:T(8,128)(2,1)S(1)}, u32[]{:S(2)}, u32[]{:S(2)}) collective-permute-start(bf16[48,2048]{1,0:T(8,128)(2,1)S(1)} %get-tuple-element.54), channel_id=1, source_target_pairs={{0,4},{4,0},{8,12},{12,8},{1,5},{5,1},{9,13},{13,9},{2,6},{6,2},{1... | collective-permute-start | bytes 589832 | tf_op jit(solution)/shard_map/ppermute | solution.py:391
  22.0 7.1 %collective-permute-start.1 = (bf16[24,8192]{1,0:T(8,128)(2,1)S(1)}, bf16[24,8192]{1,0:T(8,128)(2,1)S(1)}, u32[]{:S(2)}, u32[]{:S(2)}) collective-permute-start(bf16[24,8192]{1,0:T(8,128)(2,1)S(1)} %get-tuple-element.44), channel_id=1, source_target_pairs={{0,4},{4,0},{8,12},{12,8},{1,5},{5,1},{9,13},{13,9},{2,6},{6,2},{1... | collective-permute-start | bytes 1179656 | tf_op jit(solution)/shard_map/ppermute | solution.py:391
  22.4 6.4 %collective-permute-start.3 = (bf16[64,2048]{1,0:T(8,128)(2,1)S(1)}, bf16[64,2048]{1,0:T(8,128)(2,1)S(1)}, u32[]{:S(2)}, u32[]{:S(2)}) collective-permute-start(bf16[64,2048]{1,0:T(8,128)(2,1)S(1)} %get-tuple-element.47), channel_id=1, source_target_pairs={{0,4},{4,0},{8,12},{12,8},{1,5},{5,1},{9,13},{13,9},{2,6},{6,2},{1... | collective-permute-start | bytes 786440 | tf_op jit(solution)/shard_map/ppermute | solution.py:391
  24.4 7.3 %collective-permute-start.11 = (bf16[112,768]{1,0:T(8,128)(2,1)S(1)}, bf16[112,768]{1,0:T(8,128)(2,1)S(1)}, u32[]{:S(2)}, u32[]{:S(2)}) collective-permute-start(bf16[112,768]{1,0:T(8,128)(2,1)S(1)} %get-tuple-element.67), channel_id=1, source_target_pairs={{0,8},{4,12},{8,0},{12,4},{1,9},{5,13},{9,1},{13,5},{2,10},{6,14},... | collective-permute-start | bytes 516104 | tf_op jit(solution)/shard_map/ppermute | solution.py:391
  26.2 8.4 %collective-permute-start.12 = (bf16[112,768]{1,0:T(8,128)(2,1)S(1)}, bf16[112,768]{1,0:T(8,128)(2,1)S(1)}, u32[]{:S(2)}, u32[]{:S(2)}) collective-permute-start(bf16[112,768]{1,0:T(8,128)(2,1)S(1)} %get-tuple-element.68), channel_id=1, source_target_pairs={{0,12},{4,8},{8,4},{12,0},{1,13},{5,9},{9,5},{13,1},{2,14},{6,10},... | collective-permute-start | bytes 516104 | tf_op jit(solution)/shard_map/ppermute | solution.py:391
  27.2 14.7 %collective-permute-start.6 = (bf16[112,768]{1,0:T(8,128)(2,1)S(1)}, bf16[112,768]{1,0:T(8,128)(2,1)S(1)}, u32[]{:S(2)}, u32[]{:S(2)}) collective-permute-start(bf16[112,768]{1,0:T(8,128)(2,1)S(1)} %get-tuple-element.58), channel_id=1, source_target_pairs={{0,8},{4,12},{8,0},{12,4},{1,9},{5,13},{9,1},{13,5},{2,10},{6,14},... | collective-permute-start | bytes 516104 | tf_op jit(solution)/shard_map/ppermute | solution.py:391
  28.8 14.1 %collective-permute-start.7 = (bf16[112,768]{1,0:T(8,128)(2,1)S(1)}, bf16[112,768]{1,0:T(8,128)(2,1)S(1)}, u32[]{:S(2)}, u32[]{:S(2)}) collective-permute-start(bf16[112,768]{1,0:T(8,128)(2,1)S(1)} %get-tuple-element.61), channel_id=1, source_target_pairs={{0,12},{4,8},{8,4},{12,0},{1,13},{5,9},{9,5},{13,1},{2,14},{6,10},... | collective-permute-start | bytes 516104 | tf_op jit(solution)/shard_map/ppermute | solution.py:391
  35.6 8.8 %collective-permute-start.13 = (bf16[64,768]{1,0:T(8,128)(2,1)S(1)}, bf16[64,768]{1,0:T(8,128)(2,1)S(1)}, u32[]{:S(2)}, u32[]{:S(2)}) collective-permute-start(bf16[64,768]{1,0:T(8,128)(2,1)S(1)} %get-tuple-element.70), channel_id=1, source_target_pairs={{0,1},{1,2},{2,3},{3,0},{4,5},{5,6},{6,7},{7,4},{8,9},{9,10},{10,1... | collective-permute-start | bytes 294920 | tf_op jit(solution)/shard_map/ppermute | solution.py:438
  37.3 10.0 %collective-permute-start.14 = (bf16[64,768]{1,0:T(8,128)(2,1)S(1)}, bf16[64,768]{1,0:T(8,128)(2,1)S(1)}, u32[]{:S(2)}, u32[]{:S(2)}) collective-permute-start(bf16[64,768]{1,0:T(8,128)(2,1)S(1)} %get-tuple-element.71), channel_id=1, source_target_pairs={{0,2},{1,3},{2,0},{3,1},{4,6},{5,7},{6,4},{7,5},{8,10},{9,11},{10,... | collective-permute-start | bytes 294920 | tf_op jit(solution)/shard_map/ppermute | solution.py:438
  39.8 9.5 %collective-permute-start.15 = (bf16[64,768]{1,0:T(8,128)(2,1)S(1)}, bf16[64,768]{1,0:T(8,128)(2,1)S(1)}, u32[]{:S(2)}, u32[]{:S(2)}) collective-permute-start(bf16[64,768]{1,0:T(8,128)(2,1)S(1)} %get-tuple-element.72), channel_id=1, source_target_pairs={{0,3},{1,0},{2,1},{3,2},{4,7},{5,4},{6,5},{7,6},{8,11},{9,8},{10,9... | collective-permute-start | bytes 294920 | tf_op jit(solution)/shard_map/ppermute | solution.py:438
  41.9 9.3 %collective-permute-start.16 = (bf16[112,512]{1,0:T(8,128)(2,1)S(1)}, bf16[112,512]{1,0:T(8,128)(2,1)S(1)}, u32[]{:S(2)}, u32[]{:S(2)}) collective-permute-start(bf16[112,512]{1,0:T(8,128)(2,1)S(1)} %get-tuple-element.73), channel_id=1, source_target_pairs={{0,8},{4,12},{8,0},{12,4},{1,9},{5,13},{9,1},{13,5},{2,10},{6,14},... | collective-permute-start | bytes 344072 | tf_op jit(solution)/shard_map/ppermute | solution.py:391
  42.9 8.3 %collective-permute-start.17 = (bf16[112,512]{1,0:T(8,128)(2,1)S(1)}, bf16[112,512]{1,0:T(8,128)(2,1)S(1)}, u32[]{:S(2)}, u32[]{:S(2)}) collective-permute-start(bf16[112,512]{1,0:T(8,128)(2,1)S(1)} %get-tuple-element.74), channel_id=1, source_target_pairs={{0,12},{4,8},{8,4},{12,0},{1,13},{5,9},{9,5},{13,1},{2,14},{6,10},... | collective-permute-start | bytes 344072 | tf_op jit(solution)/shard_map/ppermute | solution.py:391
  44.4 9.9 %collective-permute-start.8 = (bf16[64,768]{1,0:T(8,128)(2,1)S(1)}, bf16[64,768]{1,0:T(8,128)(2,1)S(1)}, u32[]{:S(2)}, u32[]{:S(2)}) collective-permute-start(bf16[64,768]{1,0:T(8,128)(2,1)S(1)} %get-tuple-element.64), channel_id=1, source_target_pairs={{0,1},{1,2},{2,3},{3,0},{4,5},{5,6},{6,7},{7,4},{8,9},{9,10},{10,1... | collective-permute-start | bytes 294920 | tf_op jit(solution)/shard_map/ppermute | solution.py:438
  47.3 9.8 %collective-permute-start.9 = (bf16[64,768]{1,0:T(8,128)(2,1)S(1)}, bf16[64,768]{1,0:T(8,128)(2,1)S(1)}, u32[]{:S(2)}, u32[]{:S(2)}) collective-permute-start(bf16[64,768]{1,0:T(8,128)(2,1)S(1)} %get-tuple-element.65), channel_id=1, source_target_pairs={{0,2},{1,3},{2,0},{3,1},{4,6},{5,7},{6,4},{7,5},{8,10},{9,11},{10,... | collective-permute-start | bytes 294920 | tf_op jit(solution)/shard_map/ppermute | solution.py:438
  49.3 7.8 %collective-permute-start.10 = (bf16[64,768]{1,0:T(8,128)(2,1)S(1)}, bf16[64,768]{1,0:T(8,128)(2,1)S(1)}, u32[]{:S(2)}, u32[]{:S(2)}) collective-permute-start(bf16[64,768]{1,0:T(8,128)(2,1)S(1)} %get-tuple-element.66), channel_id=1, source_target_pairs={{0,3},{1,0},{2,1},{3,2},{4,7},{5,4},{6,5},{7,6},{8,11},{9,8},{10,9... | collective-permute-start | bytes 294920 | tf_op jit(solution)/shard_map/ppermute | solution.py:438
  52.1 6.8 %collective-permute-start.18 = (bf16[64,512]{1,0:T(8,128)(2,1)S(1)}, bf16[64,512]{1,0:T(8,128)(2,1)S(1)}, u32[]{:S(2)}, u32[]{:S(2)}) collective-permute-start(bf16[64,512]{1,0:T(8,128)(2,1)S(1)} %get-tuple-element.76), channel_id=1, source_target_pairs={{0,1},{1,2},{2,3},{3,0},{4,5},{5,6},{6,7},{7,4},{8,9},{9,10},{10,1... | collective-permute-start | bytes 196616 | tf_op jit(solution)/shard_map/ppermute | solution.py:438
  52.7 9.6 %collective-permute-start.19 = (bf16[64,512]{1,0:T(8,128)(2,1)S(1)}, bf16[64,512]{1,0:T(8,128)(2,1)S(1)}, u32[]{:S(2)}, u32[]{:S(2)}) collective-permute-start(bf16[64,512]{1,0:T(8,128)(2,1)S(1)} %get-tuple-element.77), channel_id=1, source_target_pairs={{0,2},{1,3},{2,0},{3,1},{4,6},{5,7},{6,4},{7,5},{8,10},{9,11},{10,... | collective-permute-start | bytes 196616 | tf_op jit(solution)/shard_map/ppermute | solution.py:438
  54.3 8.1 %collective-permute-start.20 = (bf16[64,512]{1,0:T(8,128)(2,1)S(1)}, bf16[64,512]{1,0:T(8,128)(2,1)S(1)}, u32[]{:S(2)}, u32[]{:S(2)}) collective-permute-start(bf16[64,512]{1,0:T(8,128)(2,1)S(1)} %get-tuple-element.78), channel_id=1, source_target_pairs={{0,3},{1,0},{2,1},{3,2},{4,7},{5,4},{6,5},{7,6},{8,11},{9,8},{10,9... | collective-permute-start | bytes 196616 | tf_op jit(solution)/shard_map/ppermute | solution.py:438

commit v5 on v4

--- a/solution.py
+++ b/solution.py
@@ -11,7 +11,7 @@
 F32 = jnp.float32
 LANES = 128
 VMEM_LIMIT = 16 * 1024 * 1024
-PARTS = (6, 6, 4)
+PARTS = (2, 3, 3)
 LAG = 4
 ORDER = (1, 2, 3)
 
@@ -271,6 +271,28 @@
     )(meta, cols, a, b, tiles)
 
 
+def first_kernel(both, w_ref, out_ref):
+    sub = out_ref.shape[1]
+    step = 256 if sub % 256 == 0 else LANES
+    for n in range(0, sub, step):
+        at = pl.ds(n, step)
+        out_ref[:, at] = jnp.dot(both[...], w_ref[:, at], preferred_element_type=F32)
+
+
+def first_of(sub, both, weight):
+    return pl.pallas_call(
+        first_kernel,
+        in_specs=[whole()] * 2,
+        out_specs=whole(),
+        out_shape=jax.ShapeDtypeStruct((both.shape[0], sub), F32),
+        compiler_params=params(),
+        name="first",
+        cost_estimate=pl.CostEstimate(
+            flops=2 * both.size * sub, bytes_accessed=2 * weight.shape[0] * sub, transcendentals=0
+        ),
+    )(both, weight)
+
+
 def send_kernel(cap, start, *refs):
     hot_ref, both, w_ref, mine_ref, other_ref, da_ref, db_ref, ma_ref, mb_ref = refs
     count = both.shape[0] // 2
@@ -279,7 +301,10 @@
     step = 256 if sub % 256 == 0 else LANES
     for n in range(0, sub, step):
         at, to = pl.ds(start + n, step), pl.ds(n, step)
-        total = jnp.dot(both[...], w_ref[:, at], preferred_element_type=F32)
+        if start == 0:
+            total = w_ref[:, to]
+        else:
+            total = jnp.dot(both[...], w_ref[:, at], preferred_element_type=F32)
         rows = jnp.concatenate([mine_ref[:, at], other_ref[:, at]], axis=0)
         total += jnp.dot(hot, rows, preferred_element_type=F32)
         ma_ref[:count, to] = total[:count].astype(BF)
@@ -290,7 +315,7 @@
 
 def send_of(cap, start, sub, hot, both, weight, mine, other, da, db):
     count = both.shape[0] // 2
-    feats = weight.shape[0]
+    feats = both.shape[1]
     rows = count + da.shape[0]
     return pl.pallas_call(
         functools.partial(send_kernel, cap, start),
@@ -415,8 +440,9 @@
         )
         other = permute(other, swap)
         for part, (start, sub) in enumerate(zip(starts, cuts)):
+            from_w = weight if start else first_of(sub, both, weight)
             m_same, m_diag = send_of(
-                cap, start, sub, far_hot, both, weight, mine, other, d_same, d_diag
+                cap, start, sub, far_hot, both, from_w, mine, other, d_same, d_diag
             )
             send(m_same, ahead(dx, False))
             send(m_diag, ahead(dx, True))

time: 63.3 us -> 61.7 us (0.975)
  waiting for transfers between devices: 16 us -> 14.5 us
    ppermute x12, waiting for transfers between devices: 9.57 us -> 6.79 us  [permute(): return lax.ppermute(v, 'rows', perm)]
    ppermute x9, waiting for transfers between devices: 6.47 us -> 7.71 us  [shards(): total = total + lax.ppermute(terms[dz], 'tensor', perm).astype(F32)]
    ppermute x9, starting transfers between devices: 16 us -> 15 us  [shards(): total = total + lax.ppermute(terms[dz], 'tensor', perm).astype(F32)]
    ppermute x12, starting transfers between devices: 8.97 us -> 9.79 us  [permute(): return lax.ppermute(v, 'rows', perm)]
    pallas_call x0 -> x1, Pallas kernels: none -> 0.72 us  [first_of(): pl.pallas_call(first_kernel, in_specs=[whole()] * 2, out_specs=whole(), o...]
  transfers between devices with their start and end apart: 21 -> 21, of which waited for: 8 -> 8; matrix products, arithmetic and copies ran while one was open for 1% -> 1% of each run, Pallas kernels for 22% -> 23%
where the time goes in v5:
time: 61.7 us; the launch traced here: 61.5 us
  starting transfers between devices  24.8 us (40%)
  Pallas kernels  20.5 us (33%)
  waiting for transfers between devices  14.5 us (24%)
  other arithmetic  0.94 us (2%)
  local copies, waits for them, and re-layouts  0.68 us (1%)
    ppermute x9, starting transfers between devices, shards(): total = total + lax.ppermute(terms[dz], 'tensor', perm).astype(F32)  15 us
    pallas_call x1, Pallas kernels, near_of(): pl.pallas_call(functools.partial(near_kernel, cap, nt, nw), in_specs=[sme...  10.7 us
    ppermute x12, starting transfers between devices, permute(): return lax.ppermute(v, 'rows', perm)  9.79 us
    ppermute x9, waiting for transfers between devices, shards(): total = total + lax.ppermute(terms[dz], 'tensor', perm).astype(F32)  7.71 us
    ppermute x12, waiting for transfers between devices, permute(): return lax.ppermute(v, 'rows', perm)  6.79 us
    pallas_call x3, Pallas kernels, merge_of(): pl.pallas_call(functools.partial(merge_kernel, cap, groups, nz, bw, start...  2.84 us
    pallas_call x1, Pallas kernels, far_of(): pl.pallas_call(functools.partial(far_kernel, cap, bw), in_specs=[smem(),...  2.45 us
    pallas_call x3, Pallas kernels, send_of(): pl.pallas_call(functools.partial(send_kernel, cap, start), in_specs=[whol...  2.25 us
  transfers between devices with their start and end apart: 21, of which 8 were waited for; matrix products, arithmetic and copies ran while one was open for 1% of the time, Pallas kernels for 23%

profile of v5, /device:TPU:0, one launch (start us, length us, event | category | flops | bytes accessed | tf_op | source)
XLA Modules:
  0.0 61.5 jit_solution(14556655278578866123)
XLA Ops:
  0.0 1.5 %hidden.1.refs_2_ = bf16[64,4224]{1,0:T(8,128)(2,1)S(1)} custom-call(s32[1,64]{1,0:T(1,128)} %bitcast.12, bf16[64,4096]{1,0:T(8,128)(2,1)} %gate_hbm.1, bf16[64,4096]{1,0:T(8,128)(2,1)} %up_hbm.1), custom_call_target="tpu_custom_call" | custom-call | flops 1572864 | bytes 1572864 | tf_op jit(solution)/shard_map/hidden/pallas_call | solution.py:61
  1.5 0.5 collective-permute-start
  2.0 2.6 %collective-permute-start.2 = (bf16[64,4224]{1,0:T(8,128)(2,1)S(1)}, bf16[64,4224]{1,0:T(8,128)(2,1)S(1)}, u32[]{:S(2)}, u32[]{:S(2)}) collective-permute-start(bf16[64,4224]{1,0:T(8,128)(2,1)S(1)} %hidden.1.refs_2_), channel_id=1, source_target_pairs={{0,8},{4,12},{8,0},{12,4},{1,9},{5,13},{9,1},{13,5},{2,10},{6,14},... | collective-permute-start | bytes 1622024 | tf_op jit(solution)/shard_map/ppermute | solution.py:416
  4.6 0.7 %copy.9 = s32[1,32,6]{1,2,0:T(8,128)S(1)} copy(s32[1,32,6]{1,0,2:T(1,128)} %param.10) | data formatting | bytes 1536
  5.3 0.1 pad_add_fusion.refs_0_
  5.3 0.0 collective-permute-done.refs_3_
  5.3 10.7 %near.1 = (bf16[24,8192]{1,0:T(8,128)(2,1)S(1)}, bf16[24,8192]{1,0:T(8,128)(2,1)S(1)}, bf16[64,2048]{1,0:T(8,128)(2,1)S(1)}, bf16[64,2048]{1,0:T(8,128)(2,1)S(1)...) custom-call(s32[2]{0:T(128)S(1)} %pad_add_fusion.refs_0_, ...), custom_call_target="tpu_custom_call" | custom-call | flops 2147483648 | bytes 46137344 | tf_op jit(solution)/shard_map/near/pallas_call | solution.py:191
  16.1 1.3 %collective-permute-done.2.refs_2_ = bf16[64,4224]{1,0:T(8,128)(2,1)S(1)} collective-permute-done((bf16[64,4224]{1,0:T(8,128)(2,1)S(1)}, bf16[64,4224]{1,0:T(8,128)(2,1)S(1)}, u32[]{:S(2)}, u32[]{:S(2)}) %collective-permute-start.2) | collective-permute-done | bytes 540704 | tf_op jit(solution)/shard_map/ppermute | solution.py:416
  17.4 0.0 collective-permute-start.4
  17.4 1.9 %collective-permute-done.4.refs_3_ = bf16[64,4224]{1,0:T(8,128)(2,1)S(1)} collective-permute-done((bf16[64,4224]{1,0:T(8,128)(2,1)S(1)}, bf16[64,4224]{1,0:T(8,128)(2,1)S(1)}, u32[]{:S(2)}, u32[]{:S(2)}) %collective-permute-start.4) | collective-permute-done | bytes 540704 | tf_op jit(solution)/shard_map/ppermute | solution.py:416
  19.4 2.5 %far.1 = (bf16[48,2048]{1,0:T(8,128)(2,1)S(1)}, bf16[48,2048]{1,0:T(8,128)(2,1)S(1)}, bf16[48,2048]{1,0:T(8,128)(2,1)S(1)}, bf16[48,2048]{1,0:T(8,128)(2,1)S(1)}...) custom-call(s32[2]{0:T(128)S(1)} %pad_add_fusion.refs_0_, s32[6,32]{1,0:T(8,128)S(1)} %bitcast.10, ...), custom_call_target="tpu_custom_call" | custom-call | flops 1207959552 | bytes 6291456 | tf_op jit(solution)/shard_map/far/pallas_call | solution.py:256
  21.8 0.2 collective-permute-start.5
  22.0 0.4 collective-permute-start.1
  22.4 0.1 collective-permute-start.3
  22.5 0.7 %first.1.refs_2_ = f32[128,512]{1,0:T(8,128)S(1)} custom-call(bf16[128,4096]{1,0:T(8,128)(2,1)S(1)} %get-tuple-element.51.refs_1_.both, bf16[4096,2048]{1,0:T(8,128)(2,1)S(1)} %get-tuple-element.52.refs_2_.w_ref), custom_call_target="tpu_custom_call" | custom-call | flops 536870912 | bytes 4194304 | tf_op jit(solution)/shard_map/first/pallas_call | solution.py:283
  23.3 0.1 collective-permute-done.5.refs_4_
  23.3 0.2 send.4
  23.5 1.8 %collective-permute-start.6 = (bf16[112,512]{1,0:T(8,128)(2,1)S(1)}, bf16[112,512]{1,0:T(8,128)(2,1)S(1)}, u32[]{:S(2)}, u32[]{:S(2)}) collective-permute-start(bf16[112,512]{1,0:T(8,128)(2,1)S(1)} %get-tuple-element.58), channel_id=1, source_target_pairs={{0,8},{4,12},{8,0},{12,4},{1,9},{5,13},{9,1},{13,5},{2,10},{6,14},... | collective-permute-start | bytes 344072 | tf_op jit(solution)/shard_map/ppermute | solution.py:416
  25.3 0.0 collective-permute-start.7
  25.4 1.0 %send.5 = (bf16[112,768]{1,0:T(8,128)(2,1)S(1)}, bf16[112,768]{1,0:T(8,128)(2,1)S(1)}) custom-call(bf16[128,128]{1,0:T(8,128)(2,1)S(1)} %get-tuple-element.50.refs_0_, bf16[128,4096]{1,0:T(8,128)(2,1)S(1)} %get-tuple-element.51.refs_1_.both, bf16[4096,2048]{1,0:T(8,128)(2,1)S(1)} %get-tuple-element.52.refs_2_.w_ref, ...), custom_call_target="tpu_custom_call" | custom-call | flops 805306368 | bytes 6291456 | tf_op jit(solution)/shard_map/send/pallas_call | solution.py:320
  26.4 1.7 %collective-permute-start.11 = (bf16[112,768]{1,0:T(8,128)(2,1)S(1)}, bf16[112,768]{1,0:T(8,128)(2,1)S(1)}, u32[]{:S(2)}, u32[]{:S(2)}) collective-permute-start(bf16[112,768]{1,0:T(8,128)(2,1)S(1)} %get-tuple-element.67), channel_id=1, source_target_pairs={{0,8},{4,12},{8,0},{12,4},{1,9},{5,13},{9,1},{13,5},{2,10},{6,14},... | collective-permute-start | bytes 516104 | tf_op jit(solution)/shard_map/ppermute | solution.py:416
  28.1 1.4 %collective-permute-done.6.refs_6_ = bf16[112,512]{1,0:T(8,128)(2,1)S(1)} collective-permute-done((bf16[112,512]{1,0:T(8,128)(2,1)S(1)}, bf16[112,512]{1,0:T(8,128)(2,1)S(1)}, u32[]{:S(2)}, u32[]{:S(2)}) %collective-permute-start.6) | collective-permute-done | bytes 114720 | tf_op jit(solution)/shard_map/ppermute | solution.py:416
  29.6 0.3 collective-permute-start.12
  29.8 1.0 %send.3 = (bf16[112,768]{1,0:T(8,128)(2,1)S(1)}, bf16[112,768]{1,0:T(8,128)(2,1)S(1)}) custom-call(bf16[128,128]{1,0:T(8,128)(2,1)S(1)} %get-tuple-element.50.refs_0_, bf16[128,4096]{1,0:T(8,128)(2,1)S(1)} %get-tuple-element.51.refs_1_.both, bf16[4096,2048]{1,0:T(8,128)(2,1)S(1)} %get-tuple-element.52.refs_2_.w_ref, ...), custom_call_target="tpu_custom_call" | custom-call | flops 805306368 | bytes 6291456 | tf_op jit(solution)/shard_map/send/pallas_call | solution.py:320
  30.9 0.4 collective-permute-done.7.refs_7_
  31.3 0.0 collective-permute-done.3.refs_5_
  31.3 0.0 collective-permute-done.1.refs_3_
  31.3 0.9 %merge.3 = (f32[64,512]{1,0:T(8,128)S(1)}, bf16[64,512]{1,0:T(8,128)(2,1)S(1)}, bf16[64,512]{1,0:T(8,128)(2,1)S(1)}, bf16[64,512]{1,0:T(8,128)(2,1)S(1)}) custom-call(s32[2]{0:T(128)S(1)} %pad_add_fusion.refs_0_, bf16[5,64,128]{2,1,0:T(8,128)(2,1)S(1)} %get-tuple-element.42.refs_1_, bf16[24,8192]{1,0:T(8,128)(2,1)S(1)} %get-tuple-element.43.refs_2_, ...), custom_call_target="tpu_custom_call" | custom-call | flops 67108864 | bytes 1048576 | tf_op jit(solution)/shard_map/merge/pallas_call | solution.py:377
  32.2 1.6 %collective-permute-start.8 = (bf16[64,512]{1,0:T(8,128)(2,1)S(1)}, bf16[64,512]{1,0:T(8,128)(2,1)S(1)}, u32[]{:S(2)}, u32[]{:S(2)}) collective-permute-start(bf16[64,512]{1,0:T(8,128)(2,1)S(1)} %get-tuple-element.64), channel_id=1, source_target_pairs={{0,1},{1,2},{2,3},{3,0},{4,5},{5,6},{6,7},{7,4},{8,9},{9,10},{10,1... | collective-permute-start | bytes 196616 | tf_op jit(solution)/shard_map/ppermute | solution.py:464
  33.8 2.6 %collective-permute-start.9 = (bf16[64,512]{1,0:T(8,128)(2,1)S(1)}, bf16[64,512]{1,0:T(8,128)(2,1)S(1)}, u32[]{:S(2)}, u32[]{:S(2)}) collective-permute-start(bf16[64,512]{1,0:T(8,128)(2,1)S(1)} %get-tuple-element.65), channel_id=1, source_target_pairs={{0,2},{1,3},{2,0},{3,1},{4,6},{5,7},{6,4},{7,5},{8,10},{9,11},{10,... | collective-permute-start | bytes 196616 | tf_op jit(solution)/shard_map/ppermute | solution.py:464
  36.4 1.3 %collective-permute-start.10 = (bf16[64,512]{1,0:T(8,128)(2,1)S(1)}, bf16[64,512]{1,0:T(8,128)(2,1)S(1)}, u32[]{:S(2)}, u32[]{:S(2)}) collective-permute-start(bf16[64,512]{1,0:T(8,128)(2,1)S(1)} %get-tuple-element.66), channel_id=1, source_target_pairs={{0,3},{1,0},{2,1},{3,2},{4,7},{5,4},{6,5},{7,6},{8,11},{9,8},{10,9... | collective-permute-start | bytes 196616 | tf_op jit(solution)/shard_map/ppermute | solution.py:464
  37.7 0.0 collective-permute-done.11.refs_6_
  37.7 1.1 %collective-permute-start.17 = (bf16[112,768]{1,0:T(8,128)(2,1)S(1)}, bf16[112,768]{1,0:T(8,128)(2,1)S(1)}, u32[]{:S(2)}, u32[]{:S(2)}) collective-permute-start(bf16[112,768]{1,0:T(8,128)(2,1)S(1)} %get-tuple-element.74), channel_id=1, source_target_pairs={{0,12},{4,8},{8,4},{12,0},{1,13},{5,9},{9,5},{13,1},{2,14},{6,10},... | collective-permute-start | bytes 516104 | tf_op jit(solution)/shard_map/ppermute | solution.py:416
  38.8 0.0 collective-permute-done.12.refs_7_
  38.8 1.1 %collective-permute-start.16 = (bf16[112,768]{1,0:T(8,128)(2,1)S(1)}, bf16[112,768]{1,0:T(8,128)(2,1)S(1)}, u32[]{:S(2)}, u32[]{:S(2)}) collective-permute-start(bf16[112,768]{1,0:T(8,128)(2,1)S(1)} %get-tuple-element.73), channel_id=1, source_target_pairs={{0,8},{4,12},{8,0},{12,4},{1,9},{5,13},{9,1},{13,5},{2,10},{6,14},... | collective-permute-start | bytes 516104 | tf_op jit(solution)/shard_map/ppermute | solution.py:416
  39.9 1.0 %merge.4 = (f32[64,768]{1,0:T(8,128)S(1)}, bf16[64,768]{1,0:T(8,128)(2,1)S(1)}, bf16[64,768]{1,0:T(8,128)(2,1)S(1)}, bf16[64,768]{1,0:T(8,128)(2,1)S(1)}) custom-call(s32[2]{0:T(128)S(1)} %pad_add_fusion.refs_0_, bf16[5,64,128]{2,1,0:T(8,128)(2,1)S(1)} %get-tuple-element.42.refs_1_, bf16[24,8192]{1,0:T(8,128)(2,1)S(1)} %get-tuple-element.43.refs_2_, ...), custom_call_target="tpu_custom_call" | custom-call | flops 100663296 | bytes 1572864 | tf_op jit(solution)/shard_map/merge/pallas_call | solution.py:377
  40.9 0.0 collective-permute-done.8
  40.9 1.6 %collective-permute-start.13 = (bf16[64,768]{1,0:T(8,128)(2,1)S(1)}, bf16[64,768]{1,0:T(8,128)(2,1)S(1)}, u32[]{:S(2)}, u32[]{:S(2)}) collective-permute-start(bf16[64,768]{1,0:T(8,128)(2,1)S(1)} %get-tuple-element.70), channel_id=1, source_target_pairs={{0,1},{1,2},{2,3},{3,0},{4,5},{5,6},{6,7},{7,4},{8,9},{9,10},{10,1... | collective-permute-start | bytes 294920 | tf_op jit(solution)/shard_map/ppermute | solution.py:464
  42.5 0.0 collective-permute-done.9
  42.6 2.6 %collective-permute-start.14 = (bf16[64,768]{1,0:T(8,128)(2,1)S(1)}, bf16[64,768]{1,0:T(8,128)(2,1)S(1)}, u32[]{:S(2)}, u32[]{:S(2)}) collective-permute-start(bf16[64,768]{1,0:T(8,128)(2,1)S(1)} %get-tuple-element.71), channel_id=1, source_target_pairs={{0,2},{1,3},{2,0},{3,1},{4,6},{5,7},{6,4},{7,5},{8,10},{9,11},{10,... | collective-permute-start | bytes 294920 | tf_op jit(solution)/shard_map/ppermute | solution.py:464
  45.2 0.0 collective-permute-done.10
  45.2 1.3 %collective-permute-start.15 = (bf16[64,768]{1,0:T(8,128)(2,1)S(1)}, bf16[64,768]{1,0:T(8,128)(2,1)S(1)}, u32[]{:S(2)}, u32[]{:S(2)}) collective-permute-start(bf16[64,768]{1,0:T(8,128)(2,1)S(1)} %get-tuple-element.72), channel_id=1, source_target_pairs={{0,3},{1,0},{2,1},{3,2},{4,7},{5,4},{6,5},{7,6},{8,11},{9,8},{10,9... | collective-permute-start | bytes 294920 | tf_op jit(solution)/shard_map/ppermute | solution.py:464
  46.5 0.0 collective-permute-done.17.refs_7_
  46.5 1.6 %collective-permute-done.16.refs_6_ = bf16[112,768]{1,0:T(8,128)(2,1)S(1)} collective-permute-done((bf16[112,768]{1,0:T(8,128)(2,1)S(1)}, bf16[112,768]{1,0:T(8,128)(2,1)S(1)}, u32[]{:S(2)}, u32[]{:S(2)}) %collective-permute-start.16) | collective-permute-done | bytes 172064 | tf_op jit(solution)/shard_map/ppermute | solution.py:416
  48.1 1.0 %merge.5 = (f32[64,768]{1,0:T(8,128)S(1)}, bf16[64,768]{1,0:T(8,128)(2,1)S(1)}, bf16[64,768]{1,0:T(8,128)(2,1)S(1)}, bf16[64,768]{1,0:T(8,128)(2,1)S(1)}) custom-call(s32[2]{0:T(128)S(1)} %pad_add_fusion.refs_0_, bf16[5,64,128]{2,1,0:T(8,128)(2,1)S(1)} %get-tuple-element.42.refs_1_, bf16[24,8192]{1,0:T(8,128)(2,1)S(1)} %get-tuple-element.43.refs_2_, ...), custom_call_target="tpu_custom_call" | custom-call | flops 100663296 | bytes 1572864 | tf_op jit(solution)/shard_map/merge/pallas_call | solution.py:377
  49.1 0.7 %collective-permute-start.18 = (bf16[64,768]{1,0:T(8,128)(2,1)S(1)}, bf16[64,768]{1,0:T(8,128)(2,1)S(1)}, u32[]{:S(2)}, u32[]{:S(2)}) collective-permute-start(bf16[64,768]{1,0:T(8,128)(2,1)S(1)} %get-tuple-element.76), channel_id=1, source_target_pairs={{0,1},{1,2},{2,3},{3,0},{4,5},{5,6},{6,7},{7,4},{8,9},{9,10},{10,1... | collective-permute-start | bytes 294920 | tf_op jit(solution)/shard_map/ppermute | solution.py:464
  49.8 1.8 %collective-permute-start.19 = (bf16[64,768]{1,0:T(8,128)(2,1)S(1)}, bf16[64,768]{1,0:T(8,128)(2,1)S(1)}, u32[]{:S(2)}, u32[]{:S(2)}) collective-permute-start(bf16[64,768]{1,0:T(8,128)(2,1)S(1)} %get-tuple-element.77), channel_id=1, source_target_pairs={{0,2},{1,3},{2,0},{3,1},{4,6},{5,7},{6,4},{7,5},{8,10},{9,11},{10,... | collective-permute-start | bytes 294920 | tf_op jit(solution)/shard_map/ppermute | solution.py:464
  51.6 0.0 collective-permute-done.13
  51.6 1.3 %collective-permute-start.20 = (bf16[64,768]{1,0:T(8,128)(2,1)S(1)}, bf16[64,768]{1,0:T(8,128)(2,1)S(1)}, u32[]{:S(2)}, u32[]{:S(2)}) collective-permute-start(bf16[64,768]{1,0:T(8,128)(2,1)S(1)} %get-tuple-element.78), channel_id=1, source_target_pairs={{0,3},{1,0},{2,1},{3,2},{4,7},{5,4},{6,5},{7,6},{8,11},{9,8},{10,9... | collective-permute-start | bytes 294920 | tf_op jit(solution)/shard_map/ppermute | solution.py:464
  53.0 0.0 collective-permute-done.14
  53.0 0.0 collective-permute-done.15
  53.0 0.1 add_convert_fusion.1
  53.0 3.6 %collective-permute-done.18 = bf16[64,768]{1,0:T(8,128)(2,1)S(1)} collective-permute-done((bf16[64,768]{1,0:T(8,128)(2,1)S(1)}, bf16[64,768]{1,0:T(8,128)(2,1)S(1)}, u32[]{:S(2)}, u32[]{:S(2)}) %collective-permute-start.18) | collective-permute-done | bytes 98336 | tf_op jit(solution)/shard_map/ppermute | solution.py:464
  56.7 4.1 %collective-permute-done.19 = bf16[64,768]{1,0:T(8,128)(2,1)S(1)} collective-permute-done((bf16[64,768]{1,0:T(8,128)(2,1)S(1)}, bf16[64,768]{1,0:T(8,128)(2,1)S(1)}, u32[]{:S(2)}, u32[]{:S(2)}) %collective-permute-start.19) | collective-permute-done | bytes 98336 | tf_op jit(solution)/shard_map/ppermute | solution.py:464
  60.7 0.0 collective-permute-done.20
  60.7 0.1 add_convert_fusion
  60.8 0.7 %pad_maximum_fusion = bf16[64,2048]{1,0:T(8,128)(2,1)} fusion(bf16[64,768]{1,0:T(8,128)(2,1)S(1)} %add_convert_fusion, bf16[64,768]{1,0:T(8,128)(2,1)S(1)} %add_convert_fusion.1, bf16[64,512]{1,0:T(8,128)(2,1)S(1)} %add_convert_fusion.2), kind=kLoop, calls=%fused_computation | loop fusion | flops 786432 | bytes 524288 | tf_op jit(solution)/shard_map/concatenate | solution.py:466
  (1 shorter events, 0.0 us)
Async XLA Ops:
  1.5 3.8 %collective-permute-start = (bf16[64,4224]{1,0:T(8,128)(2,1)S(1)}, bf16[64,4224]{1,0:T(8,128)(2,1)S(1)}, u32[]{:S(2)}, u32[]{:S(2)}) collective-permute-start(bf16[64,4224]{1,0:T(8,128)(2,1)S(1)} %hidden.1.refs_2_), channel_id=1, source_target_pairs={{0,4},{4,0},{8,12},{12,8},{1,5},{5,1},{9,13},{13,9},{2,6},{6,2},{1... | collective-permute-start | bytes 1622024 | tf_op jit(solution)/shard_map/ppermute | solution.py:416
  2.0 15.4 %collective-permute-start.2 = (bf16[64,4224]{1,0:T(8,128)(2,1)S(1)}, bf16[64,4224]{1,0:T(8,128)(2,1)S(1)}, u32[]{:S(2)}, u32[]{:S(2)}) collective-permute-start(bf16[64,4224]{1,0:T(8,128)(2,1)S(1)} %hidden.1.refs_2_), channel_id=1, source_target_pairs={{0,8},{4,12},{8,0},{12,4},{1,9},{5,13},{9,1},{13,5},{2,10},{6,14},... | collective-permute-start | bytes 1622024 | tf_op jit(solution)/shard_map/ppermute | solution.py:416
  17.4 1.9 %collective-permute-start.4 = (bf16[64,4224]{1,0:T(8,128)(2,1)S(1)}, bf16[64,4224]{1,0:T(8,128)(2,1)S(1)}, u32[]{:S(2)}, u32[]{:S(2)}) collective-permute-start(bf16[64,4224]{1,0:T(8,128)(2,1)S(1)} %collective-permute-done.2.refs_2_), channel_id=1, source_target_pairs={{0,4},{4,0},{8,12},{12,8},{1,5},{5,1},{9,13},{13,9},{2,6},{6,2},{1... | collective-permute-start | bytes 1622024 | tf_op jit(solution)/shard_map/ppermute | solution.py:416
  21.8 1.5 %collective-permute-start.5 = (bf16[48,2048]{1,0:T(8,128)(2,1)S(1)}, bf16[48,2048]{1,0:T(8,128)(2,1)S(1)}, u32[]{:S(2)}, u32[]{:S(2)}) collective-permute-start(bf16[48,2048]{1,0:T(8,128)(2,1)S(1)} %get-tuple-element.54), channel_id=1, source_target_pairs={{0,4},{4,0},{8,12},{12,8},{1,5},{5,1},{9,13},{13,9},{2,6},{6,2},{1... | collective-permute-start | bytes 589832 | tf_op jit(solution)/shard_map/ppermute | solution.py:416
  22.0 9.3 %collective-permute-start.1 = (bf16[24,8192]{1,0:T(8,128)(2,1)S(1)}, bf16[24,8192]{1,0:T(8,128)(2,1)S(1)}, u32[]{:S(2)}, u32[]{:S(2)}) collective-permute-start(bf16[24,8192]{1,0:T(8,128)(2,1)S(1)} %get-tuple-element.44), channel_id=1, source_target_pairs={{0,4},{4,0},{8,12},{12,8},{1,5},{5,1},{9,13},{13,9},{2,6},{6,2},{1... | collective-permute-start | bytes 1179656 | tf_op jit(solution)/shard_map/ppermute | solution.py:416
  22.4 8.9 %collective-permute-start.3 = (bf16[64,2048]{1,0:T(8,128)(2,1)S(1)}, bf16[64,2048]{1,0:T(8,128)(2,1)S(1)}, u32[]{:S(2)}, u32[]{:S(2)}) collective-permute-start(bf16[64,2048]{1,0:T(8,128)(2,1)S(1)} %get-tuple-element.47), channel_id=1, source_target_pairs={{0,4},{4,0},{8,12},{12,8},{1,5},{5,1},{9,13},{13,9},{2,6},{6,2},{1... | collective-permute-start | bytes 786440 | tf_op jit(solution)/shard_map/ppermute | solution.py:416
  23.5 6.0 %collective-permute-start.6 = (bf16[112,512]{1,0:T(8,128)(2,1)S(1)}, bf16[112,512]{1,0:T(8,128)(2,1)S(1)}, u32[]{:S(2)}, u32[]{:S(2)}) collective-permute-start(bf16[112,512]{1,0:T(8,128)(2,1)S(1)} %get-tuple-element.58), channel_id=1, source_target_pairs={{0,8},{4,12},{8,0},{12,4},{1,9},{5,13},{9,1},{13,5},{2,10},{6,14},... | collective-permute-start | bytes 344072 | tf_op jit(solution)/shard_map/ppermute | solution.py:416
  25.3 5.9 %collective-permute-start.7 = (bf16[112,512]{1,0:T(8,128)(2,1)S(1)}, bf16[112,512]{1,0:T(8,128)(2,1)S(1)}, u32[]{:S(2)}, u32[]{:S(2)}) collective-permute-start(bf16[112,512]{1,0:T(8,128)(2,1)S(1)} %get-tuple-element.61), channel_id=1, source_target_pairs={{0,12},{4,8},{8,4},{12,0},{1,13},{5,9},{9,5},{13,1},{2,14},{6,10},... | collective-permute-start | bytes 344072 | tf_op jit(solution)/shard_map/ppermute | solution.py:416
  26.4 11.3 %collective-permute-start.11 = (bf16[112,768]{1,0:T(8,128)(2,1)S(1)}, bf16[112,768]{1,0:T(8,128)(2,1)S(1)}, u32[]{:S(2)}, u32[]{:S(2)}) collective-permute-start(bf16[112,768]{1,0:T(8,128)(2,1)S(1)} %get-tuple-element.67), channel_id=1, source_target_pairs={{0,8},{4,12},{8,0},{12,4},{1,9},{5,13},{9,1},{13,5},{2,10},{6,14},... | collective-permute-start | bytes 516104 | tf_op jit(solution)/shard_map/ppermute | solution.py:416
  29.6 9.2 %collective-permute-start.12 = (bf16[112,768]{1,0:T(8,128)(2,1)S(1)}, bf16[112,768]{1,0:T(8,128)(2,1)S(1)}, u32[]{:S(2)}, u32[]{:S(2)}) collective-permute-start(bf16[112,768]{1,0:T(8,128)(2,1)S(1)} %get-tuple-element.68), channel_id=1, source_target_pairs={{0,12},{4,8},{8,4},{12,0},{1,13},{5,9},{9,5},{13,1},{2,14},{6,10},... | collective-permute-start | bytes 516104 | tf_op jit(solution)/shard_map/ppermute | solution.py:416
  32.2 8.7 %collective-permute-start.8 = (bf16[64,512]{1,0:T(8,128)(2,1)S(1)}, bf16[64,512]{1,0:T(8,128)(2,1)S(1)}, u32[]{:S(2)}, u32[]{:S(2)}) collective-permute-start(bf16[64,512]{1,0:T(8,128)(2,1)S(1)} %get-tuple-element.64), channel_id=1, source_target_pairs={{0,1},{1,2},{2,3},{3,0},{4,5},{5,6},{6,7},{7,4},{8,9},{9,10},{10,1... | collective-permute-start | bytes 196616 | tf_op jit(solution)/shard_map/ppermute | solution.py:464
  33.8 8.8 %collective-permute-start.9 = (bf16[64,512]{1,0:T(8,128)(2,1)S(1)}, bf16[64,512]{1,0:T(8,128)(2,1)S(1)}, u32[]{:S(2)}, u32[]{:S(2)}) collective-permute-start(bf16[64,512]{1,0:T(8,128)(2,1)S(1)} %get-tuple-element.65), channel_id=1, source_target_pairs={{0,2},{1,3},{2,0},{3,1},{4,6},{5,7},{6,4},{7,5},{8,10},{9,11},{10,... | collective-permute-start | bytes 196616 | tf_op jit(solution)/shard_map/ppermute | solution.py:464
  36.4 8.8 %collective-permute-start.10 = (bf16[64,512]{1,0:T(8,128)(2,1)S(1)}, bf16[64,512]{1,0:T(8,128)(2,1)S(1)}, u32[]{:S(2)}, u32[]{:S(2)}) collective-permute-start(bf16[64,512]{1,0:T(8,128)(2,1)S(1)} %get-tuple-element.66), channel_id=1, source_target_pairs={{0,3},{1,0},{2,1},{3,2},{4,7},{5,4},{6,5},{7,6},{8,11},{9,8},{10,9... | collective-permute-start | bytes 196616 | tf_op jit(solution)/shard_map/ppermute | solution.py:464
  37.7 8.8 %collective-permute-start.17 = (bf16[112,768]{1,0:T(8,128)(2,1)S(1)}, bf16[112,768]{1,0:T(8,128)(2,1)S(1)}, u32[]{:S(2)}, u32[]{:S(2)}) collective-permute-start(bf16[112,768]{1,0:T(8,128)(2,1)S(1)} %get-tuple-element.74), channel_id=1, source_target_pairs={{0,12},{4,8},{8,4},{12,0},{1,13},{5,9},{9,5},{13,1},{2,14},{6,10},... | collective-permute-start | bytes 516104 | tf_op jit(solution)/shard_map/ppermute | solution.py:416
  38.8 9.3 %collective-permute-start.16 = (bf16[112,768]{1,0:T(8,128)(2,1)S(1)}, bf16[112,768]{1,0:T(8,128)(2,1)S(1)}, u32[]{:S(2)}, u32[]{:S(2)}) collective-permute-start(bf16[112,768]{1,0:T(8,128)(2,1)S(1)} %get-tuple-element.73), channel_id=1, source_target_pairs={{0,8},{4,12},{8,0},{12,4},{1,9},{5,13},{9,1},{13,5},{2,10},{6,14},... | collective-permute-start | bytes 516104 | tf_op jit(solution)/shard_map/ppermute | solution.py:416
  40.9 10.7 %collective-permute-start.13 = (bf16[64,768]{1,0:T(8,128)(2,1)S(1)}, bf16[64,768]{1,0:T(8,128)(2,1)S(1)}, u32[]{:S(2)}, u32[]{:S(2)}) collective-permute-start(bf16[64,768]{1,0:T(8,128)(2,1)S(1)} %get-tuple-element.70), channel_id=1, source_target_pairs={{0,1},{1,2},{2,3},{3,0},{4,5},{5,6},{6,7},{7,4},{8,9},{9,10},{10,1... | collective-permute-start | bytes 294920 | tf_op jit(solution)/shard_map/ppermute | solution.py:464
  42.6 10.4 %collective-permute-start.14 = (bf16[64,768]{1,0:T(8,128)(2,1)S(1)}, bf16[64,768]{1,0:T(8,128)(2,1)S(1)}, u32[]{:S(2)}, u32[]{:S(2)}) collective-permute-start(bf16[64,768]{1,0:T(8,128)(2,1)S(1)} %get-tuple-element.71), channel_id=1, source_target_pairs={{0,2},{1,3},{2,0},{3,1},{4,6},{5,7},{6,4},{7,5},{8,10},{9,11},{10,... | collective-permute-start | bytes 294920 | tf_op jit(solution)/shard_map/ppermute | solution.py:464
  45.2 7.8 %collective-permute-start.15 = (bf16[64,768]{1,0:T(8,128)(2,1)S(1)}, bf16[64,768]{1,0:T(8,128)(2,1)S(1)}, u32[]{:S(2)}, u32[]{:S(2)}) collective-permute-start(bf16[64,768]{1,0:T(8,128)(2,1)S(1)} %get-tuple-element.72), channel_id=1, source_target_pairs={{0,3},{1,0},{2,1},{3,2},{4,7},{5,4},{6,5},{7,6},{8,11},{9,8},{10,9... | collective-permute-start | bytes 294920 | tf_op jit(solution)/shard_map/ppermute | solution.py:464
  49.1 7.6 %collective-permute-start.18 = (bf16[64,768]{1,0:T(8,128)(2,1)S(1)}, bf16[64,768]{1,0:T(8,128)(2,1)S(1)}, u32[]{:S(2)}, u32[]{:S(2)}) collective-permute-start(bf16[64,768]{1,0:T(8,128)(2,1)S(1)} %get-tuple-element.76), channel_id=1, source_target_pairs={{0,1},{1,2},{2,3},{3,0},{4,5},{5,6},{6,7},{7,4},{8,9},{9,10},{10,1... | collective-permute-start | bytes 294920 | tf_op jit(solution)/shard_map/ppermute | solution.py:464
  49.8 10.9 %collective-permute-start.19 = (bf16[64,768]{1,0:T(8,128)(2,1)S(1)}, bf16[64,768]{1,0:T(8,128)(2,1)S(1)}, u32[]{:S(2)}, u32[]{:S(2)}) collective-permute-start(bf16[64,768]{1,0:T(8,128)(2,1)S(1)} %get-tuple-element.77), channel_id=1, source_target_pairs={{0,2},{1,3},{2,0},{3,1},{4,6},{5,7},{6,4},{7,5},{8,10},{9,11},{10,... | collective-permute-start | bytes 294920 | tf_op jit(solution)/shard_map/ppermute | solution.py:464
  51.6 9.1 %collective-permute-start.20 = (bf16[64,768]{1,0:T(8,128)(2,1)S(1)}, bf16[64,768]{1,0:T(8,128)(2,1)S(1)}, u32[]{:S(2)}, u32[]{:S(2)}) collective-permute-start(bf16[64,768]{1,0:T(8,128)(2,1)S(1)} %get-tuple-element.78), channel_id=1, source_target_pairs={{0,3},{1,0},{2,1},{3,2},{4,7},{5,4},{6,5},{7,6},{8,11},{9,8},{10,9... | collective-permute-start | bytes 294920 | tf_op jit(solution)/shard_map/ppermute | solution.py:464

commit v6 on v5

--- a/solution.py
+++ b/solution.py
@@ -12,7 +12,7 @@
 LANES = 128
 VMEM_LIMIT = 16 * 1024 * 1024
 PARTS = (2, 3, 3)
-LAG = 4
+LAG = 5
 ORDER = (1, 2, 3)
 
 

time: 61.7 us -> 61.5 us (level)
  waiting for transfers between devices: 14.5 us -> 13.3 us
  starting transfers between devices: 24.8 us -> 25.8 us
    ppermute x12, waiting for transfers between devices: 6.79 us -> 5.27 us  [permute(): return lax.ppermute(v, 'rows', perm)]
    ppermute x9, starting transfers between devices: 15 us -> 15.7 us  [shards(): total = total + lax.ppermute(terms[dz], 'tensor', perm).astype(F32)]
where the time goes in v6:
time: 61.5 us; the launch traced here: 61.4 us
  starting transfers between devices  25.8 us (42%)
  Pallas kernels  20.5 us (33%)
  waiting for transfers between devices  13.3 us (22%)
  other arithmetic  0.93 us (2%)
  local copies, waits for them, and re-layouts  0.68 us (1%)
    ppermute x9, starting transfers between devices, shards(): total = total + lax.ppermute(terms[dz], 'tensor', perm).astype(F32)  15.7 us
    pallas_call x1, Pallas kernels, near_of(): pl.pallas_call(functools.partial(near_kernel, cap, nt, nw), in_specs=[sme...  10.8 us
    ppermute x12, starting transfers between devices, permute(): return lax.ppermute(v, 'rows', perm)  10.1 us
    ppermute x9, waiting for transfers between devices, shards(): total = total + lax.ppermute(terms[dz], 'tensor', perm).astype(F32)  8.07 us
    ppermute x12, waiting for transfers between devices, permute(): return lax.ppermute(v, 'rows', perm)  5.27 us
    pallas_call x3, Pallas kernels, merge_of(): pl.pallas_call(functools.partial(merge_kernel, cap, groups, nz, bw, start...  2.85 us
    pallas_call x1, Pallas kernels, far_of(): pl.pallas_call(functools.partial(far_kernel, cap, bw), in_specs=[smem(),...  2.44 us
    pallas_call x3, Pallas kernels, send_of(): pl.pallas_call(functools.partial(send_kernel, cap, start), in_specs=[whol...  2.25 us
  transfers between devices with their start and end apart: 21, of which 8 were waited for; matrix products, arithmetic and copies ran while one was open for 1% of the time, Pallas kernels for 23%

profile of v6, /device:TPU:0, one launch (start us, length us, event | category | flops | bytes accessed | tf_op | source)
XLA Modules:
  0.0 61.4 jit_solution(10286084925244922606)
XLA Ops:
  0.0 1.5 %hidden.1.refs_2_ = bf16[64,4224]{1,0:T(8,128)(2,1)S(1)} custom-call(s32[1,64]{1,0:T(1,128)} %bitcast.12, bf16[64,4096]{1,0:T(8,128)(2,1)} %gate_hbm.1, bf16[64,4096]{1,0:T(8,128)(2,1)} %up_hbm.1), custom_call_target="tpu_custom_call" | custom-call | flops 1572864 | bytes 1572864 | tf_op jit(solution)/shard_map/hidden/pallas_call | solution.py:61
  1.5 0.5 collective-permute-start
  2.0 2.6 %collective-permute-start.2 = (bf16[64,4224]{1,0:T(8,128)(2,1)S(1)}, bf16[64,4224]{1,0:T(8,128)(2,1)S(1)}, u32[]{:S(2)}, u32[]{:S(2)}) collective-permute-start(bf16[64,4224]{1,0:T(8,128)(2,1)S(1)} %hidden.1.refs_2_), channel_id=1, source_target_pairs={{0,8},{4,12},{8,0},{12,4},{1,9},{5,13},{9,1},{13,5},{2,10},{6,14},... | collective-permute-start | bytes 1622024 | tf_op jit(solution)/shard_map/ppermute | solution.py:416
  4.6 0.7 %copy.9 = s32[1,32,6]{1,2,0:T(8,128)S(1)} copy(s32[1,32,6]{1,0,2:T(1,128)} %param.10) | data formatting | bytes 1536
  5.3 0.1 pad_add_fusion.refs_0_
  5.3 0.0 collective-permute-done.refs_3_
  5.3 10.8 %near.1 = (bf16[24,8192]{1,0:T(8,128)(2,1)S(1)}, bf16[24,8192]{1,0:T(8,128)(2,1)S(1)}, bf16[64,2048]{1,0:T(8,128)(2,1)S(1)}, bf16[64,2048]{1,0:T(8,128)(2,1)S(1)...) custom-call(s32[2]{0:T(128)S(1)} %pad_add_fusion.refs_0_, ...), custom_call_target="tpu_custom_call" | custom-call | flops 2147483648 | bytes 46137344 | tf_op jit(solution)/shard_map/near/pallas_call | solution.py:191
  16.1 1.3 %collective-permute-done.2.refs_2_ = bf16[64,4224]{1,0:T(8,128)(2,1)S(1)} collective-permute-done((bf16[64,4224]{1,0:T(8,128)(2,1)S(1)}, bf16[64,4224]{1,0:T(8,128)(2,1)S(1)}, u32[]{:S(2)}, u32[]{:S(2)}) %collective-permute-start.2) | collective-permute-done | bytes 540704 | tf_op jit(solution)/shard_map/ppermute | solution.py:416
  17.4 0.0 collective-permute-start.4
  17.4 1.9 %collective-permute-done.4.refs_3_ = bf16[64,4224]{1,0:T(8,128)(2,1)S(1)} collective-permute-done((bf16[64,4224]{1,0:T(8,128)(2,1)S(1)}, bf16[64,4224]{1,0:T(8,128)(2,1)S(1)}, u32[]{:S(2)}, u32[]{:S(2)}) %collective-permute-start.4) | collective-permute-done | bytes 540704 | tf_op jit(solution)/shard_map/ppermute | solution.py:416
  19.4 2.4 %far.1 = (bf16[48,2048]{1,0:T(8,128)(2,1)S(1)}, bf16[48,2048]{1,0:T(8,128)(2,1)S(1)}, bf16[48,2048]{1,0:T(8,128)(2,1)S(1)}, bf16[48,2048]{1,0:T(8,128)(2,1)S(1)}...) custom-call(s32[2]{0:T(128)S(1)} %pad_add_fusion.refs_0_, s32[6,32]{1,0:T(8,128)S(1)} %bitcast.10, ...), custom_call_target="tpu_custom_call" | custom-call | flops 1207959552 | bytes 6291456 | tf_op jit(solution)/shard_map/far/pallas_call | solution.py:256
  21.8 0.2 collective-permute-start.5
  22.0 0.4 collective-permute-start.1
  22.4 0.1 collective-permute-start.3
  22.5 0.7 %first.1.refs_2_ = f32[128,512]{1,0:T(8,128)S(1)} custom-call(bf16[128,4096]{1,0:T(8,128)(2,1)S(1)} %get-tuple-element.49.refs_1_.both, bf16[4096,2048]{1,0:T(8,128)(2,1)S(1)} %get-tuple-element.50.refs_2_.w_ref), custom_call_target="tpu_custom_call" | custom-call | flops 536870912 | bytes 4194304 | tf_op jit(solution)/shard_map/first/pallas_call | solution.py:283
  23.3 0.1 collective-permute-done.5.refs_4_
  23.3 0.2 send.4
  23.5 1.8 %collective-permute-start.6 = (bf16[112,512]{1,0:T(8,128)(2,1)S(1)}, bf16[112,512]{1,0:T(8,128)(2,1)S(1)}, u32[]{:S(2)}, u32[]{:S(2)}) collective-permute-start(bf16[112,512]{1,0:T(8,128)(2,1)S(1)} %get-tuple-element.56), channel_id=1, source_target_pairs={{0,8},{4,12},{8,0},{12,4},{1,9},{5,13},{9,1},{13,5},{2,10},{6,14},... | collective-permute-start | bytes 344072 | tf_op jit(solution)/shard_map/ppermute | solution.py:416
  25.3 0.0 collective-permute-start.7
  25.4 1.0 %send.5 = (bf16[112,768]{1,0:T(8,128)(2,1)S(1)}, bf16[112,768]{1,0:T(8,128)(2,1)S(1)}) custom-call(bf16[128,128]{1,0:T(8,128)(2,1)S(1)} %get-tuple-element.48.refs_0_, bf16[128,4096]{1,0:T(8,128)(2,1)S(1)} %get-tuple-element.49.refs_1_.both, bf16[4096,2048]{1,0:T(8,128)(2,1)S(1)} %get-tuple-element.50.refs_2_.w_ref, ...), custom_call_target="tpu_custom_call" | custom-call | flops 805306368 | bytes 6291456 | tf_op jit(solution)/shard_map/send/pallas_call | solution.py:320
  26.4 1.7 %collective-permute-start.11 = (bf16[112,768]{1,0:T(8,128)(2,1)S(1)}, bf16[112,768]{1,0:T(8,128)(2,1)S(1)}, u32[]{:S(2)}, u32[]{:S(2)}) collective-permute-start(bf16[112,768]{1,0:T(8,128)(2,1)S(1)} %get-tuple-element.63), channel_id=1, source_target_pairs={{0,8},{4,12},{8,0},{12,4},{1,9},{5,13},{9,1},{13,5},{2,10},{6,14},... | collective-permute-start | bytes 516104 | tf_op jit(solution)/shard_map/ppermute | solution.py:416
  28.1 1.4 %collective-permute-done.6.refs_6_ = bf16[112,512]{1,0:T(8,128)(2,1)S(1)} collective-permute-done((bf16[112,512]{1,0:T(8,128)(2,1)S(1)}, bf16[112,512]{1,0:T(8,128)(2,1)S(1)}, u32[]{:S(2)}, u32[]{:S(2)}) %collective-permute-start.6) | collective-permute-done | bytes 114720 | tf_op jit(solution)/shard_map/ppermute | solution.py:416
  29.5 0.3 collective-permute-start.12
  29.8 1.0 %send.3 = (bf16[112,768]{1,0:T(8,128)(2,1)S(1)}, bf16[112,768]{1,0:T(8,128)(2,1)S(1)}) custom-call(bf16[128,128]{1,0:T(8,128)(2,1)S(1)} %get-tuple-element.48.refs_0_, bf16[128,4096]{1,0:T(8,128)(2,1)S(1)} %get-tuple-element.49.refs_1_.both, bf16[4096,2048]{1,0:T(8,128)(2,1)S(1)} %get-tuple-element.50.refs_2_.w_ref, ...), custom_call_target="tpu_custom_call" | custom-call | flops 805306368 | bytes 6291456 | tf_op jit(solution)/shard_map/send/pallas_call | solution.py:320
  30.9 0.0 collective-permute-done.3.refs_5_
  30.9 0.0 collective-permute-done.1.refs_3_
  30.9 0.4 collective-permute-done.7.refs_7_
  31.3 0.9 %merge.3 = (f32[64,512]{1,0:T(8,128)S(1)}, bf16[64,512]{1,0:T(8,128)(2,1)S(1)}, bf16[64,512]{1,0:T(8,128)(2,1)S(1)}, bf16[64,512]{1,0:T(8,128)(2,1)S(1)}) custom-call(s32[2]{0:T(128)S(1)} %pad_add_fusion.refs_0_, bf16[5,64,128]{2,1,0:T(8,128)(2,1)S(1)} %get-tuple-element.40.refs_1_, bf16[24,8192]{1,0:T(8,128)(2,1)S(1)} %get-tuple-element.41.refs_2_, ...), custom_call_target="tpu_custom_call" | custom-call | flops 67108864 | bytes 1048576 | tf_op jit(solution)/shard_map/merge/pallas_call | solution.py:377
  32.2 1.6 %collective-permute-start.8 = (bf16[64,512]{1,0:T(8,128)(2,1)S(1)}, bf16[64,512]{1,0:T(8,128)(2,1)S(1)}, u32[]{:S(2)}, u32[]{:S(2)}) collective-permute-start(bf16[64,512]{1,0:T(8,128)(2,1)S(1)} %get-tuple-element.60), channel_id=1, source_target_pairs={{0,1},{1,2},{2,3},{3,0},{4,5},{5,6},{6,7},{7,4},{8,9},{9,10},{10,1... | collective-permute-start | bytes 196616 | tf_op jit(solution)/shard_map/ppermute | solution.py:464
  33.8 2.6 %collective-permute-start.9 = (bf16[64,512]{1,0:T(8,128)(2,1)S(1)}, bf16[64,512]{1,0:T(8,128)(2,1)S(1)}, u32[]{:S(2)}, u32[]{:S(2)}) collective-permute-start(bf16[64,512]{1,0:T(8,128)(2,1)S(1)} %get-tuple-element.61), channel_id=1, source_target_pairs={{0,2},{1,3},{2,0},{3,1},{4,6},{5,7},{6,4},{7,5},{8,10},{9,11},{10,... | collective-permute-start | bytes 196616 | tf_op jit(solution)/shard_map/ppermute | solution.py:464
  36.4 1.4 %collective-permute-start.10 = (bf16[64,512]{1,0:T(8,128)(2,1)S(1)}, bf16[64,512]{1,0:T(8,128)(2,1)S(1)}, u32[]{:S(2)}, u32[]{:S(2)}) collective-permute-start(bf16[64,512]{1,0:T(8,128)(2,1)S(1)} %get-tuple-element.62), channel_id=1, source_target_pairs={{0,3},{1,0},{2,1},{3,2},{4,7},{5,4},{6,5},{7,6},{8,11},{9,8},{10,9... | collective-permute-start | bytes 196616 | tf_op jit(solution)/shard_map/ppermute | solution.py:464
  37.7 0.0 collective-permute-done.11.refs_6_
  37.7 1.3 %collective-permute-start.16 = (bf16[112,768]{1,0:T(8,128)(2,1)S(1)}, bf16[112,768]{1,0:T(8,128)(2,1)S(1)}, u32[]{:S(2)}, u32[]{:S(2)}) collective-permute-start(bf16[112,768]{1,0:T(8,128)(2,1)S(1)} %get-tuple-element.69), channel_id=1, source_target_pairs={{0,8},{4,12},{8,0},{12,4},{1,9},{5,13},{9,1},{13,5},{2,10},{6,14},... | collective-permute-start | bytes 516104 | tf_op jit(solution)/shard_map/ppermute | solution.py:416
  39.0 0.0 collective-permute-done.12.refs_7_
  39.0 1.2 %collective-permute-start.17 = (bf16[112,768]{1,0:T(8,128)(2,1)S(1)}, bf16[112,768]{1,0:T(8,128)(2,1)S(1)}, u32[]{:S(2)}, u32[]{:S(2)}) collective-permute-start(bf16[112,768]{1,0:T(8,128)(2,1)S(1)} %get-tuple-element.70), channel_id=1, source_target_pairs={{0,12},{4,8},{8,4},{12,0},{1,13},{5,9},{9,5},{13,1},{2,14},{6,10},... | collective-permute-start | bytes 516104 | tf_op jit(solution)/shard_map/ppermute | solution.py:416
  40.2 1.0 %merge.4 = (f32[64,768]{1,0:T(8,128)S(1)}, bf16[64,768]{1,0:T(8,128)(2,1)S(1)}, bf16[64,768]{1,0:T(8,128)(2,1)S(1)}, bf16[64,768]{1,0:T(8,128)(2,1)S(1)}) custom-call(s32[2]{0:T(128)S(1)} %pad_add_fusion.refs_0_, bf16[5,64,128]{2,1,0:T(8,128)(2,1)S(1)} %get-tuple-element.40.refs_1_, bf16[24,8192]{1,0:T(8,128)(2,1)S(1)} %get-tuple-element.41.refs_2_, ...), custom_call_target="tpu_custom_call" | custom-call | flops 100663296 | bytes 1572864 | tf_op jit(solution)/shard_map/merge/pallas_call | solution.py:377
  41.2 0.0 collective-permute-done.8
  41.2 1.6 %collective-permute-start.13 = (bf16[64,768]{1,0:T(8,128)(2,1)S(1)}, bf16[64,768]{1,0:T(8,128)(2,1)S(1)}, u32[]{:S(2)}, u32[]{:S(2)}) collective-permute-start(bf16[64,768]{1,0:T(8,128)(2,1)S(1)} %get-tuple-element.66), channel_id=1, source_target_pairs={{0,1},{1,2},{2,3},{3,0},{4,5},{5,6},{6,7},{7,4},{8,9},{9,10},{10,1... | collective-permute-start | bytes 294920 | tf_op jit(solution)/shard_map/ppermute | solution.py:464
  42.9 0.0 collective-permute-done.9
  42.9 3.2 %collective-permute-start.14 = (bf16[64,768]{1,0:T(8,128)(2,1)S(1)}, bf16[64,768]{1,0:T(8,128)(2,1)S(1)}, u32[]{:S(2)}, u32[]{:S(2)}) collective-permute-start(bf16[64,768]{1,0:T(8,128)(2,1)S(1)} %get-tuple-element.67), channel_id=1, source_target_pairs={{0,2},{1,3},{2,0},{3,1},{4,6},{5,7},{6,4},{7,5},{8,10},{9,11},{10,... | collective-permute-start | bytes 294920 | tf_op jit(solution)/shard_map/ppermute | solution.py:464
  46.1 0.0 collective-permute-done.10
  46.1 1.3 %collective-permute-start.15 = (bf16[64,768]{1,0:T(8,128)(2,1)S(1)}, bf16[64,768]{1,0:T(8,128)(2,1)S(1)}, u32[]{:S(2)}, u32[]{:S(2)}) collective-permute-start(bf16[64,768]{1,0:T(8,128)(2,1)S(1)} %get-tuple-element.68), channel_id=1, source_target_pairs={{0,3},{1,0},{2,1},{3,2},{4,7},{5,4},{6,5},{7,6},{8,11},{9,8},{10,9... | collective-permute-start | bytes 294920 | tf_op jit(solution)/shard_map/ppermute | solution.py:464
  47.4 0.0 collective-permute-done.16.refs_6_
  47.4 0.1 collective-permute-done.17.refs_7_
  47.5 1.0 %merge.5 = (f32[64,768]{1,0:T(8,128)S(1)}, bf16[64,768]{1,0:T(8,128)(2,1)S(1)}, bf16[64,768]{1,0:T(8,128)(2,1)S(1)}, bf16[64,768]{1,0:T(8,128)(2,1)S(1)}) custom-call(s32[2]{0:T(128)S(1)} %pad_add_fusion.refs_0_, bf16[5,64,128]{2,1,0:T(8,128)(2,1)S(1)} %get-tuple-element.40.refs_1_, bf16[24,8192]{1,0:T(8,128)(2,1)S(1)} %get-tuple-element.41.refs_2_, ...), custom_call_target="tpu_custom_call" | custom-call | flops 100663296 | bytes 1572864 | tf_op jit(solution)/shard_map/merge/pallas_call | solution.py:377
  48.5 0.7 %collective-permute-start.18 = (bf16[64,768]{1,0:T(8,128)(2,1)S(1)}, bf16[64,768]{1,0:T(8,128)(2,1)S(1)}, u32[]{:S(2)}, u32[]{:S(2)}) collective-permute-start(bf16[64,768]{1,0:T(8,128)(2,1)S(1)} %get-tuple-element.72), channel_id=1, source_target_pairs={{0,1},{1,2},{2,3},{3,0},{4,5},{5,6},{6,7},{7,4},{8,9},{9,10},{10,1... | collective-permute-start | bytes 294920 | tf_op jit(solution)/shard_map/ppermute | solution.py:464
  49.3 1.8 %collective-permute-start.19 = (bf16[64,768]{1,0:T(8,128)(2,1)S(1)}, bf16[64,768]{1,0:T(8,128)(2,1)S(1)}, u32[]{:S(2)}, u32[]{:S(2)}) collective-permute-start(bf16[64,768]{1,0:T(8,128)(2,1)S(1)} %get-tuple-element.73), channel_id=1, source_target_pairs={{0,2},{1,3},{2,0},{3,1},{4,6},{5,7},{6,4},{7,5},{8,10},{9,11},{10,... | collective-permute-start | bytes 294920 | tf_op jit(solution)/shard_map/ppermute | solution.py:464
  51.0 0.0 collective-permute-done.13
  51.0 1.5 %collective-permute-start.20 = (bf16[64,768]{1,0:T(8,128)(2,1)S(1)}, bf16[64,768]{1,0:T(8,128)(2,1)S(1)}, u32[]{:S(2)}, u32[]{:S(2)}) collective-permute-start(bf16[64,768]{1,0:T(8,128)(2,1)S(1)} %get-tuple-element.74), channel_id=1, source_target_pairs={{0,3},{1,0},{2,1},{3,2},{4,7},{5,4},{6,5},{7,6},{8,11},{9,8},{10,9... | collective-permute-start | bytes 294920 | tf_op jit(solution)/shard_map/ppermute | solution.py:464
  52.5 0.0 collective-permute-done.14
  52.5 0.0 collective-permute-done.15
  52.5 0.1 add_convert_fusion.1
  52.6 3.6 %collective-permute-done.18 = bf16[64,768]{1,0:T(8,128)(2,1)S(1)} collective-permute-done((bf16[64,768]{1,0:T(8,128)(2,1)S(1)}, bf16[64,768]{1,0:T(8,128)(2,1)S(1)}, u32[]{:S(2)}, u32[]{:S(2)}) %collective-permute-start.18) | collective-permute-done | bytes 98336 | tf_op jit(solution)/shard_map/ppermute | solution.py:464
  56.2 4.4 %collective-permute-done.19 = bf16[64,768]{1,0:T(8,128)(2,1)S(1)} collective-permute-done((bf16[64,768]{1,0:T(8,128)(2,1)S(1)}, bf16[64,768]{1,0:T(8,128)(2,1)S(1)}, u32[]{:S(2)}, u32[]{:S(2)}) %collective-permute-start.19) | collective-permute-done | bytes 98336 | tf_op jit(solution)/shard_map/ppermute | solution.py:464
  60.6 0.0 collective-permute-done.20
  60.6 0.1 add_convert_fusion
  60.7 0.7 %pad_maximum_fusion = bf16[64,2048]{1,0:T(8,128)(2,1)} fusion(bf16[64,768]{1,0:T(8,128)(2,1)S(1)} %add_convert_fusion, bf16[64,768]{1,0:T(8,128)(2,1)S(1)} %add_convert_fusion.1, bf16[64,512]{1,0:T(8,128)(2,1)S(1)} %add_convert_fusion.2), kind=kLoop, calls=%fused_computation | loop fusion | flops 786432 | bytes 524288 | tf_op jit(solution)/shard_map/concatenate | solution.py:466
  (1 shorter events, 0.0 us)
Async XLA Ops:
  1.5 3.8 %collective-permute-start = (bf16[64,4224]{1,0:T(8,128)(2,1)S(1)}, bf16[64,4224]{1,0:T(8,128)(2,1)S(1)}, u32[]{:S(2)}, u32[]{:S(2)}) collective-permute-start(bf16[64,4224]{1,0:T(8,128)(2,1)S(1)} %hidden.1.refs_2_), channel_id=1, source_target_pairs={{0,4},{4,0},{8,12},{12,8},{1,5},{5,1},{9,13},{13,9},{2,6},{6,2},{1... | collective-permute-start | bytes 1622024 | tf_op jit(solution)/shard_map/ppermute | solution.py:416
  2.0 15.4 %collective-permute-start.2 = (bf16[64,4224]{1,0:T(8,128)(2,1)S(1)}, bf16[64,4224]{1,0:T(8,128)(2,1)S(1)}, u32[]{:S(2)}, u32[]{:S(2)}) collective-permute-start(bf16[64,4224]{1,0:T(8,128)(2,1)S(1)} %hidden.1.refs_2_), channel_id=1, source_target_pairs={{0,8},{4,12},{8,0},{12,4},{1,9},{5,13},{9,1},{13,5},{2,10},{6,14},... | collective-permute-start | bytes 1622024 | tf_op jit(solution)/shard_map/ppermute | solution.py:416
  17.4 1.9 %collective-permute-start.4 = (bf16[64,4224]{1,0:T(8,128)(2,1)S(1)}, bf16[64,4224]{1,0:T(8,128)(2,1)S(1)}, u32[]{:S(2)}, u32[]{:S(2)}) collective-permute-start(bf16[64,4224]{1,0:T(8,128)(2,1)S(1)} %collective-permute-done.2.refs_2_), channel_id=1, source_target_pairs={{0,4},{4,0},{8,12},{12,8},{1,5},{5,1},{9,13},{13,9},{2,6},{6,2},{1... | collective-permute-start | bytes 1622024 | tf_op jit(solution)/shard_map/ppermute | solution.py:416
  21.8 1.5 %collective-permute-start.5 = (bf16[48,2048]{1,0:T(8,128)(2,1)S(1)}, bf16[48,2048]{1,0:T(8,128)(2,1)S(1)}, u32[]{:S(2)}, u32[]{:S(2)}) collective-permute-start(bf16[48,2048]{1,0:T(8,128)(2,1)S(1)} %get-tuple-element.52), channel_id=1, source_target_pairs={{0,4},{4,0},{8,12},{12,8},{1,5},{5,1},{9,13},{13,9},{2,6},{6,2},{1... | collective-permute-start | bytes 589832 | tf_op jit(solution)/shard_map/ppermute | solution.py:416
  22.0 8.9 %collective-permute-start.1 = (bf16[24,8192]{1,0:T(8,128)(2,1)S(1)}, bf16[24,8192]{1,0:T(8,128)(2,1)S(1)}, u32[]{:S(2)}, u32[]{:S(2)}) collective-permute-start(bf16[24,8192]{1,0:T(8,128)(2,1)S(1)} %get-tuple-element.42), channel_id=1, source_target_pairs={{0,4},{4,0},{8,12},{12,8},{1,5},{5,1},{9,13},{13,9},{2,6},{6,2},{1... | collective-permute-start | bytes 1179656 | tf_op jit(solution)/shard_map/ppermute | solution.py:416
  22.4 8.5 %collective-permute-start.3 = (bf16[64,2048]{1,0:T(8,128)(2,1)S(1)}, bf16[64,2048]{1,0:T(8,128)(2,1)S(1)}, u32[]{:S(2)}, u32[]{:S(2)}) collective-permute-start(bf16[64,2048]{1,0:T(8,128)(2,1)S(1)} %get-tuple-element.45), channel_id=1, source_target_pairs={{0,4},{4,0},{8,12},{12,8},{1,5},{5,1},{9,13},{13,9},{2,6},{6,2},{1... | collective-permute-start | bytes 786440 | tf_op jit(solution)/shard_map/ppermute | solution.py:416
  23.5 6.0 %collective-permute-start.6 = (bf16[112,512]{1,0:T(8,128)(2,1)S(1)}, bf16[112,512]{1,0:T(8,128)(2,1)S(1)}, u32[]{:S(2)}, u32[]{:S(2)}) collective-permute-start(bf16[112,512]{1,0:T(8,128)(2,1)S(1)} %get-tuple-element.56), channel_id=1, source_target_pairs={{0,8},{4,12},{8,0},{12,4},{1,9},{5,13},{9,1},{13,5},{2,10},{6,14},... | collective-permute-start | bytes 344072 | tf_op jit(solution)/shard_map/ppermute | solution.py:416
  25.3 5.9 %collective-permute-start.7 = (bf16[112,512]{1,0:T(8,128)(2,1)S(1)}, bf16[112,512]{1,0:T(8,128)(2,1)S(1)}, u32[]{:S(2)}, u32[]{:S(2)}) collective-permute-start(bf16[112,512]{1,0:T(8,128)(2,1)S(1)} %get-tuple-element.58), channel_id=1, source_target_pairs={{0,12},{4,8},{8,4},{12,0},{1,13},{5,9},{9,5},{13,1},{2,14},{6,10},... | collective-permute-start | bytes 344072 | tf_op jit(solution)/shard_map/ppermute | solution.py:416
  26.4 11.3 %collective-permute-start.11 = (bf16[112,768]{1,0:T(8,128)(2,1)S(1)}, bf16[112,768]{1,0:T(8,128)(2,1)S(1)}, u32[]{:S(2)}, u32[]{:S(2)}) collective-permute-start(bf16[112,768]{1,0:T(8,128)(2,1)S(1)} %get-tuple-element.63), channel_id=1, source_target_pairs={{0,8},{4,12},{8,0},{12,4},{1,9},{5,13},{9,1},{13,5},{2,10},{6,14},... | collective-permute-start | bytes 516104 | tf_op jit(solution)/shard_map/ppermute | solution.py:416
  29.5 9.5 %collective-permute-start.12 = (bf16[112,768]{1,0:T(8,128)(2,1)S(1)}, bf16[112,768]{1,0:T(8,128)(2,1)S(1)}, u32[]{:S(2)}, u32[]{:S(2)}) collective-permute-start(bf16[112,768]{1,0:T(8,128)(2,1)S(1)} %get-tuple-element.64), channel_id=1, source_target_pairs={{0,12},{4,8},{8,4},{12,0},{1,13},{5,9},{9,5},{13,1},{2,14},{6,10},... | collective-permute-start | bytes 516104 | tf_op jit(solution)/shard_map/ppermute | solution.py:416
  32.2 9.1 %collective-permute-start.8 = (bf16[64,512]{1,0:T(8,128)(2,1)S(1)}, bf16[64,512]{1,0:T(8,128)(2,1)S(1)}, u32[]{:S(2)}, u32[]{:S(2)}) collective-permute-start(bf16[64,512]{1,0:T(8,128)(2,1)S(1)} %get-tuple-element.60), channel_id=1, source_target_pairs={{0,1},{1,2},{2,3},{3,0},{4,5},{5,6},{6,7},{7,4},{8,9},{9,10},{10,1... | collective-permute-start | bytes 196616 | tf_op jit(solution)/shard_map/ppermute | solution.py:464
  33.8 9.1 %collective-permute-start.9 = (bf16[64,512]{1,0:T(8,128)(2,1)S(1)}, bf16[64,512]{1,0:T(8,128)(2,1)S(1)}, u32[]{:S(2)}, u32[]{:S(2)}) collective-permute-start(bf16[64,512]{1,0:T(8,128)(2,1)S(1)} %get-tuple-element.61), channel_id=1, source_target_pairs={{0,2},{1,3},{2,0},{3,1},{4,6},{5,7},{6,4},{7,5},{8,10},{9,11},{10,... | collective-permute-start | bytes 196616 | tf_op jit(solution)/shard_map/ppermute | solution.py:464
  36.4 9.7 %collective-permute-start.10 = (bf16[64,512]{1,0:T(8,128)(2,1)S(1)}, bf16[64,512]{1,0:T(8,128)(2,1)S(1)}, u32[]{:S(2)}, u32[]{:S(2)}) collective-permute-start(bf16[64,512]{1,0:T(8,128)(2,1)S(1)} %get-tuple-element.62), channel_id=1, source_target_pairs={{0,3},{1,0},{2,1},{3,2},{4,7},{5,4},{6,5},{7,6},{8,11},{9,8},{10,9... | collective-permute-start | bytes 196616 | tf_op jit(solution)/shard_map/ppermute | solution.py:464
  37.7 9.7 %collective-permute-start.16 = (bf16[112,768]{1,0:T(8,128)(2,1)S(1)}, bf16[112,768]{1,0:T(8,128)(2,1)S(1)}, u32[]{:S(2)}, u32[]{:S(2)}) collective-permute-start(bf16[112,768]{1,0:T(8,128)(2,1)S(1)} %get-tuple-element.69), channel_id=1, source_target_pairs={{0,8},{4,12},{8,0},{12,4},{1,9},{5,13},{9,1},{13,5},{2,10},{6,14},... | collective-permute-start | bytes 516104 | tf_op jit(solution)/shard_map/ppermute | solution.py:416
  39.0 8.5 %collective-permute-start.17 = (bf16[112,768]{1,0:T(8,128)(2,1)S(1)}, bf16[112,768]{1,0:T(8,128)(2,1)S(1)}, u32[]{:S(2)}, u32[]{:S(2)}) collective-permute-start(bf16[112,768]{1,0:T(8,128)(2,1)S(1)} %get-tuple-element.70), channel_id=1, source_target_pairs={{0,12},{4,8},{8,4},{12,0},{1,13},{5,9},{9,5},{13,1},{2,14},{6,10},... | collective-permute-start | bytes 516104 | tf_op jit(solution)/shard_map/ppermute | solution.py:416
  41.2 9.8 %collective-permute-start.13 = (bf16[64,768]{1,0:T(8,128)(2,1)S(1)}, bf16[64,768]{1,0:T(8,128)(2,1)S(1)}, u32[]{:S(2)}, u32[]{:S(2)}) collective-permute-start(bf16[64,768]{1,0:T(8,128)(2,1)S(1)} %get-tuple-element.66), channel_id=1, source_target_pairs={{0,1},{1,2},{2,3},{3,0},{4,5},{5,6},{6,7},{7,4},{8,9},{9,10},{10,1... | collective-permute-start | bytes 294920 | tf_op jit(solution)/shard_map/ppermute | solution.py:464
  42.9 9.6 %collective-permute-start.14 = (bf16[64,768]{1,0:T(8,128)(2,1)S(1)}, bf16[64,768]{1,0:T(8,128)(2,1)S(1)}, u32[]{:S(2)}, u32[]{:S(2)}) collective-permute-start(bf16[64,768]{1,0:T(8,128)(2,1)S(1)} %get-tuple-element.67), channel_id=1, source_target_pairs={{0,2},{1,3},{2,0},{3,1},{4,6},{5,7},{6,4},{7,5},{8,10},{9,11},{10,... | collective-permute-start | bytes 294920 | tf_op jit(solution)/shard_map/ppermute | solution.py:464
  46.1 6.4 %collective-permute-start.15 = (bf16[64,768]{1,0:T(8,128)(2,1)S(1)}, bf16[64,768]{1,0:T(8,128)(2,1)S(1)}, u32[]{:S(2)}, u32[]{:S(2)}) collective-permute-start(bf16[64,768]{1,0:T(8,128)(2,1)S(1)} %get-tuple-element.68), channel_id=1, source_target_pairs={{0,3},{1,0},{2,1},{3,2},{4,7},{5,4},{6,5},{7,6},{8,11},{9,8},{10,9... | collective-permute-start | bytes 294920 | tf_op jit(solution)/shard_map/ppermute | solution.py:464
  48.5 7.6 %collective-permute-start.18 = (bf16[64,768]{1,0:T(8,128)(2,1)S(1)}, bf16[64,768]{1,0:T(8,128)(2,1)S(1)}, u32[]{:S(2)}, u32[]{:S(2)}) collective-permute-start(bf16[64,768]{1,0:T(8,128)(2,1)S(1)} %get-tuple-element.72), channel_id=1, source_target_pairs={{0,1},{1,2},{2,3},{3,0},{4,5},{5,6},{6,7},{7,4},{8,9},{9,10},{10,1... | collective-permute-start | bytes 294920 | tf_op jit(solution)/shard_map/ppermute | solution.py:464
  49.3 11.4 %collective-permute-start.19 = (bf16[64,768]{1,0:T(8,128)(2,1)S(1)}, bf16[64,768]{1,0:T(8,128)(2,1)S(1)}, u32[]{:S(2)}, u32[]{:S(2)}) collective-permute-start(bf16[64,768]{1,0:T(8,128)(2,1)S(1)} %get-tuple-element.73), channel_id=1, source_target_pairs={{0,2},{1,3},{2,0},{3,1},{4,6},{5,7},{6,4},{7,5},{8,10},{9,11},{10,... | collective-permute-start | bytes 294920 | tf_op jit(solution)/shard_map/ppermute | solution.py:464
  51.0 9.6 %collective-permute-start.20 = (bf16[64,768]{1,0:T(8,128)(2,1)S(1)}, bf16[64,768]{1,0:T(8,128)(2,1)S(1)}, u32[]{:S(2)}, u32[]{:S(2)}) collective-permute-start(bf16[64,768]{1,0:T(8,128)(2,1)S(1)} %get-tuple-element.74), channel_id=1, source_target_pairs={{0,3},{1,0},{2,1},{3,2},{4,7},{5,4},{6,5},{7,6},{8,11},{9,8},{10,9... | collective-permute-start | bytes 294920 | tf_op jit(solution)/shard_map/ppermute | solution.py:464
